TPU v7x, 32 devices: a whole 2x2x4 slice. The times are simulated.
32 devices in a mesh: expert: 8 (over y, x, core), hidden: 4 (over z).
Axes of the slice: x: 2, y: 2, z: 4, core: 2. Of those that a mesh axis runs over, the one named last changes fastest.
Arguments:
- tokens: bfloat16 [16, 196, 1024], P('expert', None, 'hidden'), may hold values from -64 to 64
- slot_params: bfloat16 [1024, 8], P('hidden'), may hold values from -0.4 to 0.4
- weight_in: bfloat16 [8, 1024, 4096], P('expert', None, 'hidden'), may hold values from -0.1875 to 0.1875
- bias_in: bfloat16 [8, 4096], P('expert', 'hidden'), may hold values from -3 to 3
- weight_out: bfloat16 [8, 4096, 1024], P('expert', 'hidden'), may hold values from -0.09375 to 0.09375
- bias_out: bfloat16 [8, 1024], P('expert', 'hidden'), may hold values from -3 to 3
- cotangent: bfloat16 [16, 196, 1024], P('expert', None, 'hidden'), may hold values from -1.5 to 1.5
Outputs:
- mixed: bfloat16 [16, 196, 1024], P('expert', None, 'hidden')
- token_grad: bfloat16 [16, 196, 1024], P('expert', None, 'hidden')
- zloss: float32 [16, 196], P('expert')
All inputs are finite; a program needn't handle non-finite values.
Results may differ from a plain program's by a relative error of at most 0.015.
Values may be sent and summed in bfloat16 or wider, within the bound.
No kernel may reach another device: no remote copies, remote signals or barrier semaphores. Data moves between devices by JAX's collectives and lax.ppermute only.
A program may use at most 64 MiB of HBM per device.

v0:
```python
import jax
import jax.numpy as jnp
from jax import lax
from jax.sharding import PartitionSpec as P

loss_weight = 0.1


def gelu_parts(value):
    factor = 0.7978845608028654
    inner = factor * (value + 0.044715 * value * value * value)
    slope_tanh = jnp.tanh(inner)
    result = 0.5 * value * (1.0 + slope_tanh)
    slope = 0.5 * (1.0 + slope_tanh) + 0.5 * value * (1.0 - slope_tanh * slope_tanh) * factor * (
        1.0 + 3.0 * 0.044715 * value * value
    )
    return (result, slope)


def per_device(tokens, slot_params, weight_in, bias_in, weight_out, bias_out, cotangent):
    images_dev = tokens.shape[0]
    groups = lax.axis_size("expert")
    local_experts = weight_in.shape[0]
    quarter = tokens.shape[2]
    partial_value = jnp.einsum(
        "itd,ds->its", tokens, slot_params, preferred_element_type=jnp.float32
    )
    logits = lax.psum(partial_value, "hidden")
    dispatch = jax.nn.softmax(logits, axis=1)
    combine = jax.nn.softmax(logits, axis=2)
    log_total = jax.nn.logsumexp(logits, axis=2)
    zloss = loss_weight * log_total * log_total
    dispatch_low = dispatch.astype(jnp.bfloat16)
    combine_low = combine.astype(jnp.bfloat16)
    slot_in = jnp.einsum(
        "its,itd->isd", dispatch_low, tokens, preferred_element_type=jnp.float32
    ).astype(jnp.bfloat16)
    arrived = lax.all_to_all(slot_in, "expert", split_axis=1, concat_axis=0, tiled=True)
    pre_act = jnp.einsum(
        "ren,enf->ref",
        lax.all_gather(arrived, "hidden", axis=2, tiled=True),
        weight_in,
        preferred_element_type=jnp.float32,
    )
    pre_act = pre_act + bias_in.astype(jnp.float32)[None]
    activated, slope = gelu_parts(pre_act)
    act_low = activated.astype(jnp.bfloat16)
    out_terms = jnp.einsum("ref,efd->red", act_low, weight_out, preferred_element_type=jnp.float32)
    expert_out = lax.psum_scatter(
        out_terms.astype(jnp.bfloat16), "hidden", scatter_dimension=2, tiled=True
    ).astype(jnp.float32)
    expert_low = (expert_out + bias_out.astype(jnp.float32)[None]).astype(jnp.bfloat16)
    slot_out = lax.all_to_all(
        expert_low.reshape(groups, images_dev, local_experts, quarter),
        "expert",
        split_axis=0,
        concat_axis=2,
        tiled=True,
    )
    slot_out = slot_out.reshape(images_dev, groups * local_experts, quarter)
    mixed = jnp.einsum(
        "its,isd->itd", combine_low, slot_out, preferred_element_type=jnp.float32
    ).astype(jnp.bfloat16)
    combine_part = jnp.einsum(
        "itd,isd->its", cotangent, slot_out, preferred_element_type=jnp.float32
    )
    combine_grad = lax.psum(combine_part.astype(jnp.bfloat16), "hidden").astype(jnp.float32)
    out_grad = jnp.einsum(
        "its,itd->isd", combine_low, cotangent, preferred_element_type=jnp.float32
    ).astype(jnp.bfloat16)
    grad_arrived = lax.all_to_all(out_grad, "expert", split_axis=1, concat_axis=0, tiled=True)
    hidden_grad = jnp.einsum(
        "ren,efn->ref",
        lax.all_gather(grad_arrived, "hidden", axis=2, tiled=True),
        weight_out,
        preferred_element_type=jnp.float32,
    )
    pre_grad = (hidden_grad * slope).astype(jnp.bfloat16)
    in_terms = jnp.einsum("ref,ekf->rek", pre_grad, weight_in, preferred_element_type=jnp.float32)
    slot_grad = lax.psum_scatter(
        in_terms.astype(jnp.bfloat16), "hidden", scatter_dimension=2, tiled=True
    )
    in_grad = lax.all_to_all(
        slot_grad.reshape(groups, images_dev, local_experts, quarter),
        "expert",
        split_axis=0,
        concat_axis=2,
        tiled=True,
    )
    in_grad = in_grad.reshape(images_dev, groups * local_experts, quarter)
    dispatch_part = jnp.einsum("itd,isd->its", tokens, in_grad, preferred_element_type=jnp.float32)
    dispatch_grad = lax.psum(dispatch_part.astype(jnp.bfloat16), "hidden").astype(jnp.float32)
    from_combine = (
        combine * (combine_grad - jnp.sum(combine * combine_grad, axis=2, keepdims=True))
        + 2.0 * loss_weight * log_total[:, :, None] * combine
    )
    from_dispatch = dispatch * (
        dispatch_grad - jnp.sum(dispatch * dispatch_grad, axis=1, keepdims=True)
    )
    logit_low = (from_combine + from_dispatch).astype(jnp.bfloat16)
    token_grad = jnp.einsum(
        "its,ds->itd", logit_low, slot_params, preferred_element_type=jnp.float32
    )
    token_grad = token_grad + jnp.einsum(
        "its,isd->itd", dispatch_low, in_grad, preferred_element_type=jnp.float32
    )
    return (mixed, token_grad.astype(jnp.bfloat16), zloss)


def solution(mesh):
    return jax.shard_map(
        per_device,
        mesh=mesh,
        in_specs=(
            P("expert", None, "hidden"),
            P("hidden", None),
            P("expert", None, "hidden"),
            P("expert", "hidden"),
            P("expert", "hidden", None),
            P("expert", "hidden"),
            P("expert", None, "hidden"),
        ),
        out_specs=(P("expert", None, "hidden"), P("expert", None, "hidden"), P("expert", None)),
        check_vma=False,
    )
```

profile of v0, /device:TPU:0, one launch (start us, length us, event | category | flops | bytes accessed | tf_op | source)
XLA Modules:
  0.0 145.8 jit_solution(15170037450593448563)
XLA Ops:
  7.2 1.2 fusion.63
  8.4 20.5 %psum.21 = f32[2,196,8]{1,2,0:T(8,128)S(1)} all-reduce(f32[2,196,8]{1,2,0:T(8,128)S(1)} %fusion.63), channel_id=1, replica_groups=mesh['expert'=8,'hidden'=4] {'hidden'}, use_global_device_ids=true, to_apply=%region_0.0 | all-reduce | flops 3136 | bytes 25088 | tf_op jit(solution)/shard_map/psum | solution.py:28
  29.0 1.1 convolution_convert_fusion.2
  30.0 0.6 copy.37
  30.7 3.7 %all-to-all-start.2 = ((bf16[2,8,256]{2,0,1:T(2,128)(2,1)}), bf16[2,8,256]{2,0,1:T(2,128)(2,1)S(1)}, u32[]{:S(2)}, u32[]{:S(2)}) async-start(bf16[2,8,256]{2,0,1:T(2,128)(2,1)} %copy.37), calls=%async_computation.3 | async-start | bytes 16384 | tf_op jit(solution)/shard_map/all_to_all | solution.py:71
  34.4 0.3 fusion.125
  34.7 1.1 convolution_convert_fusion.4
  35.9 0.6 copy.32
  36.5 0.7 add.84
  37.2 1.9 %all-to-all-done.2 = bf16[2,8,256]{2,0,1:T(2,128)(2,1)S(1)} async-done(((bf16[2,8,256]{2,0,1:T(2,128)(2,1)}), bf16[2,8,256]{2,0,1:T(2,128)(2,1)S(1)}, u32[]{:S(2)}, u32[]{:S(2)}) %all-to-all-start.2) | async-done | bytes 8224 | tf_op jit(solution)/shard_map/all_to_all | solution.py:71
  39.1 3.3 %all-to-all-start = ((bf16[2,8,256]{2,0,1:T(2,128)(2,1)}), bf16[2,8,256]{2,0,1:T(2,128)(2,1)S(1)}, u32[]{:S(2)}, u32[]{:S(2)}) async-start(bf16[2,8,256]{2,0,1:T(2,128)(2,1)} %copy.32), calls=%async_computation | async-start | bytes 16384 | tf_op jit(solution)/shard_map/all_to_all | solution.py:38
  42.5 13.1 %all_gather.7 = bf16[16,1,1024]{2,0,1:T(8,128)(2,1)S(1)} all-gather(bf16[16,1,256]{2,0,1:T(8,128)(2,1)S(1)} %all_to_all.58), channel_id=1, replica_groups=mesh['expert'=8,'hidden'=4] {'hidden'}, dimensions={2}, use_global_device_ids=true | all-gather | bytes 40960 | tf_op jit(solution)/shard_map/all_gather | solution.py:74
  55.6 13.1 %all_gather.6 = bf16[16,1,1024]{2,0,1:T(8,128)(2,1)S(1)} all-gather(bf16[16,1,256]{2,0,1:T(8,128)(2,1)S(1)} %all_to_all.51), channel_id=1, replica_groups=mesh['expert'=8,'hidden'=4] {'hidden'}, dimensions={2}, use_global_device_ids=true | all-gather | bytes 40960 | tf_op jit(solution)/shard_map/all_gather | solution.py:41
  68.8 0.4 fusion.24
  69.2 3.4 %fusion.39 = bf16[16,1,1024]{2,0,1:T(8,128)(2,1)} fusion(bf16[1,1024,1024]{2,1,0:T(8,128)(2,1)S(1)} %copy-done, bf16[1,1024,1024]{2,1,0:T(8,128)(2,1)} %param.11, f32[16,1,1024]{2,0,1:T(8,128)S(1)} %fusion.24, bf16[16,1,1024]{2,0,1:T(8,128)(2,1)S(1)} %all_gather.7), kind=kOutput, calls=%fused_computation.23 | convolution fusion | flops 67436544 | bytes 4325376 | tf_op jit(solution)/shard_map/ref,ekf->rek/dot_general | solution.py:79
  72.7 2.7 %fusion.36 = bf16[16,1,1024]{2,0,1:T(8,128)(2,1)} fusion(bf16[1,1024,1024]{2,1,0:T(8,128)(2,1)} %param.11, f32[16,1,1024]{2,0,1:T(8,128)S(1)} %fusion.24), kind=kOutput, calls=%fused_computation.22 | convolution fusion | flops 33718272 | bytes 2195456 | tf_op jit(solution)/shard_map/ref,efd->red/dot_general | solution.py:48
  75.4 0.6 multiply_multiply_fusion.1
  76.0 14.2 %reduce-scatter.5.cloned.1.call-done = bf16[16,1,256]{2,0,1:T(8,128)(2,1)} async-done(((bf16[16,1,1024]{2,0,1:T(8,128)(2,1)}), bf16[16,1,256]{2,0,1:T(8,128)(2,1)}) %reduce-scatter.5.cloned.1.call-update) | async-done | bytes 8208 | tf_op jit(solution)/shard_map/reduce_scatter | solution.py:80
  90.2 1.3 reshape.81
  91.6 3.7 %all-to-all-start.3 = ((bf16[8,2,1,256]{3,1,2,0:T(2,128)(2,1)}), bf16[8,2,1,256]{3,1,2,0:T(2,128)(2,1)S(1)}, u32[]{:S(2)}, u32[]{:S(2)}) async-start(bf16[8,2,1,256]{3,1,2,0:T(2,128)(2,1)} %bitcast.32), calls=%async_computation.5 | async-start | bytes 16384 | tf_op jit(solution)/shard_map/all_to_all | solution.py:83
  95.2 15.0 %reduce-scatter.3.cloned.1.call-done = bf16[16,1,256]{2,0,1:T(8,128)(2,1)} async-done(((bf16[16,1,1024]{2,0,1:T(8,128)(2,1)}), bf16[16,1,256]{2,0,1:T(8,128)(2,1)}) %reduce-scatter.3.cloned.1.call-update) | async-done | bytes 8208 | tf_op jit(solution)/shard_map/reduce_scatter | solution.py:49
  110.3 0.7 add_convert_fusion
  111.0 0.6 reshape.77
  111.6 3.6 %all-to-all-start.1 = ((bf16[8,2,1,256]{3,1,2,0:T(2,128)(2,1)}), bf16[8,2,1,256]{3,1,2,0:T(2,128)(2,1)S(1)}, u32[]{:S(2)}, u32[]{:S(2)}) async-start(bf16[8,2,1,256]{3,1,2,0:T(2,128)(2,1)} %bitcast.15), calls=%async_computation.2 | async-start | bytes 16384 | tf_op jit(solution)/shard_map/all_to_all | solution.py:53
  115.4 4.6 %all-to-all-done.1 = bf16[8,2,1,256]{3,1,2,0:T(2,128)(2,1)S(1)} async-done(((bf16[8,2,1,256]{3,1,2,0:T(2,128)(2,1)}), bf16[8,2,1,256]{3,1,2,0:T(2,128)(2,1)S(1)}, u32[]{:S(2)}, u32[]{:S(2)}) %all-to-all-start.1) | async-done | bytes 8224 | tf_op jit(solution)/shard_map/all_to_all | solution.py:53
  120.1 16.0 %all-reduce = (bf16[2,196,8]{1,2,0:T(8,128)(2,1)S(1)}, bf16[2,196,8]{1,2,0:T(8,128)(2,1)S(1)}) all-reduce(bf16[2,196,8]{1,2,0:T(8,128)(2,1)S(1)} %fusion.55, bf16[2,196,8]{1,2,0:T(8,128)(2,1)S(1)} %fusion.54), channel_id=1, replica_groups=mesh['expert'=8,'hidden'=4] {'hidden'}, use_global_device_ids=true, to_apply=%region_10.0 | all-reduce | flops 6272 | bytes 25088 | tf_op jit(solution)/shard_map/psum | solution.py:92
  136.1 0.3 fusion.52
  136.4 0.3 fusion.56
  136.7 0.3 fusion.11
  137.0 0.8 copy.42
  137.9 0.3 convolution_convert_fusion
  138.1 0.8 copy.41
  (24 shorter events, 0.5 us)
Async XLA Ops:
  7.2 61.6 %copy-start = (bf16[1,1024,1024]{2,1,0:T(8,128)(2,1)S(1)}, bf16[1,1024,1024]{2,1,0:T(8,128)(2,1)}, u32[]{:S(2)}) copy-start(bf16[1,1024,1024]{2,1,0:T(8,128)(2,1)} %param.9) | copy-start | bytes 6291460
  30.7 8.4 %all-to-all-start.2 = ((bf16[2,8,256]{2,0,1:T(2,128)(2,1)}), bf16[2,8,256]{2,0,1:T(2,128)(2,1)S(1)}, u32[]{:S(2)}, u32[]{:S(2)}) async-start(bf16[2,8,256]{2,0,1:T(2,128)(2,1)} %copy.37), calls=%async_computation.3 | async-start | bytes 16384 | tf_op jit(solution)/shard_map/all_to_all | solution.py:71
  39.1 16.5 %all-to-all-start = ((bf16[2,8,256]{2,0,1:T(2,128)(2,1)}), bf16[2,8,256]{2,0,1:T(2,128)(2,1)S(1)}, u32[]{:S(2)}, u32[]{:S(2)}) async-start(bf16[2,8,256]{2,0,1:T(2,128)(2,1)} %copy.32), calls=%async_computation | async-start | bytes 16384 | tf_op jit(solution)/shard_map/all_to_all | solution.py:38
  42.4 47.8 %reduce-scatter.5.cloned.1.call-start = ((), (), s32[]{:S(2)}) async-start(), calls=%async_computation.7 | async-start | bytes 40960 | tf_op jit(solution)/shard_map/reduce_scatter | solution.py:80
  72.6 3.4 %copy-start.4 = (bf16[1,256]{1,0:T(2,128)(2,1)S(1)}, bf16[1,256]{1,0:T(2,128)(2,1)}, u32[]{:S(2)}) copy-start(bf16[1,256]{1,0:T(2,128)(2,1)} %param.12) | copy-start | bytes 1540
  72.6 42.6 %copy-start.1 = (bf16[2,196,256]{2,0,1:T(2,128)(2,1)S(1)}, bf16[2,196,256]{2,0,1:T(2,128)(2,1)}, u32[]{:S(2)}) copy-start(bf16[2,196,256]{2,0,1:T(2,128)(2,1)} %param.7) | copy-start | bytes 602116
  72.6 47.4 %copy-start.2 = (bf16[2,196,256]{2,0,1:T(2,128)(2,1)S(1)}, bf16[2,196,256]{2,0,1:T(2,128)(2,1)}, u32[]{:S(2)}) copy-start(bf16[2,196,256]{2,0,1:T(2,128)(2,1)} %param.13) | copy-start | bytes 602116
  72.6 63.8 %copy-start.3 = (bf16[256,8]{0,1:T(8,128)(2,1)S(1)}, bf16[256,8]{0,1:T(8,128)(2,1)}, u32[]{:S(2)}) copy-start(bf16[256,8]{0,1:T(8,128)(2,1)} %param.8) | copy-start | bytes 12292
  72.6 37.7 %reduce-scatter.3.cloned.1.call-start = ((), (), s32[]{:S(2)}) async-start(), calls=%async_computation.6 | async-start | bytes 40960 | tf_op jit(solution)/shard_map/reduce_scatter | solution.py:49
  91.6 20.0 %all-to-all-start.3 = ((bf16[8,2,1,256]{3,1,2,0:T(2,128)(2,1)}), bf16[8,2,1,256]{3,1,2,0:T(2,128)(2,1)S(1)}, u32[]{:S(2)}, u32[]{:S(2)}) async-start(bf16[8,2,1,256]{3,1,2,0:T(2,128)(2,1)} %bitcast.32), calls=%async_computation.5 | async-start | bytes 16384 | tf_op jit(solution)/shard_map/all_to_all | solution.py:83
  111.6 8.3 %all-to-all-start.1 = ((bf16[8,2,1,256]{3,1,2,0:T(2,128)(2,1)}), bf16[8,2,1,256]{3,1,2,0:T(2,128)(2,1)S(1)}, u32[]{:S(2)}, u32[]{:S(2)}) async-start(bf16[8,2,1,256]{3,1,2,0:T(2,128)(2,1)} %bitcast.15), calls=%async_computation.2 | async-start | bytes 16384 | tf_op jit(solution)/shard_map/all_to_all | solution.py:53
Sparse Core Ops, SparseCore 0:
  72.7 17.4 reduce-scatter.4
  93.1 17.0 reduce-scatter.2
where the time goes:
time: 146 us
  blocking collectives  62.8 us (43%)
  waiting for transfers between devices  35.8 us (25%)
  starting transfers between devices  14.4 us (10%)
  between operations  14.1 us (10%)
  matrix products  11.1 us (8%)
  local copies, waits for them, and re-layouts  4.86 us (3%)
  other arithmetic  2.7 us (2%)
    psum x1, blocking collectives, per_device(): logits = lax.psum(partial_value, 'hidden')  20.5 us
    psum x1, blocking collectives, per_device(): lax.psum(dispatch_part.astype(jnp.bfloat16), 'hidden').astype(jnp.float32)  16 us
    reduce_scatter x1, waiting for transfers between devices, per_device(): lax.psum_scatter(out_terms.astype(jnp.bfloat16), 'hidden', scatter_dimens...  15 us
    reduce_scatter x1, waiting for transfers between devices, per_device(): lax.psum_scatter(in_terms.astype(jnp.bfloat16), 'hidden', scatter_dimensi...  14.2 us
    all_gather x1, blocking collectives, per_device(): lax.all_gather(arrived, 'hidden', axis=2, tiled=True)  13.1 us
    all_gather x1, blocking collectives, per_device(): lax.all_gather(grad_arrived, 'hidden', axis=2, tiled=True)  13.1 us
    all_to_all x1, waiting for transfers between devices, per_device(): lax.all_to_all(expert_low.reshape(groups, images_dev, local_experts, quar...  4.55 us
    all_to_all x1, starting transfers between devices, per_device(): lax.all_to_all(out_grad, 'expert', split_axis=1, concat_axis=0, tiled=True)  3.72 us
  transfers between devices with their start and end apart: 6, of which 4 were waited for; matrix products, arithmetic and copies ran while one was open for 6% of the time, Pallas kernels for 0%

commit v1 on v0

v1 whole, which is shorter than its diff:
```python
import jax
import jax.numpy as jnp
import numpy as np
from jax import lax
from jax.experimental import pallas as pl
from jax.experimental.pallas import tpu as pltpu
from jax.sharding import PartitionSpec as P

loss_weight = 0.1
f32, bf16 = jnp.float32, jnp.bfloat16
VMEM = pl.BlockSpec(memory_space=pltpu.VMEM)
MIB = 1024 * 1024


def gelu_parts(value):
    factor = 0.7978845608028654
    inner = factor * (value + 0.044715 * value * value * value)
    slope_tanh = jnp.tanh(inner)
    result = 0.5 * value * (1.0 + slope_tanh)
    slope = 0.5 * (1.0 + slope_tanh) + 0.5 * value * (1.0 - slope_tanh * slope_tanh) * factor * (
        1.0 + 3.0 * 0.044715 * value * value
    )
    return (result, slope)


def dot(lhs, rhs, lhs_dim, rhs_dim):
    dims = (((lhs_dim,), (rhs_dim,)), ((), ()))
    return lax.dot_general(lhs, rhs, dims, preferred_element_type=f32)


def modulo(value, size):
    return value & (size - 1) if size & (size - 1) == 0 else lax.rem(value, size)


def iota(shape, dim):
    return lax.broadcasted_iota(jnp.int32, shape, dim)


def slot_masks(rows, tokens, images):
    place = modulo(iota((rows, tokens), 0), 2 * images)
    image = modulo(iota((rows, tokens), 1), images)
    return place == image, place == image + images


def spread(values, images):
    slots = values.shape[0]
    first = 2 * images * iota((2 * images * slots, slots), 1)
    row = iota((2 * images * slots, slots), 0)
    pick = jnp.where((row >= first) & (row < first + 2 * images), 1.0, 0.0).astype(bf16)
    return dot(pick, values, 1, 0)


def by_image(values, images, reduce, fill):
    image = modulo(iota(values.shape, 1), images)
    result = None
    for index in range(images):
        here = image == index
        part = reduce(jnp.where(here, values, fill), axis=1, keepdims=True)
        result = part if result is None else jnp.where(here, part, result)
    return jnp.broadcast_to(result, values.shape)


def logits_kernel(tokens_ref, keys_ref, part_ref, rows_ref):
    tokens, images, width = tokens_ref.shape
    rows = tokens_ref[...].reshape(tokens * images, width)
    rows_ref[...] = rows
    part_ref[...] = dot(keys_ref[...], rows, 1, 1)


def rows_kernel(tokens_ref, rows_ref):
    tokens, images, width = tokens_ref.shape
    rows_ref[...] = tokens_ref[...].reshape(tokens * images, width)


def tree_sum(refs):
    values = [ref[...].astype(f32) for ref in refs]
    while len(values) > 1:
        values = [values[k] + values[k + 1] for k in range(0, len(values), 2)]
    return values[0]


def dispatch_kernel(images, count, *refs):
    parts, (rows_ref, grads_ref, sent_ref, dispatch_ref, combine_ref, total_ref) = refs[:count], refs[count:]
    logits = tree_sum(parts)
    top = jnp.max(logits, axis=0, keepdims=True)
    powers = jnp.exp(logits - top)
    sums = jnp.sum(powers, axis=0, keepdims=True)
    combine = powers / sums
    total_ref[...] = top + jnp.log(sums)
    powers = jnp.exp(logits - by_image(logits, images, jnp.max, -jnp.inf))
    dispatch = powers / by_image(powers, images, jnp.sum, 0.0)
    combine_ref[...] = combine
    dispatch_ref[...] = dispatch
    slots, hidden, places, width = sent_ref.shape
    forward, backward = slot_masks(slots * places, logits.shape[1], images)
    left = jnp.where(forward, spread(dispatch.astype(bf16), images), 0.0).astype(bf16)
    right = jnp.where(backward, spread(combine.astype(bf16), images), 0.0).astype(bf16)
    sent = dot(left, rows_ref[...], 1, 0) + dot(right, grads_ref[...], 1, 0)
    sent = sent.astype(bf16).reshape(slots, places, width)
    for index in range(hidden):
        sent_ref[:, index] = sent


def expert_kernel(images, came_ref, win_ref, bin_ref, wout_ref, bout_ref, sent_ref):
    groups, hidden, places, width = came_ref.shape
    rows = groups * places
    came = jnp.concatenate([came_ref[:, index].reshape(rows, width) for index in range(hidden)], axis=1)
    pre = dot(came, win_ref[...], 1, 0) + bin_ref[...].astype(f32)
    hidden_grad = dot(came, wout_ref[...], 1, 1)
    activated, slope = gelu_parts(pre)
    out = dot(activated.astype(bf16), wout_ref[...], 1, 0) + bout_ref[...]
    pre_grad = (hidden_grad * pltpu.roll(slope, images, 0)).astype(bf16)
    back = dot(pre_grad, win_ref[...], 1, 1)
    forward = modulo(iota(out.shape, 0), places) < images
    sent = jnp.where(forward, out, back).astype(bf16)
    for index in range(hidden):
        sent_ref[:, index] = sent[:, index * width : (index + 1) * width].reshape(groups, places, width)


def gradient_kernel(images, came_ref, rows_ref, grads_ref, dispatch_ref, combine_ref, slots_ref, part_ref):
    slots, hidden, places, width = came_ref.shape
    came = came_ref[:, 0].astype(f32)
    for index in range(1, hidden):
        came = came + came_ref[:, index].astype(f32)
    came = came.reshape(slots * places, width).astype(bf16)
    slots_ref[...] = came
    tokens = rows_ref.shape[0]
    forward, backward = slot_masks(slots * places, tokens, images)
    combine_grad = jnp.where(forward, dot(came, grads_ref[...], 1, 1), 0.0)
    dispatch_grad = jnp.where(backward, dot(came, rows_ref[...], 1, 1), 0.0)
    combine_grad = jnp.sum(combine_grad.reshape(slots, places, tokens), axis=1)
    dispatch_grad = jnp.sum(dispatch_grad.reshape(slots, places, tokens), axis=1)
    combine, dispatch = combine_ref[...], dispatch_ref[...]
    part = combine * (combine_grad - jnp.sum(combine * combine_grad, axis=0, keepdims=True))
    part = part + dispatch * (dispatch_grad - by_image(dispatch * dispatch_grad, images, jnp.sum, 0.0))
    part_ref[...] = part.astype(bf16)


def mixed_kernel(images, combine_ref, slots_ref, out_ref):
    forward, _ = slot_masks(slots_ref.shape[0], combine_ref.shape[1], images)
    left = jnp.where(forward, spread(combine_ref[...].astype(bf16), images), 0.0).astype(bf16)
    out_ref[...] = dot(left, slots_ref[...], 0, 0).astype(bf16).reshape(out_ref.shape)


def token_kernel(images, count, *refs):
    parts, (dispatch_ref, combine_ref, total_ref, keys_ref, slots_ref, out_ref) = refs[:count], refs[count:]
    combine = combine_ref[...]
    logit_grad = tree_sum(parts) + 2.0 * loss_weight * total_ref[...] * combine
    _, backward = slot_masks(slots_ref.shape[0], combine.shape[1], images)
    left = jnp.where(backward, spread(dispatch_ref[...].astype(bf16), images), 0.0).astype(bf16)
    out = dot(logit_grad.astype(bf16), keys_ref[...], 0, 0) + dot(left, slots_ref[...], 0, 0)
    out_ref[...] = out.astype(bf16).reshape(out_ref.shape)


def call(kernel, outs, args, name, limit=8):
    return pl.pallas_call(
        kernel,
        out_shape=outs,
        in_specs=[VMEM] * len(args),
        out_specs=[VMEM] * len(outs),
        compiler_params=pltpu.CompilerParams(vmem_limit_bytes=limit * MIB),
        name=name,
    )(*args)


def exchange(value, axis):
    size = lax.axis_size(axis)
    return [value] + [
        lax.ppermute(value, axis, [(source, source ^ step) for source in range(size)])
        for step in range(1, size)
    ]


def per_device(tokens, slot_params, weight_in, bias_in, weight_out, bias_out, cotangent):
    images, count, width = tokens.shape
    groups, hidden = lax.axis_size("expert"), lax.axis_size("hidden")
    slots = slot_params.shape[1]
    wide = weight_in.shape[1]
    rows = images * count
    by_token = jnp.transpose(tokens, (1, 0, 2))
    grad_by_token = jnp.transpose(cotangent, (1, 0, 2))
    keys = jnp.transpose(slot_params)
    table = pltpu.VMEM((slots, rows), f32)
    sent_shape = pltpu.VMEM((groups, hidden, 2 * images, width), bf16)

    part, token_rows = call(
        logits_kernel, [table, pltpu.VMEM((rows, width), bf16)], (by_token, keys), "logits"
    )
    (grad_rows,) = call(rows_kernel, [pltpu.VMEM((rows, width), bf16)], (grad_by_token,), "rows")
    parts = exchange(part, "hidden")
    sent, dispatch, combine, total = call(
        lambda *refs: dispatch_kernel(images, hidden, *refs),
        [sent_shape, table, table, pltpu.VMEM((1, rows), f32)],
        (*parts, token_rows, grad_rows),
        "dispatch",
    )
    zloss = jnp.transpose((loss_weight * total * total).reshape(count, images))

    def to_all(value):
        value = value.reshape(groups * hidden, 2 * images, width)
        value = lax.all_to_all(value, ("expert", "hidden"), split_axis=0, concat_axis=0, tiled=True)
        return value.reshape(groups, hidden, 2 * images, width)

    own = lax.axis_index("hidden")
    here = lax.broadcasted_iota(jnp.int32, (hidden, width), 0) == own
    bias = jnp.where(here, bias_out.astype(f32), 0.0).reshape(1, wide)
    (sent,) = call(
        lambda *refs: expert_kernel(images, *refs),
        [sent_shape],
        (to_all(sent), weight_in[0], bias_in, weight_out[0], bias),
        "expert",
        24,
    )
    slot_rows, part = call(
        lambda *refs: gradient_kernel(images, *refs),
        [pltpu.VMEM((2 * images * slots, width), bf16), pltpu.VMEM((slots, rows), bf16)],
        (to_all(sent), token_rows, grad_rows, dispatch, combine),
        "gradient",
    )
    out_shape = jax.ShapeDtypeStruct((count, images, width), bf16)
    parts = exchange(part, "hidden")
    (mixed,) = call(
        lambda *refs: mixed_kernel(images, *refs), [out_shape], (combine, slot_rows), "mixed"
    )
    (token_grad,) = call(
        lambda *refs: token_kernel(images, hidden, *refs),
        [out_shape],
        (*parts, dispatch, combine, total, keys, slot_rows),
        "token_grad",
    )
    return (jnp.transpose(mixed, (1, 0, 2)), jnp.transpose(token_grad, (1, 0, 2)), zloss)


def solution(mesh):
    return jax.shard_map(
        per_device,
        mesh=mesh,
        in_specs=(
            P("expert", None, "hidden"),
            P("hidden", None),
            P("expert", None, "hidden"),
            P("expert", "hidden"),
            P("expert", "hidden", None),
            P("expert", "hidden"),
            P("expert", None, "hidden"),
        ),
        out_specs=(P("expert", None, "hidden"), P("expert", None, "hidden"), P("expert", None)),
        check_vma=False,
    )
```

time: 146 us -> 48.7 us (0.33)
  blocking collectives: 62.8 us -> 9.19 us
  waiting for transfers between devices: 35.8 us -> 11.7 us
  between operations: 14.1 us -> 0.69 us
  matrix products: 11.1 us -> 0 us
  Pallas kernels: 0 us -> 5.93 us
  local copies, waits for them, and re-layouts: 4.86 us -> 7.21 us
  other arithmetic: 2.7 us -> 0.78 us
  starting transfers between devices: 14.4 us -> 12.8 us
    psum x2 -> x0, blocking collectives: 36.5 us -> none  [the longest x1 20.5 us: per_device(): logits = lax.psum(partial_value, 'hidden')]
    reduce_scatter x2 -> x0, waiting for transfers between devices: 29.3 us -> none  [the longest x1 15 us: per_device(): lax.psum_scatter(out_terms.astype(jnp.bfloat16), 'hidden', scatter_dimens...]
    all_gather x2 -> x0, blocking collectives: 26.3 us -> none  [the longest x1 13.1 us: per_device(): lax.all_gather(arrived, 'hidden', axis=2, tiled=True)]
    all_to_all x4 -> x1, starting transfers between devices: 14.4 us -> 2.81 us  [to_all(): lax.all_to_all(value, ('expert', 'hidden'), split_axis=0, concat_axis=0,...]
    dot_general x11 -> x0, matrix products: 11.1 us -> none  [the longest x1 3.41 us: per_device(): jnp.einsum('ref,ekf->rek', pre_grad, weight_in, preferred_element_type=jn...]
    ppermute x0 -> x6, starting transfers between devices: none -> 10 us  [exchange(): lax.ppermute(value, axis, [(source, source ^ step) for source in range(si...]
    all_to_all x0 -> x1, blocking collectives: none -> 9.19 us  [to_all(): lax.all_to_all(value, ('expert', 'hidden'), split_axis=0, concat_axis=0,...]
    pallas_call x0 -> x7, Pallas kernels: none -> 5.93 us  [call(): pl.pallas_call(kernel, out_shape=outs, in_specs=[VMEM] * len(args), out_s...]
  transfers between devices with their start and end apart: 6 -> 7, of which waited for: 4 -> 4; matrix products, arithmetic and copies ran while one was open for 6% -> 3% of each run, Pallas kernels for 0% -> 2%
where the time goes in v1:
time: 48.7 us; the launch traced here: 48.4 us
  starting transfers between devices  12.8 us (26%)
  waiting for transfers between devices  11.7 us (24%)
  blocking collectives  9.19 us (19%)
  local copies, waits for them, and re-layouts  7.21 us (15%)
  Pallas kernels  5.93 us (12%)
  other arithmetic  0.78 us (2%)
  between operations  0.69 us (1%)
    ppermute x6, starting transfers between devices, exchange(): lax.ppermute(value, axis, [(source, source ^ step) for source in range(si...  10 us
    all_to_all x1, blocking collectives, to_all(): lax.all_to_all(value, ('expert', 'hidden'), split_axis=0, concat_axis=0,...  9.19 us
    all_to_all x1, waiting for transfers between devices, to_all(): lax.all_to_all(value, ('expert', 'hidden'), split_axis=0, concat_axis=0,...  7.41 us
    unnamed x16, local copies, waits for them, and re-layouts  7.07 us
    pallas_call x7, Pallas kernels, call(): pl.pallas_call(kernel, out_shape=outs, in_specs=[VMEM] * len(args), out_s...  5.93 us
    ppermute x6, waiting for transfers between devices, exchange(): lax.ppermute(value, axis, [(source, source ^ step) for source in range(si...  4.33 us
    all_to_all x1, starting transfers between devices, to_all(): lax.all_to_all(value, ('expert', 'hidden'), split_axis=0, concat_axis=0,...  2.81 us
  transfers between devices with their start and end apart: 7, of which 4 were waited for; matrix products, arithmetic and copies ran while one was open for 3% of the time, Pallas kernels for 2%

profile of v1, /device:TPU:0, one launch (start us, length us, event | category | flops | bytes accessed | tf_op | source)
XLA Modules:
  0.0 48.4 jit_solution(3717297886653256951)
XLA Ops:
  0.6 0.9 %copy-done.2 = bf16[2,196,256]{2,0,1:T(2,128)(2,1)S(1)} copy-done((bf16[2,196,256]{2,0,1:T(2,128)(2,1)S(1)}, bf16[2,196,256]{2,0,1:T(2,128)(2,1)}, u32[]{:S(2)}) %copy-start.2) | copy-done | bytes 200728
  1.6 0.7 %copy-done.4 = bf16[256,8]{0,1:T(8,128)(2,1)S(1)} copy-done((bf16[256,8]{0,1:T(8,128)(2,1)S(1)}, bf16[256,8]{0,1:T(8,128)(2,1)}, u32[]{:S(2)}) %copy-start.4) | copy-done | bytes 4120
  2.2 0.2 logits.1
  2.5 3.0 %collective-permute-start = (f32[8,392]{1,0:T(8,128)S(1)}, f32[8,392]{1,0:T(8,128)S(1)}, u32[]{:S(2)}, u32[]{:S(2)}) collective-permute-start(f32[8,392]{1,0:T(8,128)S(1)} %get-tuple-element.11.refs_0_), channel_id=1, source_target_pairs={{0,1},{1,0},{2,3},{3,2},{4,5},{5,4},{6,7},{7,6},{8,9},{9,8},{10,11... | collective-permute-start | bytes 37640 | tf_op jit(solution)/shard_map/ppermute | solution.py:169
  5.5 2.6 %collective-permute-start.1 = (f32[8,392]{1,0:T(8,128)S(1)}, f32[8,392]{1,0:T(8,128)S(1)}, u32[]{:S(2)}, u32[]{:S(2)}) collective-permute-start(f32[8,392]{1,0:T(8,128)S(1)} %get-tuple-element.11.refs_0_), channel_id=1, source_target_pairs={{0,2},{1,3},{2,0},{3,1},{4,6},{5,7},{6,4},{7,5},{8,10},{9,11},{10,... | collective-permute-start | bytes 37640 | tf_op jit(solution)/shard_map/ppermute | solution.py:169
  8.1 0.0 collective-permute-start.2
  8.1 0.9 %copy-done.3 = bf16[2,196,256]{2,0,1:T(2,128)(2,1)S(1)} copy-done((bf16[2,196,256]{2,0,1:T(2,128)(2,1)S(1)}, bf16[2,196,256]{2,0,1:T(2,128)(2,1)}, u32[]{:S(2)}) %copy-start.3) | copy-done | bytes 200728
  9.0 0.1 rows.1.refs_5_.refs_2_
  9.1 0.7 %broadcast_in_dim.21 = f32[1,256]{1,0:T(1,128)S(1)} convert(bf16[1,256]{1,0:T(2,128)(2,1)} %param.12) | non-fusion elementwise | flops 256 | bytes 1536 | tf_op jit(solution)/shard_map/jit(_where)/broadcast_in_dim | solution.py:206
  9.8 0.0 collective-permute-done.refs_1_
  9.8 0.4 collective-permute-done.1.refs_2_
  10.2 3.4 %collective-permute-done.2.refs_3_ = f32[8,392]{1,0:T(8,128)S(1)} collective-permute-done((f32[8,392]{1,0:T(8,128)S(1)}, f32[8,392]{1,0:T(8,128)S(1)}, u32[]{:S(2)}, u32[]{:S(2)}) %collective-permute-start.2) | collective-permute-done | bytes 12576 | tf_op jit(solution)/shard_map/ppermute | solution.py:169
  13.6 1.1 %dispatch.1 = (bf16[8,4,4,256]{3,2,1,0:T(4,128)(2,1)}, f32[8,392]{1,0:T(8,128)S(1)}, f32[8,392]{1,0:T(8,128)S(1)}, f32[1,392]{1,0:T(1,128)S(1)}) custom-call(f32[8,392]{1,0:T(8,128)S(1)} %get-tuple-element.11.refs_0_, f32[8,392]{1,0:T(8,128)S(1)} %collective-permute-done.refs_1_, f32[8,392]{1,0:T(8,128)S(1)} %collective-permute-done.1.refs_2_, ...), custom_call_target="tpu_custom_call" | custom-call | tf_op jit(solution)/shard_map/dispatch/pallas_call | solution.py:156
  14.7 2.8 %all-to-all-start = ((bf16[32,4,256]{2,1,0:T(4,128)(2,1)}), bf16[32,4,256]{2,1,0:T(4,128)(2,1)S(1)}, u32[]{:S(2)}, u32[]{:S(2)}) async-start(bf16[32,4,256]{2,1,0:T(4,128)(2,1)} %bitcast.3), calls=%async_computation | async-start | bytes 131072 | tf_op jit(solution)/shard_map/all_to_all | solution.py:201
  17.5 0.1 select_bitcast_fusion
  17.6 7.4 %all-to-all-done = bf16[32,4,256]{2,1,0:T(4,128)(2,1)S(1)} async-done(((bf16[32,4,256]{2,1,0:T(4,128)(2,1)}), bf16[32,4,256]{2,1,0:T(4,128)(2,1)S(1)}, u32[]{:S(2)}, u32[]{:S(2)}) %all-to-all-start) | async-done | bytes 65568 | tf_op jit(solution)/shard_map/all_to_all | solution.py:201
  25.0 1.6 %copy-done = bf16[1,1024,1024]{2,1,0:T(8,128)(2,1)S(1)} copy-done((bf16[1,1024,1024]{2,1,0:T(8,128)(2,1)S(1)}, bf16[1,1024,1024]{2,1,0:T(8,128)(2,1)}, u32[]{:S(2)}) %copy-start) | copy-done | bytes 2097176
  26.6 1.6 %copy-done.1 = bf16[1,1024,1024]{2,1,0:T(8,128)(2,1)S(1)} copy-done((bf16[1,1024,1024]{2,1,0:T(8,128)(2,1)S(1)}, bf16[1,1024,1024]{2,1,0:T(8,128)(2,1)}, u32[]{:S(2)}) %copy-start.1) | copy-done | bytes 2097176
  28.2 0.7 %copy-done.6 = bf16[1,1024]{1,0:T(2,128)(2,1)S(1)} copy-done((bf16[1,1024]{1,0:T(2,128)(2,1)S(1)}, bf16[1,1024]{1,0:T(2,128)(2,1)}, u32[]{:S(2)}) %copy-start.6) | copy-done | bytes 2072
  28.9 2.1 %expert.1 = bf16[8,4,4,256]{3,2,1,0:T(4,128)(2,1)S(1)} custom-call(bf16[8,4,4,256]{3,2,1,0:T(4,128)(2,1)S(1)} %bitcast.19, bf16[1024,1024]{1,0:T(8,128)(2,1)S(1)} %bitcast.17, bf16[1,1024]{1,0:T(2,128)(2,1)S(1)} %copy-done.6, bf16[1024,1024]{1,0:T(8,128)(2,1)S(1)} %bitcast.18, f32[1,1024]{1,0:T(1,128)S(1)} %bitcast.26), custom_call_target="tpu_custom_call" | custom-call | tf_op jit(solution)/shard_map/expert/pallas_call | solution.py:156
  31.0 9.2 %all_to_all.10 = bf16[32,4,256]{2,1,0:T(4,128)(2,1)S(1)} all-to-all(bf16[32,4,256]{2,1,0:T(4,128)(2,1)S(1)} %bitcast.20), channel_id=1, replica_groups=mesh['expert'=8,'hidden'=4] {'expert','hidden'}, dimensions={0} | all-to-all | bytes 131072 | tf_op jit(solution)/shard_map/all_to_all | solution.py:201
  40.2 0.3 gradient.1
  40.5 0.2 collective-permute-start.3
  40.8 1.1 %collective-permute-start.4 = (bf16[8,392]{1,0:T(8,128)(2,1)S(1)}, bf16[8,392]{1,0:T(8,128)(2,1)S(1)}, u32[]{:S(2)}, u32[]{:S(2)}) collective-permute-start(bf16[8,392]{1,0:T(8,128)(2,1)S(1)} %get-tuple-element.17.refs_0_), channel_id=1, source_target_pairs={{0,2},{1,3},{2,0},{3,1},{4,6},{5,7},{6,4},{7,5},{8,10},{9,11},{10,... | collective-permute-start | bytes 18824 | tf_op jit(solution)/shard_map/ppermute | solution.py:169
  41.8 3.1 %collective-permute-start.5 = (bf16[8,392]{1,0:T(8,128)(2,1)S(1)}, bf16[8,392]{1,0:T(8,128)(2,1)S(1)}, u32[]{:S(2)}, u32[]{:S(2)}) collective-permute-start(bf16[8,392]{1,0:T(8,128)(2,1)S(1)} %get-tuple-element.17.refs_0_), channel_id=1, source_target_pairs={{0,3},{1,2},{2,1},{3,0},{4,7},{5,6},{6,5},{7,4},{8,11},{9,10},{10,... | collective-permute-start | bytes 18824 | tf_op jit(solution)/shard_map/ppermute | solution.py:169
  44.9 0.1 reshape.49
  45.1 0.7 %copy.11 = f32[2,196]{1,0:T(2,128)} copy(f32[2,196]{0,1:T(8,128)S(1)} %bitcast.27) | data formatting | bytes 3136
  45.7 1.1 %mixed.1 = bf16[196,2,256]{2,1,0:T(2,128)(2,1)} custom-call(f32[8,392]{1,0:T(8,128)S(1)} %get-tuple-element.13.refs_4_.refs_0_.refs_5_, bf16[32,256]{1,0:T(8,128)(2,1)S(1)} %get-tuple-element.16.refs_1_.refs_8_), custom_call_target="tpu_custom_call" | custom-call | tf_op jit(solution)/shard_map/mixed/pallas_call | solution.py:156
  46.8 0.0 collective-permute-done.3.refs_1_
  46.8 0.0 collective-permute-done.4.refs_2_
  46.8 0.5 collective-permute-done.5.refs_3_
  47.3 1.1 %token_grad.1 = bf16[196,2,256]{2,1,0:T(2,128)(2,1)} custom-call(bf16[8,392]{1,0:T(8,128)(2,1)S(1)} %get-tuple-element.17.refs_0_, bf16[8,392]{1,0:T(8,128)(2,1)S(1)} %collective-permute-done.3.refs_1_, bf16[8,392]{1,0:T(8,128)(2,1)S(1)} %collective-permute-done.4.refs_2_, bf16[8,392]{1,0:T(8,128)(2,1)S(1)} %collective-permute-done.5.refs_3_, ...), custom_call_target="tpu_custom_call" | custom-call | tf_op jit(solution)/shard_map/token_grad/pallas_call | solution.py:156
  (11 shorter events, 0.0 us)
Async XLA Ops:
  0.6 0.9 %copy-start.2 = (bf16[2,196,256]{2,0,1:T(2,128)(2,1)S(1)}, bf16[2,196,256]{2,0,1:T(2,128)(2,1)}, u32[]{:S(2)}) copy-start(bf16[2,196,256]{2,0,1:T(2,128)(2,1)} %param.7) | copy-start | bytes 602116
  1.6 0.7 %copy-start.4 = (bf16[256,8]{0,1:T(8,128)(2,1)S(1)}, bf16[256,8]{0,1:T(8,128)(2,1)}, u32[]{:S(2)}) copy-start(bf16[256,8]{0,1:T(8,128)(2,1)} %param.8) | copy-start | bytes 12292
  2.5 7.3 %collective-permute-start = (f32[8,392]{1,0:T(8,128)S(1)}, f32[8,392]{1,0:T(8,128)S(1)}, u32[]{:S(2)}, u32[]{:S(2)}) collective-permute-start(f32[8,392]{1,0:T(8,128)S(1)} %get-tuple-element.11.refs_0_), channel_id=1, source_target_pairs={{0,1},{1,0},{2,3},{3,2},{4,5},{5,4},{6,7},{7,6},{8,9},{9,8},{10,11... | collective-permute-start | bytes 37640 | tf_op jit(solution)/shard_map/ppermute | solution.py:169
  5.5 4.7 %collective-permute-start.1 = (f32[8,392]{1,0:T(8,128)S(1)}, f32[8,392]{1,0:T(8,128)S(1)}, u32[]{:S(2)}, u32[]{:S(2)}) collective-permute-start(f32[8,392]{1,0:T(8,128)S(1)} %get-tuple-element.11.refs_0_), channel_id=1, source_target_pairs={{0,2},{1,3},{2,0},{3,1},{4,6},{5,7},{6,4},{7,5},{8,10},{9,11},{10,... | collective-permute-start | bytes 37640 | tf_op jit(solution)/shard_map/ppermute | solution.py:169
  8.1 5.5 %collective-permute-start.2 = (f32[8,392]{1,0:T(8,128)S(1)}, f32[8,392]{1,0:T(8,128)S(1)}, u32[]{:S(2)}, u32[]{:S(2)}) collective-permute-start(f32[8,392]{1,0:T(8,128)S(1)} %get-tuple-element.11.refs_0_), channel_id=1, source_target_pairs={{0,3},{1,2},{2,1},{3,0},{4,7},{5,6},{6,5},{7,4},{8,11},{9,10},{10,... | collective-permute-start | bytes 37640 | tf_op jit(solution)/shard_map/ppermute | solution.py:169
  8.1 0.9 %copy-start.3 = (bf16[2,196,256]{2,0,1:T(2,128)(2,1)S(1)}, bf16[2,196,256]{2,0,1:T(2,128)(2,1)}, u32[]{:S(2)}) copy-start(bf16[2,196,256]{2,0,1:T(2,128)(2,1)} %param.13) | copy-start | bytes 602116
  14.7 10.3 %all-to-all-start = ((bf16[32,4,256]{2,1,0:T(4,128)(2,1)}), bf16[32,4,256]{2,1,0:T(4,128)(2,1)S(1)}, u32[]{:S(2)}, u32[]{:S(2)}) async-start(bf16[32,4,256]{2,1,0:T(4,128)(2,1)} %bitcast.3), calls=%async_computation | async-start | bytes 131072 | tf_op jit(solution)/shard_map/all_to_all | solution.py:201
  25.0 1.6 %copy-start = (bf16[1,1024,1024]{2,1,0:T(8,128)(2,1)S(1)}, bf16[1,1024,1024]{2,1,0:T(8,128)(2,1)}, u32[]{:S(2)}) copy-start(bf16[1,1024,1024]{2,1,0:T(8,128)(2,1)} %param.9) | copy-start | bytes 6291460
  26.6 1.6 %copy-start.1 = (bf16[1,1024,1024]{2,1,0:T(8,128)(2,1)S(1)}, bf16[1,1024,1024]{2,1,0:T(8,128)(2,1)}, u32[]{:S(2)}) copy-start(bf16[1,1024,1024]{2,1,0:T(8,128)(2,1)} %param.11) | copy-start | bytes 6291460
  28.2 0.7 %copy-start.6 = (bf16[1,1024]{1,0:T(2,128)(2,1)S(1)}, bf16[1,1024]{1,0:T(2,128)(2,1)}, u32[]{:S(2)}) copy-start(bf16[1,1024]{1,0:T(2,128)(2,1)} %refs_2_.1) | copy-start | bytes 6148
  28.9 18.4 %copy-start.5 = (bf16[256,8]{0,1:T(8,128)(2,1)S(1)}, bf16[256,8]{0,1:T(8,128)(2,1)}, u32[]{:S(2)}) copy-start(bf16[256,8]{0,1:T(8,128)(2,1)} %param.8) | copy-start | bytes 12292
  40.5 6.3 %collective-permute-start.3 = (bf16[8,392]{1,0:T(8,128)(2,1)S(1)}, bf16[8,392]{1,0:T(8,128)(2,1)S(1)}, u32[]{:S(2)}, u32[]{:S(2)}) collective-permute-start(bf16[8,392]{1,0:T(8,128)(2,1)S(1)} %get-tuple-element.17.refs_0_), channel_id=1, source_target_pairs={{0,1},{1,0},{2,3},{3,2},{4,5},{5,4},{6,7},{7,6},{8,9},{9,8},{10,11... | collective-permute-start | bytes 18824 | tf_op jit(solution)/shard_map/ppermute | solution.py:169
  40.8 6.0 %collective-permute-start.4 = (bf16[8,392]{1,0:T(8,128)(2,1)S(1)}, bf16[8,392]{1,0:T(8,128)(2,1)S(1)}, u32[]{:S(2)}, u32[]{:S(2)}) collective-permute-start(bf16[8,392]{1,0:T(8,128)(2,1)S(1)} %get-tuple-element.17.refs_0_), channel_id=1, source_target_pairs={{0,2},{1,3},{2,0},{3,1},{4,6},{5,7},{6,4},{7,5},{8,10},{9,11},{10,... | collective-permute-start | bytes 18824 | tf_op jit(solution)/shard_map/ppermute | solution.py:169
  41.8 5.4 %collective-permute-start.5 = (bf16[8,392]{1,0:T(8,128)(2,1)S(1)}, bf16[8,392]{1,0:T(8,128)(2,1)S(1)}, u32[]{:S(2)}, u32[]{:S(2)}) collective-permute-start(bf16[8,392]{1,0:T(8,128)(2,1)S(1)} %get-tuple-element.17.refs_0_), channel_id=1, source_target_pairs={{0,3},{1,2},{2,1},{3,0},{4,7},{5,6},{6,5},{7,4},{8,11},{9,10},{10,... | collective-permute-start | bytes 18824 | tf_op jit(solution)/shard_map/ppermute | solution.py:169

commit v2 on v1

--- a/solution.py
+++ b/solution.py
@@ -1,6 +1,5 @@
 import jax
 import jax.numpy as jnp
-import numpy as np
 from jax import lax
 from jax.experimental import pallas as pl
 from jax.experimental.pallas import tpu as pltpu
@@ -9,6 +8,7 @@
 loss_weight = 0.1
 f32, bf16 = jnp.float32, jnp.bfloat16
 VMEM = pl.BlockSpec(memory_space=pltpu.VMEM)
+HBM = pl.BlockSpec(memory_space=pltpu.HBM)
 MIB = 1024 * 1024
 
 
@@ -60,16 +60,37 @@
     return jnp.broadcast_to(result, values.shape)
 
 
-def logits_kernel(tokens_ref, keys_ref, part_ref, rows_ref):
+def load(sources, targets, sems):
+    copies = [pltpu.make_async_copy(*pair, sems.at[k]) for k, pair in enumerate(zip(sources, targets))]
+    for copy in copies:
+        copy.start()
+    return copies
+
+
+def logits_kernel(tokens_ref, keys_in_ref, part_ref, rows_ref, keys_ref, held_ref, sems):
     tokens, images, width = tokens_ref.shape
-    rows = tokens_ref[...].reshape(tokens * images, width)
+    for copy in load((tokens_ref, keys_in_ref), (held_ref, keys_ref), sems):
+        copy.wait()
+    rows = held_ref[...].reshape(tokens * images, width)
     rows_ref[...] = rows
     part_ref[...] = dot(keys_ref[...], rows, 1, 1)
 
 
-def rows_kernel(tokens_ref, rows_ref):
+def prepare_kernel(axis, after_ref, tokens_ref, win_in_ref, bin_in_ref, wout_in_ref, bout_in_ref,
+                   rows_ref, win_ref, bin_ref, wout_ref, bout_ref, held_ref, held_bout_ref, sems):
+    del after_ref
     tokens, images, width = tokens_ref.shape
-    rows_ref[...] = tokens_ref[...].reshape(tokens * images, width)
+    sources = (tokens_ref, bout_in_ref, bin_in_ref, win_in_ref, wout_in_ref)
+    copies = load(sources, (held_ref, held_bout_ref, bin_ref, win_ref, wout_ref), sems)
+    for copy in copies[:2]:
+        copy.wait()
+    rows_ref[...] = held_ref[...].reshape(tokens * images, width)
+    own = lax.axis_index(axis)
+    for index in range(bout_ref.shape[1] // width):
+        bias = jnp.where(own == index, held_bout_ref[...].astype(f32), 0.0)
+        bout_ref[:, index * width : (index + 1) * width] = bias
+    for copy in copies[2:]:
+        copy.wait()
 
 
 def tree_sum(refs):
@@ -105,12 +126,17 @@
     groups, hidden, places, width = came_ref.shape
     rows = groups * places
     came = jnp.concatenate([came_ref[:, index].reshape(rows, width) for index in range(hidden)], axis=1)
-    pre = dot(came, win_ref[...], 1, 0) + bin_ref[...].astype(f32)
-    hidden_grad = dot(came, wout_ref[...], 1, 1)
-    activated, slope = gelu_parts(pre)
-    out = dot(activated.astype(bf16), wout_ref[...], 1, 0) + bout_ref[...]
-    pre_grad = (hidden_grad * pltpu.roll(slope, images, 0)).astype(bf16)
-    back = dot(pre_grad, win_ref[...], 1, 1)
+    units = win_ref.shape[1]
+    step = 256 if units % 256 == 0 else units
+    out, back = bout_ref[...], 0.0
+    for start in range(0, units, step):
+        part = slice(start, start + step)
+        pre = dot(came, win_ref[:, part], 1, 0) + bin_ref[:, part].astype(f32)
+        hidden_grad = dot(came, wout_ref[part], 1, 1)
+        activated, slope = gelu_parts(pre)
+        out = out + dot(activated.astype(bf16), wout_ref[part], 1, 0)
+        pre_grad = (hidden_grad * pltpu.roll(slope, images, 0)).astype(bf16)
+        back = back + dot(pre_grad, win_ref[:, part], 1, 1)
     forward = modulo(iota(out.shape, 0), places) < images
     sent = jnp.where(forward, out, back).astype(bf16)
     for index in range(hidden):
@@ -136,28 +162,32 @@
     part_ref[...] = part.astype(bf16)
 
 
-def mixed_kernel(images, combine_ref, slots_ref, out_ref):
-    forward, _ = slot_masks(slots_ref.shape[0], combine_ref.shape[1], images)
+def mixed_kernel(images, dispatch_ref, combine_ref, slots_ref, out_ref, direct_ref):
+    forward, backward = slot_masks(slots_ref.shape[0], combine_ref.shape[1], images)
     left = jnp.where(forward, spread(combine_ref[...].astype(bf16), images), 0.0).astype(bf16)
     out_ref[...] = dot(left, slots_ref[...], 0, 0).astype(bf16).reshape(out_ref.shape)
-
-
-def token_kernel(images, count, *refs):
-    parts, (dispatch_ref, combine_ref, total_ref, keys_ref, slots_ref, out_ref) = refs[:count], refs[count:]
-    combine = combine_ref[...]
-    logit_grad = tree_sum(parts) + 2.0 * loss_weight * total_ref[...] * combine
-    _, backward = slot_masks(slots_ref.shape[0], combine.shape[1], images)
     left = jnp.where(backward, spread(dispatch_ref[...].astype(bf16), images), 0.0).astype(bf16)
-    out = dot(logit_grad.astype(bf16), keys_ref[...], 0, 0) + dot(left, slots_ref[...], 0, 0)
+    direct_ref[...] = dot(left, slots_ref[...], 0, 0)
+
+
+def token_kernel(count, *refs):
+    parts, (combine_ref, total_ref, keys_ref, direct_ref, out_ref) = refs[:count], refs[count:]
+    logit_grad = tree_sum(parts) + 2.0 * loss_weight * total_ref[...] * combine_ref[...]
+    out = dot(logit_grad.astype(bf16), keys_ref[...], 0, 0) + direct_ref[...]
     out_ref[...] = out.astype(bf16).reshape(out_ref.shape)
 
 
-def call(kernel, outs, args, name, limit=8):
+def stay(value):
+    return pltpu.with_memory_space_constraint(value, pltpu.HBM)
+
+
+def call(kernel, outs, args, name, limit=8, place=VMEM, scratch=()):
     return pl.pallas_call(
         kernel,
         out_shape=outs,
-        in_specs=[VMEM] * len(args),
+        in_specs=[place] * len(args),
         out_specs=[VMEM] * len(outs),
+        scratch_shapes=scratch,
         compiler_params=pltpu.CompilerParams(vmem_limit_bytes=limit * MIB),
         name=name,
     )(*args)
@@ -171,22 +201,44 @@
     ]
 
 
+def prepare(after, cotangent, weight_in, bias_in, weight_out, bias_out, row_shape, held_shape):
+    wide = weight_in.shape[0]
+    shapes = [pltpu.VMEM(value.shape, bf16) for value in (weight_in, bias_in, weight_out)]
+    specs = [VMEM if value is after else HBM for value in (after, cotangent, weight_in, bias_in, weight_out, bias_out)]
+    return pl.pallas_call(
+        lambda *refs: prepare_kernel("hidden", *refs),
+        out_shape=[row_shape, *shapes, pltpu.VMEM((1, wide), f32)],
+        in_specs=specs,
+        out_specs=[VMEM] * 5,
+        scratch_shapes=[held_shape, pltpu.VMEM(bias_out.shape, bf16), pltpu.SemaphoreType.DMA((5,))],
+        compiler_params=pltpu.CompilerParams(vmem_limit_bytes=16 * MIB),
+        name="prepare",
+    )(after, *map(stay, (cotangent, weight_in, bias_in, weight_out, bias_out)))
+
+
 def per_device(tokens, slot_params, weight_in, bias_in, weight_out, bias_out, cotangent):
     images, count, width = tokens.shape
     groups, hidden = lax.axis_size("expert"), lax.axis_size("hidden")
     slots = slot_params.shape[1]
-    wide = weight_in.shape[1]
     rows = images * count
     by_token = jnp.transpose(tokens, (1, 0, 2))
     grad_by_token = jnp.transpose(cotangent, (1, 0, 2))
-    keys = jnp.transpose(slot_params)
     table = pltpu.VMEM((slots, rows), f32)
+    row_shape = pltpu.VMEM((rows, width), bf16)
+    held_shape = pltpu.VMEM(by_token.shape, bf16)
     sent_shape = pltpu.VMEM((groups, hidden, 2 * images, width), bf16)
 
-    part, token_rows = call(
-        logits_kernel, [table, pltpu.VMEM((rows, width), bf16)], (by_token, keys), "logits"
-    )
-    (grad_rows,) = call(rows_kernel, [pltpu.VMEM((rows, width), bf16)], (grad_by_token,), "rows")
+    part, token_rows, keys = call(
+        logits_kernel,
+        [table, row_shape, pltpu.VMEM((slots, width), bf16)],
+        (stay(by_token), stay(jnp.transpose(slot_params))),
+        "logits",
+        place=HBM,
+        scratch=[held_shape, pltpu.SemaphoreType.DMA((2,))],
+    )
+    grad_rows, win, bin_, wout, bout = prepare(
+        part, grad_by_token, weight_in[0], bias_in, weight_out[0], bias_out, row_shape, held_shape
+    )
     parts = exchange(part, "hidden")
     sent, dispatch, combine, total = call(
         lambda *refs: dispatch_kernel(images, hidden, *refs),
@@ -201,13 +253,10 @@
         value = lax.all_to_all(value, ("expert", "hidden"), split_axis=0, concat_axis=0, tiled=True)
         return value.reshape(groups, hidden, 2 * images, width)
 
-    own = lax.axis_index("hidden")
-    here = lax.broadcasted_iota(jnp.int32, (hidden, width), 0) == own
-    bias = jnp.where(here, bias_out.astype(f32), 0.0).reshape(1, wide)
     (sent,) = call(
         lambda *refs: expert_kernel(images, *refs),
         [sent_shape],
-        (to_all(sent), weight_in[0], bias_in, weight_out[0], bias),
+        (to_all(sent), win, bin_, wout, bout),
         "expert",
         24,
     )
@@ -219,13 +268,16 @@
     )
     out_shape = jax.ShapeDtypeStruct((count, images, width), bf16)
     parts = exchange(part, "hidden")
-    (mixed,) = call(
-        lambda *refs: mixed_kernel(images, *refs), [out_shape], (combine, slot_rows), "mixed"
+    mixed, direct = call(
+        lambda *refs: mixed_kernel(images, *refs),
+        [out_shape, pltpu.VMEM((rows, width), f32)],
+        (dispatch, combine, slot_rows),
+        "mixed",
     )
     (token_grad,) = call(
-        lambda *refs: token_kernel(images, hidden, *refs),
+        lambda *refs: token_kernel(hidden, *refs),
         [out_shape],
-        (*parts, dispatch, combine, total, keys, slot_rows),
+        (*parts, combine, total, keys, direct),
         "token_grad",
     )
     return (jnp.transpose(mixed, (1, 0, 2)), jnp.transpose(token_grad, (1, 0, 2)), zloss)

time: 48.7 us -> 43.4 us (0.89)
  blocking collectives: 9.19 us -> 19.5 us
  waiting for transfers between devices: 11.7 us -> 3.53 us
  local copies, waits for them, and re-layouts: 7.21 us -> 0.8 us
  starting transfers between devices: 12.8 us -> 10.1 us
  Pallas kernels: 5.93 us -> 8.62 us
  other arithmetic: 0.78 us -> 0.02 us
    all_to_all x1 -> x2, blocking collectives: 9.19 us -> 19.5 us  [to_all(): lax.all_to_all(value, ('expert', 'hidden'), split_axis=0, concat_axis=0,...]
    all_to_all x1 -> x0, waiting for transfers between devices: 7.41 us -> none  [to_all(): lax.all_to_all(value, ('expert', 'hidden'), split_axis=0, concat_axis=0,...]
    unnamed x16 -> x1, local copies, waits for them, and re-layouts: 7.07 us -> 0.66 us
    all_to_all x1 -> x0, starting transfers between devices: 2.81 us -> none  [to_all(): lax.all_to_all(value, ('expert', 'hidden'), split_axis=0, concat_axis=0,...]
    pallas_call x7, Pallas kernels: 5.93 us -> 8.62 us  [the longest x6 6.2 us: call(): pl.pallas_call(kernel, out_shape=outs, in_specs=[place] * len(args), out_...]
    ppermute x6, waiting for transfers between devices: 4.33 us -> 3.53 us  [exchange(): lax.ppermute(value, axis, [(source, source ^ step) for source in range(si...]
    broadcast_in_dim x1 -> x0, other arithmetic: 0.68 us -> none  [per_device(): bias = jnp.where(here, bias_out.astype(f32), 0.0).reshape(1, wide)]
  transfers between devices with their start and end apart: 7 -> 6, of which waited for: 4 -> 2; matrix products, arithmetic and copies ran while one was open for 3% -> 2% of each run, Pallas kernels for 2% -> 8%
where the time goes in v2:
time: 43.4 us; the launch traced here: 43.2 us
  blocking collectives  19.5 us (45%)
  starting transfers between devices  10.1 us (23%)
  Pallas kernels  8.62 us (20%)
  waiting for transfers between devices  3.53 us (8%)
  local copies, waits for them, and re-layouts  0.8 us (2%)
  between operations  0.69 us (2%)
    all_to_all x2, blocking collectives, to_all(): lax.all_to_all(value, ('expert', 'hidden'), split_axis=0, concat_axis=0,...  19.5 us
    ppermute x6, starting transfers between devices, exchange(): lax.ppermute(value, axis, [(source, source ^ step) for source in range(si...  10.1 us
    pallas_call x6, Pallas kernels, call(): pl.pallas_call(kernel, out_shape=outs, in_specs=[place] * len(args), out_...  6.2 us
    ppermute x6, waiting for transfers between devices, exchange(): lax.ppermute(value, axis, [(source, source ^ step) for source in range(si...  3.53 us
    pallas_call x1, Pallas kernels, prepare(): pl.pallas_call(lambda *refs: prepare_kernel('hidden', *refs), out_shape=[...  2.42 us
  transfers between devices with their start and end apart: 6, of which 2 were waited for; matrix products, arithmetic and copies ran while one was open for 2% of the time, Pallas kernels for 8%

profile of v2, /device:TPU:0, one launch (start us, length us, event | category | flops | bytes accessed | tf_op | source)
XLA Modules:
  0.0 43.2 jit_solution(11633067525817325689)
XLA Ops:
  0.6 1.2 %logits.1 = (f32[8,392]{1,0:T(8,128)S(1)}, bf16[392,256]{1,0:T(8,128)(2,1)S(1)}, bf16[8,256]{1,0:T(8,128)(2,1)S(1)}) custom-call(bf16[196,2,256]{2,1,0:T(2,128)(2,1)} %bitcast.20, bf16[8,256]{1,0:T(8,128)(2,1)} %bitcast.22), custom_call_target="tpu_custom_call" | custom-call | tf_op jit(solution)/shard_map/logits/pallas_call | solution.py:185
  1.8 3.1 %collective-permute-start = (f32[8,392]{1,0:T(8,128)S(1)}, f32[8,392]{1,0:T(8,128)S(1)}, u32[]{:S(2)}, u32[]{:S(2)}) collective-permute-start(f32[8,392]{1,0:T(8,128)S(1)} %get-tuple-element.19.refs_0_), channel_id=1, source_target_pairs={{0,1},{1,0},{2,3},{3,2},{4,5},{5,4},{6,7},{7,6},{8,9},{9,8},{10,11... | collective-permute-start | bytes 37640 | tf_op jit(solution)/shard_map/ppermute | solution.py:199
  4.9 2.6 %collective-permute-start.1 = (f32[8,392]{1,0:T(8,128)S(1)}, f32[8,392]{1,0:T(8,128)S(1)}, u32[]{:S(2)}, u32[]{:S(2)}) collective-permute-start(f32[8,392]{1,0:T(8,128)S(1)} %get-tuple-element.19.refs_0_), channel_id=1, source_target_pairs={{0,2},{1,3},{2,0},{3,1},{4,6},{5,7},{6,4},{7,5},{8,10},{9,11},{10,... | collective-permute-start | bytes 37640 | tf_op jit(solution)/shard_map/ppermute | solution.py:199
  7.5 0.0 collective-permute-start.2
  7.5 2.4 %prepare.1 = (bf16[392,256]{1,0:T(8,128)(2,1)S(1)}, bf16[1024,1024]{1,0:T(8,128)(2,1)S(1)}, bf16[1,1024]{1,0:T(2,128)(2,1)S(1)}, bf16[1024,1024]{1,0:T(8,128)(2,1)S(1)}, f32[1,1024]{1,0:T(1,128)S(1)}) custom-call(f32[8,392]{1,0:T(8,128)S(1)} %get-tuple-element.19.refs_0_, bf16[196,2,256]{2,1,0:T(2,128)(2,1)} %bitcast.19, bf16[1024,1024]{1,0:T(8,128)(2,1)} %bitcast.16, ...), custom_call_target="tpu_custom_call" | custom-call | tf_op jit(solution)/shard_map/prepare/pallas_call | solution.py:208
  9.9 0.0 collective-permute-done.refs_1_
  9.9 0.0 collective-permute-done.1.refs_2_
  9.9 3.1 %collective-permute-done.2.refs_3_ = f32[8,392]{1,0:T(8,128)S(1)} collective-permute-done((f32[8,392]{1,0:T(8,128)S(1)}, f32[8,392]{1,0:T(8,128)S(1)}, u32[]{:S(2)}, u32[]{:S(2)}) %collective-permute-start.2) | collective-permute-done | bytes 12576 | tf_op jit(solution)/shard_map/ppermute | solution.py:199
  13.0 0.5 %dispatch.1 = (bf16[8,4,4,256]{3,2,1,0:T(4,128)(2,1)S(1)}, f32[8,392]{1,0:T(8,128)S(1)}, f32[8,392]{1,0:T(8,128)S(1)}, f32[1,392]{1,0:T(1,128)S(1)}) custom-call(f32[8,392]{1,0:T(8,128)S(1)} %get-tuple-element.19.refs_0_, f32[8,392]{1,0:T(8,128)S(1)} %collective-permute-done.refs_1_, f32[8,392]{1,0:T(8,128)S(1)} %collective-permute-done.1.refs_2_, ...), custom_call_target="tpu_custom_call" | custom-call | tf_op jit(solution)/shard_map/dispatch/pallas_call | solution.py:185
  13.5 10.3 %all_to_all.10 = bf16[32,4,256]{2,1,0:T(4,128)(2,1)S(1)} all-to-all(bf16[32,4,256]{2,1,0:T(4,128)(2,1)S(1)} %bitcast.15), channel_id=1, replica_groups=mesh['expert'=8,'hidden'=4] {'expert','hidden'}, dimensions={0} | all-to-all | bytes 131072 | tf_op jit(solution)/shard_map/all_to_all | solution.py:253
  23.8 2.2 %expert.1 = bf16[8,4,4,256]{3,2,1,0:T(4,128)(2,1)S(1)} custom-call(bf16[8,4,4,256]{3,2,1,0:T(4,128)(2,1)S(1)} %bitcast.12, bf16[1024,1024]{1,0:T(8,128)(2,1)S(1)} %get-tuple-element.25.refs_1_, bf16[1,1024]{1,0:T(2,128)(2,1)S(1)} %get-tuple-element.26.refs_2_, bf16[1024,1024]{1,0:T(8,128)(2,1)S(1)} %get-tuple-element.27.refs_3_, ...), custom_call_target="tpu_custom_call" | custom-call | tf_op jit(solution)/shard_map/expert/pallas_call | solution.py:185
  26.0 9.2 %all_to_all.11 = bf16[32,4,256]{2,1,0:T(4,128)(2,1)S(1)} all-to-all(bf16[32,4,256]{2,1,0:T(4,128)(2,1)S(1)} %bitcast.13), channel_id=1, replica_groups=mesh['expert'=8,'hidden'=4] {'expert','hidden'}, dimensions={0} | all-to-all | bytes 131072 | tf_op jit(solution)/shard_map/all_to_all | solution.py:253
  35.2 0.3 gradient.1
  35.5 0.2 collective-permute-start.3
  35.8 1.1 %collective-permute-start.4 = (bf16[8,392]{1,0:T(8,128)(2,1)S(1)}, bf16[8,392]{1,0:T(8,128)(2,1)S(1)}, u32[]{:S(2)}, u32[]{:S(2)}) collective-permute-start(bf16[8,392]{1,0:T(8,128)(2,1)S(1)} %get-tuple-element.31.refs_0_), channel_id=1, source_target_pairs={{0,2},{1,3},{2,0},{3,1},{4,6},{5,7},{6,4},{7,5},{8,10},{9,11},{10,... | collective-permute-start | bytes 18824 | tf_op jit(solution)/shard_map/ppermute | solution.py:199
  36.8 3.1 %collective-permute-start.5 = (bf16[8,392]{1,0:T(8,128)(2,1)S(1)}, bf16[8,392]{1,0:T(8,128)(2,1)S(1)}, u32[]{:S(2)}, u32[]{:S(2)}) collective-permute-start(bf16[8,392]{1,0:T(8,128)(2,1)S(1)} %get-tuple-element.31.refs_0_), channel_id=1, source_target_pairs={{0,3},{1,2},{2,1},{3,0},{4,7},{5,6},{6,5},{7,4},{8,11},{9,10},{10,... | collective-permute-start | bytes 18824 | tf_op jit(solution)/shard_map/ppermute | solution.py:199
  39.9 0.1 reshape.25
  40.1 0.7 %copy.11 = f32[2,196]{1,0:T(2,128)} copy(f32[2,196]{0,1:T(8,128)S(1)} %bitcast.18) | data formatting | bytes 3136
  40.7 1.1 %mixed.1 = (bf16[196,2,256]{2,1,0:T(2,128)(2,1)}, f32[392,256]{1,0:T(8,128)S(1)}) custom-call(f32[8,392]{1,0:T(8,128)S(1)} %get-tuple-element.22.refs_3_.refs_0_, f32[8,392]{1,0:T(8,128)S(1)} %get-tuple-element.23.refs_4_.refs_1_, bf16[32,256]{1,0:T(8,128)(2,1)S(1)} %get-tuple-element.29.refs_2_), custom_call_target="tpu_custom_call" | custom-call | tf_op jit(solution)/shard_map/mixed/pallas_call | solution.py:185
  41.8 0.0 collective-permute-done.3.refs_1_
  41.8 0.0 collective-permute-done.4.refs_2_
  41.8 0.4 collective-permute-done.5.refs_3_
  42.3 0.9 %token_grad.1 = bf16[196,2,256]{2,1,0:T(2,128)(2,1)} custom-call(bf16[8,392]{1,0:T(8,128)(2,1)S(1)} %get-tuple-element.31.refs_0_, bf16[8,392]{1,0:T(8,128)(2,1)S(1)} %collective-permute-done.3.refs_1_, bf16[8,392]{1,0:T(8,128)(2,1)S(1)} %collective-permute-done.4.refs_2_, bf16[8,392]{1,0:T(8,128)(2,1)S(1)} %collective-permute-done.5.refs_3_, ...), custom_call_target="tpu_custom_call" | custom-call | tf_op jit(solution)/shard_map/token_grad/pallas_call | solution.py:185
  (1 shorter events, 0.0 us)
Async XLA Ops:
  1.8 8.1 %collective-permute-start = (f32[8,392]{1,0:T(8,128)S(1)}, f32[8,392]{1,0:T(8,128)S(1)}, u32[]{:S(2)}, u32[]{:S(2)}) collective-permute-start(f32[8,392]{1,0:T(8,128)S(1)} %get-tuple-element.19.refs_0_), channel_id=1, source_target_pairs={{0,1},{1,0},{2,3},{3,2},{4,5},{5,4},{6,7},{7,6},{8,9},{9,8},{10,11... | collective-permute-start | bytes 37640 | tf_op jit(solution)/shard_map/ppermute | solution.py:199
  4.9 5.0 %collective-permute-start.1 = (f32[8,392]{1,0:T(8,128)S(1)}, f32[8,392]{1,0:T(8,128)S(1)}, u32[]{:S(2)}, u32[]{:S(2)}) collective-permute-start(f32[8,392]{1,0:T(8,128)S(1)} %get-tuple-element.19.refs_0_), channel_id=1, source_target_pairs={{0,2},{1,3},{2,0},{3,1},{4,6},{5,7},{6,4},{7,5},{8,10},{9,11},{10,... | collective-permute-start | bytes 37640 | tf_op jit(solution)/shard_map/ppermute | solution.py:199
  7.5 5.5 %collective-permute-start.2 = (f32[8,392]{1,0:T(8,128)S(1)}, f32[8,392]{1,0:T(8,128)S(1)}, u32[]{:S(2)}, u32[]{:S(2)}) collective-permute-start(f32[8,392]{1,0:T(8,128)S(1)} %get-tuple-element.19.refs_0_), channel_id=1, source_target_pairs={{0,3},{1,2},{2,1},{3,0},{4,7},{5,6},{6,5},{7,4},{8,11},{9,10},{10,... | collective-permute-start | bytes 37640 | tf_op jit(solution)/shard_map/ppermute | solution.py:199
  35.5 6.3 %collective-permute-start.3 = (bf16[8,392]{1,0:T(8,128)(2,1)S(1)}, bf16[8,392]{1,0:T(8,128)(2,1)S(1)}, u32[]{:S(2)}, u32[]{:S(2)}) collective-permute-start(bf16[8,392]{1,0:T(8,128)(2,1)S(1)} %get-tuple-element.31.refs_0_), channel_id=1, source_target_pairs={{0,1},{1,0},{2,3},{3,2},{4,5},{5,4},{6,7},{7,6},{8,9},{9,8},{10,11... | collective-permute-start | bytes 18824 | tf_op jit(solution)/shard_map/ppermute | solution.py:199
  35.8 6.1 %collective-permute-start.4 = (bf16[8,392]{1,0:T(8,128)(2,1)S(1)}, bf16[8,392]{1,0:T(8,128)(2,1)S(1)}, u32[]{:S(2)}, u32[]{:S(2)}) collective-permute-start(bf16[8,392]{1,0:T(8,128)(2,1)S(1)} %get-tuple-element.31.refs_0_), channel_id=1, source_target_pairs={{0,2},{1,3},{2,0},{3,1},{4,6},{5,7},{6,4},{7,5},{8,10},{9,11},{10,... | collective-permute-start | bytes 18824 | tf_op jit(solution)/shard_map/ppermute | solution.py:199
  36.8 5.4 %collective-permute-start.5 = (bf16[8,392]{1,0:T(8,128)(2,1)S(1)}, bf16[8,392]{1,0:T(8,128)(2,1)S(1)}, u32[]{:S(2)}, u32[]{:S(2)}) collective-permute-start(bf16[8,392]{1,0:T(8,128)(2,1)S(1)} %get-tuple-element.31.refs_0_), channel_id=1, source_target_pairs={{0,3},{1,2},{2,1},{3,0},{4,7},{5,6},{6,5},{7,4},{8,11},{9,10},{10,... | collective-permute-start | bytes 18824 | tf_op jit(solution)/shard_map/ppermute | solution.py:199

commit v3 on v2

--- a/solution.py
+++ b/solution.py
@@ -76,8 +76,8 @@
     part_ref[...] = dot(keys_ref[...], rows, 1, 1)
 
 
-def prepare_kernel(axis, after_ref, tokens_ref, win_in_ref, bin_in_ref, wout_in_ref, bout_in_ref,
-                   rows_ref, win_ref, bin_ref, wout_ref, bout_ref, held_ref, held_bout_ref, sems):
+def prepare_kernel(axis, after_ref, tokens_ref, bout_in_ref, bin_in_ref, win_in_ref, wout_in_ref,
+                   rows_ref, bout_ref, bin_ref, win_ref, wout_ref, held_ref, held_bout_ref, sems):
     del after_ref
     tokens, images, width = tokens_ref.shape
     sources = (tokens_ref, bout_in_ref, bin_in_ref, win_in_ref, wout_in_ref)
@@ -93,8 +93,13 @@
         copy.wait()
 
 
+def steps(size):
+    return [1] + list(range(size - 1, 1, -1))
+
+
 def tree_sum(refs):
-    values = [ref[...].astype(f32) for ref in refs]
+    order = [0] + steps(len(refs))
+    values = [refs[order.index(step)][...].astype(f32) for step in range(len(refs))]
     while len(values) > 1:
         values = [values[k] + values[k + 1] for k in range(0, len(values), 2)]
     return values[0]
@@ -126,17 +131,12 @@
     groups, hidden, places, width = came_ref.shape
     rows = groups * places
     came = jnp.concatenate([came_ref[:, index].reshape(rows, width) for index in range(hidden)], axis=1)
-    units = win_ref.shape[1]
-    step = 256 if units % 256 == 0 else units
-    out, back = bout_ref[...], 0.0
-    for start in range(0, units, step):
-        part = slice(start, start + step)
-        pre = dot(came, win_ref[:, part], 1, 0) + bin_ref[:, part].astype(f32)
-        hidden_grad = dot(came, wout_ref[part], 1, 1)
-        activated, slope = gelu_parts(pre)
-        out = out + dot(activated.astype(bf16), wout_ref[part], 1, 0)
-        pre_grad = (hidden_grad * pltpu.roll(slope, images, 0)).astype(bf16)
-        back = back + dot(pre_grad, win_ref[:, part], 1, 1)
+    pre = dot(came, win_ref[...], 1, 0) + bin_ref[...].astype(f32)
+    hidden_grad = dot(came, wout_ref[...], 1, 1)
+    activated, slope = gelu_parts(pre)
+    out = dot(activated.astype(bf16), wout_ref[...], 1, 0) + bout_ref[...]
+    pre_grad = (hidden_grad * pltpu.roll(slope, images, 0)).astype(bf16)
+    back = dot(pre_grad, win_ref[...], 1, 1)
     forward = modulo(iota(out.shape, 0), places) < images
     sent = jnp.where(forward, out, back).astype(bf16)
     for index in range(hidden):
@@ -162,65 +162,64 @@
     part_ref[...] = part.astype(bf16)
 
 
-def mixed_kernel(images, dispatch_ref, combine_ref, slots_ref, out_ref, direct_ref):
+def mixed_kernel(images, dispatch_ref, combine_ref, total_ref, slots_ref, mixed_ref, direct_ref, loss_ref):
     forward, backward = slot_masks(slots_ref.shape[0], combine_ref.shape[1], images)
     left = jnp.where(forward, spread(combine_ref[...].astype(bf16), images), 0.0).astype(bf16)
-    out_ref[...] = dot(left, slots_ref[...], 0, 0).astype(bf16).reshape(out_ref.shape)
+    mixed_ref[...] = dot(left, slots_ref[...], 0, 0).astype(bf16).reshape(mixed_ref.shape)
     left = jnp.where(backward, spread(dispatch_ref[...].astype(bf16), images), 0.0).astype(bf16)
     direct_ref[...] = dot(left, slots_ref[...], 0, 0)
+    total = jnp.broadcast_to(total_ref[...], (8, total_ref.shape[1]))
+    tokens = loss_ref.shape[1]
+    row, token = iota((images * tokens, tokens), 0), iota((images * tokens, tokens), 1)
+    for index in range(images):
+        pick = jnp.where(row == images * token + index, 1.0, 0.0)
+        own = lax.dot_general(
+            total, pick, (((1,), (0,)), ((), ())), precision=lax.Precision.HIGHEST, preferred_element_type=f32
+        )[:1]
+        loss_ref[index : index + 1] = loss_weight * own * own
 
 
 def token_kernel(count, *refs):
-    parts, (combine_ref, total_ref, keys_ref, direct_ref, out_ref) = refs[:count], refs[count:]
+    parts, refs = refs[:count], refs[count:]
+    (combine_ref, total_ref, keys_ref, direct_ref, mixed_ref, loss_ref) = refs[:6]
+    (out_ref, mixed_out_ref, loss_out_ref, held_ref, sems) = refs[6:]
+    copies = load((mixed_ref, loss_ref), (mixed_out_ref, loss_out_ref), sems)
     logit_grad = tree_sum(parts) + 2.0 * loss_weight * total_ref[...] * combine_ref[...]
     out = dot(logit_grad.astype(bf16), keys_ref[...], 0, 0) + direct_ref[...]
-    out_ref[...] = out.astype(bf16).reshape(out_ref.shape)
-
-
-def stay(value):
-    return pltpu.with_memory_space_constraint(value, pltpu.HBM)
-
-
-def call(kernel, outs, args, name, limit=8, place=VMEM, scratch=()):
+    held_ref[...] = out.astype(bf16).reshape(held_ref.shape)
+    last = pltpu.make_async_copy(held_ref, out_ref, sems.at[2])
+    last.start()
+    for copy in (*copies, last):
+        copy.wait()
+
+
+def call(kernel, outs, args, name, limit=8, far=(), far_outs=False, scratch=(), cost=None):
     return pl.pallas_call(
         kernel,
         out_shape=outs,
-        in_specs=[place] * len(args),
-        out_specs=[VMEM] * len(outs),
+        in_specs=[VMEM] * len(args) + [HBM] * len(far),
+        out_specs=[HBM if far_outs else VMEM] * len(outs),
         scratch_shapes=scratch,
         compiler_params=pltpu.CompilerParams(vmem_limit_bytes=limit * MIB),
+        cost_estimate=cost,
         name=name,
-    )(*args)
+    )(*args, *(pltpu.with_memory_space_constraint(value, pltpu.HBM) for value in far))
 
 
 def exchange(value, axis):
     size = lax.axis_size(axis)
     return [value] + [
-        lax.ppermute(value, axis, [(source, source ^ step) for source in range(size)])
-        for step in range(1, size)
+        lax.ppermute(value, axis, [(source, source ^ step) for source in range(size)]) for step in steps(size)
     ]
-
-
-def prepare(after, cotangent, weight_in, bias_in, weight_out, bias_out, row_shape, held_shape):
-    wide = weight_in.shape[0]
-    shapes = [pltpu.VMEM(value.shape, bf16) for value in (weight_in, bias_in, weight_out)]
-    specs = [VMEM if value is after else HBM for value in (after, cotangent, weight_in, bias_in, weight_out, bias_out)]
-    return pl.pallas_call(
-        lambda *refs: prepare_kernel("hidden", *refs),
-        out_shape=[row_shape, *shapes, pltpu.VMEM((1, wide), f32)],
-        in_specs=specs,
-        out_specs=[VMEM] * 5,
-        scratch_shapes=[held_shape, pltpu.VMEM(bias_out.shape, bf16), pltpu.SemaphoreType.DMA((5,))],
-        compiler_params=pltpu.CompilerParams(vmem_limit_bytes=16 * MIB),
-        name="prepare",
-    )(after, *map(stay, (cotangent, weight_in, bias_in, weight_out, bias_out)))
 
 
 def per_device(tokens, slot_params, weight_in, bias_in, weight_out, bias_out, cotangent):
     images, count, width = tokens.shape
     groups, hidden = lax.axis_size("expert"), lax.axis_size("hidden")
     slots = slot_params.shape[1]
+    wide = weight_in.shape[1]
     rows = images * count
+    weight_in, weight_out = weight_in[0], weight_out[0]
     by_token = jnp.transpose(tokens, (1, 0, 2))
     grad_by_token = jnp.transpose(cotangent, (1, 0, 2))
     table = pltpu.VMEM((slots, rows), f32)
@@ -231,13 +230,18 @@
     part, token_rows, keys = call(
         logits_kernel,
         [table, row_shape, pltpu.VMEM((slots, width), bf16)],
-        (stay(by_token), stay(jnp.transpose(slot_params))),
+        (),
         "logits",
-        place=HBM,
+        far=(by_token, jnp.transpose(slot_params)),
         scratch=[held_shape, pltpu.SemaphoreType.DMA((2,))],
     )
-    grad_rows, win, bin_, wout, bout = prepare(
-        part, grad_by_token, weight_in[0], bias_in, weight_out[0], bias_out, row_shape, held_shape
+    grad_rows, bias_out, bias_in, weight_in, weight_out = call(
+        lambda *refs: prepare_kernel("hidden", *refs),
+        [row_shape, pltpu.VMEM((1, wide), f32), *[pltpu.VMEM(v.shape, bf16) for v in (bias_in, weight_in, weight_out)]],
+        (part,),
+        "prepare",
+        far=(grad_by_token, bias_out, bias_in, weight_in, weight_out),
+        scratch=[held_shape, pltpu.VMEM(bias_out.shape, bf16), pltpu.SemaphoreType.DMA((5,))],
     )
     parts = exchange(part, "hidden")
     sent, dispatch, combine, total = call(
@@ -246,7 +250,6 @@
         (*parts, token_rows, grad_rows),
         "dispatch",
     )
-    zloss = jnp.transpose((loss_weight * total * total).reshape(count, images))
 
     def to_all(value):
         value = value.reshape(groups * hidden, 2 * images, width)
@@ -256,7 +259,7 @@
     (sent,) = call(
         lambda *refs: expert_kernel(images, *refs),
         [sent_shape],
-        (to_all(sent), win, bin_, wout, bout),
+        (to_all(sent), weight_in, bias_in, weight_out, bias_out),
         "expert",
         24,
     )
@@ -266,19 +269,21 @@
         (to_all(sent), token_rows, grad_rows, dispatch, combine),
         "gradient",
     )
-    out_shape = jax.ShapeDtypeStruct((count, images, width), bf16)
     parts = exchange(part, "hidden")
-    mixed, direct = call(
+    mixed, direct, zloss = call(
         lambda *refs: mixed_kernel(images, *refs),
-        [out_shape, pltpu.VMEM((rows, width), f32)],
-        (dispatch, combine, slot_rows),
+        [held_shape, pltpu.VMEM((rows, width), f32), pltpu.VMEM((images, count), f32)],
+        (dispatch, combine, total, slot_rows),
         "mixed",
     )
-    (token_grad,) = call(
+    out_shape = jax.ShapeDtypeStruct(by_token.shape, bf16)
+    token_grad, mixed, zloss = call(
         lambda *refs: token_kernel(hidden, *refs),
-        [out_shape],
-        (*parts, combine, total, keys, direct),
+        [out_shape, out_shape, jax.ShapeDtypeStruct((images, count), f32)],
+        (*parts, combine, total, keys, direct, mixed, zloss),
         "token_grad",
+        far_outs=True,
+        scratch=[held_shape, pltpu.SemaphoreType.DMA((3,))],
     )
     return (jnp.transpose(mixed, (1, 0, 2)), jnp.transpose(token_grad, (1, 0, 2)), zloss)
 

time: 43.4 us -> 42.5 us (0.979)
  blocking collectives: 19.5 us -> 20.8 us
  starting transfers between devices: 10.1 us -> 9.18 us
  local copies, waits for them, and re-layouts: 0.8 us -> 0 us
    all_to_all x2, blocking collectives: 19.5 us -> 20.8 us  [to_all(): lax.all_to_all(value, ('expert', 'hidden'), split_axis=0, concat_axis=0,...]
    ppermute x6, starting transfers between devices: 10.1 us -> 9.18 us  [exchange(): lax.ppermute(value, axis, [(source, source ^ step) for source in range(si...]
    unnamed x1 -> x0, local copies, waits for them, and re-layouts: 0.66 us -> none
  transfers between devices with their start and end apart: 6 -> 6, of which waited for: 2 -> 4; matrix products, arithmetic and copies ran while one was open for 2% -> 0% of each run, Pallas kernels for 8% -> 8%
where the time goes in v3:
time: 42.5 us; the launch traced here: 42.3 us
  blocking collectives  20.8 us (49%)
  starting transfers between devices  9.18 us (22%)
  Pallas kernels  8.23 us (19%)
  waiting for transfers between devices  3.48 us (8%)
  between operations  0.68 us (2%)
    all_to_all x2, blocking collectives, to_all(): lax.all_to_all(value, ('expert', 'hidden'), split_axis=0, concat_axis=0,...  20.8 us
    ppermute x6, starting transfers between devices, exchange(): lax.ppermute(value, axis, [(source, source ^ step) for source in range(si...  9.18 us
    pallas_call x7, Pallas kernels, call(): pl.pallas_call(kernel, out_shape=outs, in_specs=[VMEM] * len(args) + [HBM...  8.23 us
    ppermute x6, waiting for transfers between devices, exchange(): lax.ppermute(value, axis, [(source, source ^ step) for source in range(si...  3.48 us
  transfers between devices with their start and end apart: 6, of which 4 were waited for; matrix products, arithmetic and copies ran while one was open for 0% of the time, Pallas kernels for 8%

profile of v3, /device:TPU:0, one launch (start us, length us, event | category | flops | bytes accessed | tf_op | source)
XLA Modules:
  0.0 42.3 jit_solution(2664950248474131436)
XLA Ops:
  0.6 1.2 %logits.1 = (f32[8,392]{1,0:T(8,128)S(1)}, bf16[392,256]{1,0:T(8,128)(2,1)S(1)}, bf16[8,256]{1,0:T(8,128)(2,1)S(1)}) custom-call(bf16[196,2,256]{2,1,0:T(2,128)(2,1)} %bitcast.18, bf16[8,256]{1,0:T(8,128)(2,1)} %bitcast.19), custom_call_target="tpu_custom_call" | custom-call | tf_op jit(solution)/shard_map/logits/pallas_call | solution.py:197
  1.8 4.1 %collective-permute-start.2 = (f32[8,392]{1,0:T(8,128)S(1)}, f32[8,392]{1,0:T(8,128)S(1)}, u32[]{:S(2)}, u32[]{:S(2)}) collective-permute-start(f32[8,392]{1,0:T(8,128)S(1)} %get-tuple-element.23.refs_0_), channel_id=1, source_target_pairs={{0,2},{1,3},{2,0},{3,1},{4,6},{5,7},{6,4},{7,5},{8,10},{9,11},{10,... | collective-permute-start | bytes 37640 | tf_op jit(solution)/shard_map/ppermute | solution.py:212
  5.9 1.3 %collective-permute-start.1 = (f32[8,392]{1,0:T(8,128)S(1)}, f32[8,392]{1,0:T(8,128)S(1)}, u32[]{:S(2)}, u32[]{:S(2)}) collective-permute-start(f32[8,392]{1,0:T(8,128)S(1)} %get-tuple-element.23.refs_0_), channel_id=1, source_target_pairs={{0,3},{1,2},{2,1},{3,0},{4,7},{5,6},{6,5},{7,4},{8,11},{9,10},{10,... | collective-permute-start | bytes 37640 | tf_op jit(solution)/shard_map/ppermute | solution.py:212
  7.3 0.2 collective-permute-start
  7.5 2.4 %prepare.1 = (bf16[392,256]{1,0:T(8,128)(2,1)S(1)}, f32[1,1024]{1,0:T(1,128)S(1)}, bf16[1,1024]{1,0:T(2,128)(2,1)S(1)}, bf16[1024,1024]{1,0:T(8,128)(2,1)S(1)}, bf16[1024,1024]{1,0:T(8,128)(2,1)S(1)}) custom-call(f32[8,392]{1,0:T(8,128)S(1)} %get-tuple-element.23.refs_0_, bf16[196,2,256]{2,1,0:T(2,128)(2,1)} %bitcast.17, bf16[1,256]{1,0:T(2,128)(2,1)} %refs_2_.1, ...), custom_call_target="tpu_custom_call" | custom-call | tf_op jit(solution)/shard_map/prepare/pallas_call | solution.py:197
  9.9 0.0 collective-permute-done.2.refs_3_
  9.9 1.5 %collective-permute-done.1.refs_2_ = f32[8,392]{1,0:T(8,128)S(1)} collective-permute-done((f32[8,392]{1,0:T(8,128)S(1)}, f32[8,392]{1,0:T(8,128)S(1)}, u32[]{:S(2)}, u32[]{:S(2)}) %collective-permute-start.1) | collective-permute-done | bytes 12576 | tf_op jit(solution)/shard_map/ppermute | solution.py:212
  11.4 0.0 collective-permute-done.refs_1_
  11.4 0.5 %dispatch.1 = (bf16[8,4,4,256]{3,2,1,0:T(4,128)(2,1)S(1)}, f32[8,392]{1,0:T(8,128)S(1)}, f32[8,392]{1,0:T(8,128)S(1)}, f32[1,392]{1,0:T(1,128)S(1)}) custom-call(f32[8,392]{1,0:T(8,128)S(1)} %get-tuple-element.23.refs_0_, f32[8,392]{1,0:T(8,128)S(1)} %collective-permute-done.refs_1_, f32[8,392]{1,0:T(8,128)S(1)} %collective-permute-done.1.refs_2_, ...), custom_call_target="tpu_custom_call" | custom-call | tf_op jit(solution)/shard_map/dispatch/pallas_call | solution.py:197
  11.9 11.6 %all_to_all.10 = bf16[32,4,256]{2,1,0:T(4,128)(2,1)S(1)} all-to-all(bf16[32,4,256]{2,1,0:T(4,128)(2,1)S(1)} %bitcast.14), channel_id=1, replica_groups=mesh['expert'=8,'hidden'=4] {'expert','hidden'}, dimensions={0} | all-to-all | bytes 131072 | tf_op jit(solution)/shard_map/all_to_all | solution.py:256
  23.5 2.1 %expert.1 = bf16[8,4,4,256]{3,2,1,0:T(4,128)(2,1)S(1)} custom-call(bf16[8,4,4,256]{3,2,1,0:T(4,128)(2,1)S(1)} %bitcast.11, bf16[1024,1024]{1,0:T(8,128)(2,1)S(1)} %get-tuple-element.27.refs_1_, bf16[1,1024]{1,0:T(2,128)(2,1)S(1)} %get-tuple-element.28.refs_2_, bf16[1024,1024]{1,0:T(8,128)(2,1)S(1)} %get-tuple-element.29.refs_3_, ...), custom_call_target="tpu_custom_call" | custom-call | tf_op jit(solution)/shard_map/expert/pallas_call | solution.py:197
  25.6 9.2 %all_to_all.11 = bf16[32,4,256]{2,1,0:T(4,128)(2,1)S(1)} all-to-all(bf16[32,4,256]{2,1,0:T(4,128)(2,1)S(1)} %bitcast.12), channel_id=1, replica_groups=mesh['expert'=8,'hidden'=4] {'expert','hidden'}, dimensions={0} | all-to-all | bytes 131072 | tf_op jit(solution)/shard_map/all_to_all | solution.py:256
  34.8 0.3 gradient.1
  35.1 0.5 %collective-permute-start.5 = (bf16[8,392]{1,0:T(8,128)(2,1)S(1)}, bf16[8,392]{1,0:T(8,128)(2,1)S(1)}, u32[]{:S(2)}, u32[]{:S(2)}) collective-permute-start(bf16[8,392]{1,0:T(8,128)(2,1)S(1)} %get-tuple-element.33.refs_0_), channel_id=1, source_target_pairs={{0,2},{1,3},{2,0},{3,1},{4,6},{5,7},{6,4},{7,5},{8,10},{9,11},{10,... | collective-permute-start | bytes 18824 | tf_op jit(solution)/shard_map/ppermute | solution.py:212
  35.6 2.1 %collective-permute-start.4 = (bf16[8,392]{1,0:T(8,128)(2,1)S(1)}, bf16[8,392]{1,0:T(8,128)(2,1)S(1)}, u32[]{:S(2)}, u32[]{:S(2)}) collective-permute-start(bf16[8,392]{1,0:T(8,128)(2,1)S(1)} %get-tuple-element.33.refs_0_), channel_id=1, source_target_pairs={{0,3},{1,2},{2,1},{3,0},{4,7},{5,6},{6,5},{7,4},{8,11},{9,10},{10,... | collective-permute-start | bytes 18824 | tf_op jit(solution)/shard_map/ppermute | solution.py:212
  37.7 0.9 %collective-permute-start.3 = (bf16[8,392]{1,0:T(8,128)(2,1)S(1)}, bf16[8,392]{1,0:T(8,128)(2,1)S(1)}, u32[]{:S(2)}, u32[]{:S(2)}) collective-permute-start(bf16[8,392]{1,0:T(8,128)(2,1)S(1)} %get-tuple-element.33.refs_0_), channel_id=1, source_target_pairs={{0,1},{1,0},{2,3},{3,2},{4,5},{5,4},{6,7},{7,6},{8,9},{9,8},{10,11... | collective-permute-start | bytes 18824 | tf_op jit(solution)/shard_map/ppermute | solution.py:212
  38.6 0.8 %mixed.1 = (bf16[196,2,256]{2,1,0:T(2,128)(2,1)S(1)}, f32[392,256]{1,0:T(8,128)S(1)}, f32[2,196]{1,0:T(2,128)S(1)}) custom-call(f32[8,392]{1,0:T(8,128)S(1)} %get-tuple-element.31.refs_3_.refs_0_, f32[8,392]{1,0:T(8,128)S(1)} %get-tuple-element.32.refs_4_.refs_1_, f32[1,392]{1,0:T(1,128)S(1)} %get-tuple-element.34.refs_2_.refs_5_, ...), custom_call_target="tpu_custom_call" | custom-call | tf_op jit(solution)/shard_map/mixed/pallas_call | solution.py:197
  39.4 0.3 collective-permute-done.5.refs_3_
  39.7 1.3 %collective-permute-done.4.refs_2_ = bf16[8,392]{1,0:T(8,128)(2,1)S(1)} collective-permute-done((bf16[8,392]{1,0:T(8,128)(2,1)S(1)}, bf16[8,392]{1,0:T(8,128)(2,1)S(1)}, u32[]{:S(2)}, u32[]{:S(2)}) %collective-permute-start.4) | collective-permute-done | bytes 6304 | tf_op jit(solution)/shard_map/ppermute | solution.py:212
  41.0 0.3 collective-permute-done.3.refs_1_
  41.4 1.0 %token_grad.1 = (bf16[196,2,256]{2,1,0:T(2,128)(2,1)}, bf16[196,2,256]{2,1,0:T(2,128)(2,1)}, f32[2,196]{1,0:T(2,128)}) custom-call(bf16[8,392]{1,0:T(8,128)(2,1)S(1)} %get-tuple-element.33.refs_0_, bf16[8,392]{1,0:T(8,128)(2,1)S(1)} %collective-permute-done.3.refs_1_, bf16[8,392]{1,0:T(8,128)(2,1)S(1)} %collective-permute-done.4.refs_2_, ...), custom_call_target="tpu_custom_call" | custom-call | tf_op jit(solution)/shard_map/token_grad/pallas_call | solution.py:197
Async XLA Ops:
  1.8 8.1 %collective-permute-start.2 = (f32[8,392]{1,0:T(8,128)S(1)}, f32[8,392]{1,0:T(8,128)S(1)}, u32[]{:S(2)}, u32[]{:S(2)}) collective-permute-start(f32[8,392]{1,0:T(8,128)S(1)} %get-tuple-element.23.refs_0_), channel_id=1, source_target_pairs={{0,2},{1,3},{2,0},{3,1},{4,6},{5,7},{6,4},{7,5},{8,10},{9,11},{10,... | collective-permute-start | bytes 37640 | tf_op jit(solution)/shard_map/ppermute | solution.py:212
  5.9 5.5 %collective-permute-start.1 = (f32[8,392]{1,0:T(8,128)S(1)}, f32[8,392]{1,0:T(8,128)S(1)}, u32[]{:S(2)}, u32[]{:S(2)}) collective-permute-start(f32[8,392]{1,0:T(8,128)S(1)} %get-tuple-element.23.refs_0_), channel_id=1, source_target_pairs={{0,3},{1,2},{2,1},{3,0},{4,7},{5,6},{6,5},{7,4},{8,11},{9,10},{10,... | collective-permute-start | bytes 37640 | tf_op jit(solution)/shard_map/ppermute | solution.py:212
  7.3 4.2 %collective-permute-start = (f32[8,392]{1,0:T(8,128)S(1)}, f32[8,392]{1,0:T(8,128)S(1)}, u32[]{:S(2)}, u32[]{:S(2)}) collective-permute-start(f32[8,392]{1,0:T(8,128)S(1)} %get-tuple-element.23.refs_0_), channel_id=1, source_target_pairs={{0,1},{1,0},{2,3},{3,2},{4,5},{5,4},{6,7},{7,6},{8,9},{9,8},{10,11... | collective-permute-start | bytes 37640 | tf_op jit(solution)/shard_map/ppermute | solution.py:212
  35.1 4.6 %collective-permute-start.5 = (bf16[8,392]{1,0:T(8,128)(2,1)S(1)}, bf16[8,392]{1,0:T(8,128)(2,1)S(1)}, u32[]{:S(2)}, u32[]{:S(2)}) collective-permute-start(bf16[8,392]{1,0:T(8,128)(2,1)S(1)} %get-tuple-element.33.refs_0_), channel_id=1, source_target_pairs={{0,2},{1,3},{2,0},{3,1},{4,6},{5,7},{6,4},{7,5},{8,10},{9,11},{10,... | collective-permute-start | bytes 18824 | tf_op jit(solution)/shard_map/ppermute | solution.py:212
  35.6 5.4 %collective-permute-start.4 = (bf16[8,392]{1,0:T(8,128)(2,1)S(1)}, bf16[8,392]{1,0:T(8,128)(2,1)S(1)}, u32[]{:S(2)}, u32[]{:S(2)}) collective-permute-start(bf16[8,392]{1,0:T(8,128)(2,1)S(1)} %get-tuple-element.33.refs_0_), channel_id=1, source_target_pairs={{0,3},{1,2},{2,1},{3,0},{4,7},{5,6},{6,5},{7,4},{8,11},{9,10},{10,... | collective-permute-start | bytes 18824 | tf_op jit(solution)/shard_map/ppermute | solution.py:212
  37.7 3.7 %collective-permute-start.3 = (bf16[8,392]{1,0:T(8,128)(2,1)S(1)}, bf16[8,392]{1,0:T(8,128)(2,1)S(1)}, u32[]{:S(2)}, u32[]{:S(2)}) collective-permute-start(bf16[8,392]{1,0:T(8,128)(2,1)S(1)} %get-tuple-element.33.refs_0_), channel_id=1, source_target_pairs={{0,1},{1,0},{2,3},{3,2},{4,5},{5,4},{6,7},{7,6},{8,9},{9,8},{10,11... | collective-permute-start | bytes 18824 | tf_op jit(solution)/shard_map/ppermute | solution.py:212

commit v4 on v3

--- a/solution.py
+++ b/solution.py
@@ -36,18 +36,23 @@
     return lax.broadcasted_iota(jnp.int32, shape, dim)
 
 
-def slot_masks(rows, tokens, images):
-    place = modulo(iota((rows, tokens), 0), 2 * images)
-    image = modulo(iota((rows, tokens), 1), images)
-    return place == image, place == image + images
+def same_image(rows, tokens, images):
+    return modulo(iota((rows, tokens), 0), images) == modulo(iota((rows, tokens), 1), images)
 
 
 def spread(values, images):
-    slots = values.shape[0]
-    first = 2 * images * iota((2 * images * slots, slots), 1)
-    row = iota((2 * images * slots, slots), 0)
-    pick = jnp.where((row >= first) & (row < first + 2 * images), 1.0, 0.0).astype(bf16)
-    return dot(pick, values, 1, 0)
+    slots, tokens = values.shape
+    first = images * iota((images * slots, slots), 1)
+    row = iota((images * slots, slots), 0)
+    pick = jnp.where((row >= first) & (row < first + images), 1.0, 0.0).astype(bf16)
+    wide = dot(pick, values.astype(bf16), 1, 0)
+    return jnp.where(same_image(images * slots, tokens, images), wide, 0.0).astype(bf16)
+
+
+def gather(values, images):
+    rows, tokens = values.shape
+    values = jnp.where(same_image(rows, tokens, images), values, 0.0)
+    return jnp.sum(values.reshape(rows // images, images, tokens), axis=1)
 
 
 def by_image(values, images, reduce, fill):
@@ -93,12 +98,12 @@
         copy.wait()
 
 
-def steps(size):
-    return [1] + list(range(size - 1, 1, -1))
-
-
-def tree_sum(refs):
-    order = [0] + steps(len(refs))
+def steps(size, first):
+    return [1] + list(range(size - 1, 1, -1)) if first else list(range(1, size))
+
+
+def tree_sum(refs, first):
+    order = [0] + steps(len(refs), first)
     values = [refs[order.index(step)][...].astype(f32) for step in range(len(refs))]
     while len(values) > 1:
         values = [values[k] + values[k + 1] for k in range(0, len(values), 2)]
@@ -107,7 +112,7 @@
 
 def dispatch_kernel(images, count, *refs):
     parts, (rows_ref, grads_ref, sent_ref, dispatch_ref, combine_ref, total_ref) = refs[:count], refs[count:]
-    logits = tree_sum(parts)
+    logits = tree_sum(parts, True)
     top = jnp.max(logits, axis=0, keepdims=True)
     powers = jnp.exp(logits - top)
     sums = jnp.sum(powers, axis=0, keepdims=True)
@@ -117,57 +122,52 @@
     dispatch = powers / by_image(powers, images, jnp.sum, 0.0)
     combine_ref[...] = combine
     dispatch_ref[...] = dispatch
-    slots, hidden, places, width = sent_ref.shape
-    forward, backward = slot_masks(slots * places, logits.shape[1], images)
-    left = jnp.where(forward, spread(dispatch.astype(bf16), images), 0.0).astype(bf16)
-    right = jnp.where(backward, spread(combine.astype(bf16), images), 0.0).astype(bf16)
-    sent = dot(left, rows_ref[...], 1, 0) + dot(right, grads_ref[...], 1, 0)
-    sent = sent.astype(bf16).reshape(slots, places, width)
-    for index in range(hidden):
-        sent_ref[:, index] = sent
-
-
-def expert_kernel(images, came_ref, win_ref, bin_ref, wout_ref, bout_ref, sent_ref):
-    groups, hidden, places, width = came_ref.shape
-    rows = groups * places
-    came = jnp.concatenate([came_ref[:, index].reshape(rows, width) for index in range(hidden)], axis=1)
-    pre = dot(came, win_ref[...], 1, 0) + bin_ref[...].astype(f32)
-    hidden_grad = dot(came, wout_ref[...], 1, 1)
-    activated, slope = gelu_parts(pre)
+    send(sent_ref, [dot(spread(dispatch, images), rows_ref[...], 1, 0)], [dot(spread(combine, images), grads_ref[...], 1, 0)])
+
+
+def send(sent_ref, forward, backward):
+    groups, hidden, images, width = sent_ref.shape
+    width //= 2
+    for half, parts in enumerate((forward, backward)):
+        parts = [part.astype(bf16).reshape(groups, images, width) for part in parts]
+        for index in range(hidden):
+            sent_ref[:, index, :, half * width : (half + 1) * width] = parts[index % len(parts)]
+
+
+def expert_kernel(came_ref, win_ref, bin_ref, wout_ref, bout_ref, sent_ref):
+    groups, hidden, images, width = came_ref.shape
+    came = [came_ref[:, index].reshape(groups * images, width) for index in range(hidden)]
+    width //= 2
+    forward = jnp.concatenate([part[:, :width] for part in came], axis=1)
+    backward = jnp.concatenate([part[:, width:] for part in came], axis=1)
+    activated, slope = gelu_parts(dot(forward, win_ref[...], 1, 0) + bin_ref[...].astype(f32))
+    hidden_grad = dot(backward, wout_ref[...], 1, 1)
     out = dot(activated.astype(bf16), wout_ref[...], 1, 0) + bout_ref[...]
-    pre_grad = (hidden_grad * pltpu.roll(slope, images, 0)).astype(bf16)
-    back = dot(pre_grad, win_ref[...], 1, 1)
-    forward = modulo(iota(out.shape, 0), places) < images
-    sent = jnp.where(forward, out, back).astype(bf16)
-    for index in range(hidden):
-        sent_ref[:, index] = sent[:, index * width : (index + 1) * width].reshape(groups, places, width)
-
-
-def gradient_kernel(images, came_ref, rows_ref, grads_ref, dispatch_ref, combine_ref, slots_ref, part_ref):
-    slots, hidden, places, width = came_ref.shape
+    back = dot((hidden_grad * slope).astype(bf16), win_ref[...], 1, 1)
+    parts = [slice(index * width, (index + 1) * width) for index in range(hidden)]
+    send(sent_ref, [out[:, part] for part in parts], [back[:, part] for part in parts])
+
+
+def gradient_kernel(came_ref, rows_ref, grads_ref, dispatch_ref, combine_ref, out_ref, back_ref, part_ref):
+    slots, hidden, images, width = came_ref.shape
     came = came_ref[:, 0].astype(f32)
     for index in range(1, hidden):
         came = came + came_ref[:, index].astype(f32)
-    came = came.reshape(slots * places, width).astype(bf16)
-    slots_ref[...] = came
-    tokens = rows_ref.shape[0]
-    forward, backward = slot_masks(slots * places, tokens, images)
-    combine_grad = jnp.where(forward, dot(came, grads_ref[...], 1, 1), 0.0)
-    dispatch_grad = jnp.where(backward, dot(came, rows_ref[...], 1, 1), 0.0)
-    combine_grad = jnp.sum(combine_grad.reshape(slots, places, tokens), axis=1)
-    dispatch_grad = jnp.sum(dispatch_grad.reshape(slots, places, tokens), axis=1)
+    came = came.astype(bf16).reshape(slots * images, width)
+    out, back = came[:, : width // 2], came[:, width // 2 :]
+    out_ref[...], back_ref[...] = out, back
+    combine_grad = gather(dot(out, grads_ref[...], 1, 1), images)
+    dispatch_grad = gather(dot(back, rows_ref[...], 1, 1), images)
     combine, dispatch = combine_ref[...], dispatch_ref[...]
     part = combine * (combine_grad - jnp.sum(combine * combine_grad, axis=0, keepdims=True))
     part = part + dispatch * (dispatch_grad - by_image(dispatch * dispatch_grad, images, jnp.sum, 0.0))
     part_ref[...] = part.astype(bf16)
 
 
-def mixed_kernel(images, dispatch_ref, combine_ref, total_ref, slots_ref, mixed_ref, direct_ref, loss_ref):
-    forward, backward = slot_masks(slots_ref.shape[0], combine_ref.shape[1], images)
-    left = jnp.where(forward, spread(combine_ref[...].astype(bf16), images), 0.0).astype(bf16)
-    mixed_ref[...] = dot(left, slots_ref[...], 0, 0).astype(bf16).reshape(mixed_ref.shape)
-    left = jnp.where(backward, spread(dispatch_ref[...].astype(bf16), images), 0.0).astype(bf16)
-    direct_ref[...] = dot(left, slots_ref[...], 0, 0)
+def mixed_kernel(dispatch_ref, combine_ref, total_ref, out_ref, back_ref, mixed_ref, direct_ref, loss_ref):
+    images = loss_ref.shape[0]
+    mixed_ref[...] = dot(spread(combine_ref[...], images), out_ref[...], 0, 0).astype(bf16).reshape(mixed_ref.shape)
+    direct_ref[...] = dot(spread(dispatch_ref[...], images), back_ref[...], 0, 0)
     total = jnp.broadcast_to(total_ref[...], (8, total_ref.shape[1]))
     tokens = loss_ref.shape[1]
     row, token = iota((images * tokens, tokens), 0), iota((images * tokens, tokens), 1)
@@ -184,7 +184,7 @@
     (combine_ref, total_ref, keys_ref, direct_ref, mixed_ref, loss_ref) = refs[:6]
     (out_ref, mixed_out_ref, loss_out_ref, held_ref, sems) = refs[6:]
     copies = load((mixed_ref, loss_ref), (mixed_out_ref, loss_out_ref), sems)
-    logit_grad = tree_sum(parts) + 2.0 * loss_weight * total_ref[...] * combine_ref[...]
+    logit_grad = tree_sum(parts, False) + 2.0 * loss_weight * total_ref[...] * combine_ref[...]
     out = dot(logit_grad.astype(bf16), keys_ref[...], 0, 0) + direct_ref[...]
     held_ref[...] = out.astype(bf16).reshape(held_ref.shape)
     last = pltpu.make_async_copy(held_ref, out_ref, sems.at[2])
@@ -206,10 +206,10 @@
     )(*args, *(pltpu.with_memory_space_constraint(value, pltpu.HBM) for value in far))
 
 
-def exchange(value, axis):
+def exchange(value, axis, first):
     size = lax.axis_size(axis)
     return [value] + [
-        lax.ppermute(value, axis, [(source, source ^ step) for source in range(size)]) for step in steps(size)
+        lax.ppermute(value, axis, [(source, source ^ step) for source in range(size)]) for step in steps(size, first)
     ]
 
 
@@ -225,7 +225,7 @@
     table = pltpu.VMEM((slots, rows), f32)
     row_shape = pltpu.VMEM((rows, width), bf16)
     held_shape = pltpu.VMEM(by_token.shape, bf16)
-    sent_shape = pltpu.VMEM((groups, hidden, 2 * images, width), bf16)
+    sent_shape = pltpu.VMEM((groups, hidden, images, 2 * width), bf16)
 
     part, token_rows, keys = call(
         logits_kernel,
@@ -243,7 +243,7 @@
         far=(grad_by_token, bias_out, bias_in, weight_in, weight_out),
         scratch=[held_shape, pltpu.VMEM(bias_out.shape, bf16), pltpu.SemaphoreType.DMA((5,))],
     )
-    parts = exchange(part, "hidden")
+    parts = exchange(part, "hidden", True)
     sent, dispatch, combine, total = call(
         lambda *refs: dispatch_kernel(images, hidden, *refs),
         [sent_shape, table, table, pltpu.VMEM((1, rows), f32)],
@@ -252,28 +252,28 @@
     )
 
     def to_all(value):
-        value = value.reshape(groups * hidden, 2 * images, width)
+        value = value.reshape(groups * hidden, images, 2 * width)
         value = lax.all_to_all(value, ("expert", "hidden"), split_axis=0, concat_axis=0, tiled=True)
-        return value.reshape(groups, hidden, 2 * images, width)
+        return value.reshape(groups, hidden, images, 2 * width)
 
     (sent,) = call(
-        lambda *refs: expert_kernel(images, *refs),
+        expert_kernel,
         [sent_shape],
         (to_all(sent), weight_in, bias_in, weight_out, bias_out),
         "expert",
         24,
     )
-    slot_rows, part = call(
-        lambda *refs: gradient_kernel(images, *refs),
-        [pltpu.VMEM((2 * images * slots, width), bf16), pltpu.VMEM((slots, rows), bf16)],
+    slot_out, in_grad, part = call(
+        gradient_kernel,
+        [*[pltpu.VMEM((slots * images, width), bf16)] * 2, pltpu.VMEM((slots, rows), bf16)],
         (to_all(sent), token_rows, grad_rows, dispatch, combine),
         "gradient",
     )
-    parts = exchange(part, "hidden")
+    parts = exchange(part, "hidden", False)
     mixed, direct, zloss = call(
-        lambda *refs: mixed_kernel(images, *refs),
+        mixed_kernel,
         [held_shape, pltpu.VMEM((rows, width), f32), pltpu.VMEM((images, count), f32)],
-        (dispatch, combine, total, slot_rows),
+        (dispatch, combine, total, slot_out, in_grad),
         "mixed",
     )
     out_shape = jax.ShapeDtypeStruct(by_token.shape, bf16)

time: 42.5 us -> 41.9 us (0.986)
  waiting for transfers between devices: 3.48 us -> 2.38 us
  starting transfers between devices: 9.18 us -> 10.1 us
    ppermute x6, waiting for transfers between devices: 3.48 us -> 2.38 us  [exchange(): lax.ppermute(value, axis, [(source, source ^ step) for source in range(si...]
    ppermute x6, starting transfers between devices: 9.18 us -> 10.1 us  [exchange(): lax.ppermute(value, axis, [(source, source ^ step) for source in range(si...]
  transfers between devices with their start and end apart: 6 -> 6, of which waited for: 4 -> 3; matrix products, arithmetic and copies ran while one was open for 0% -> 0% of each run, Pallas kernels for 8% -> 8%
where the time goes in v4:
time: 41.9 us; the launch traced here: 41.7 us
  blocking collectives  20.8 us (50%)
  starting transfers between devices  10.1 us (24%)
  Pallas kernels  7.85 us (19%)
  waiting for transfers between devices  2.38 us (6%)
  between operations  0.67 us (2%)
    all_to_all x2, blocking collectives, to_all(): lax.all_to_all(value, ('expert', 'hidden'), split_axis=0, concat_axis=0,...  20.8 us
    ppermute x6, starting transfers between devices, exchange(): lax.ppermute(value, axis, [(source, source ^ step) for source in range(si...  10.1 us
    pallas_call x7, Pallas kernels, call(): pl.pallas_call(kernel, out_shape=outs, in_specs=[VMEM] * len(args) + [HBM...  7.85 us
    ppermute x6, waiting for transfers between devices, exchange(): lax.ppermute(value, axis, [(source, source ^ step) for source in range(si...  2.38 us
  transfers between devices with their start and end apart: 6, of which 3 were waited for; matrix products, arithmetic and copies ran while one was open for 0% of the time, Pallas kernels for 8%

profile of v4, /device:TPU:0, one launch (start us, length us, event | category | flops | bytes accessed | tf_op | source)
XLA Modules:
  0.0 41.7 jit_solution(17531498224883753857)
XLA Ops:
  0.6 1.2 %logits.1 = (f32[8,392]{1,0:T(8,128)S(1)}, bf16[392,256]{1,0:T(8,128)(2,1)S(1)}, bf16[8,256]{1,0:T(8,128)(2,1)S(1)}) custom-call(bf16[196,2,256]{2,1,0:T(2,128)(2,1)} %bitcast.18, bf16[8,256]{1,0:T(8,128)(2,1)} %bitcast.19), custom_call_target="tpu_custom_call" | custom-call | tf_op jit(solution)/shard_map/logits/pallas_call | solution.py:197
  1.8 4.1 %collective-permute-start.2 = (f32[8,392]{1,0:T(8,128)S(1)}, f32[8,392]{1,0:T(8,128)S(1)}, u32[]{:S(2)}, u32[]{:S(2)}) collective-permute-start(f32[8,392]{1,0:T(8,128)S(1)} %get-tuple-element.24.refs_0_), channel_id=1, source_target_pairs={{0,2},{1,3},{2,0},{3,1},{4,6},{5,7},{6,4},{7,5},{8,10},{9,11},{10,... | collective-permute-start | bytes 37640 | tf_op jit(solution)/shard_map/ppermute | solution.py:212
  5.9 1.3 %collective-permute-start.1 = (f32[8,392]{1,0:T(8,128)S(1)}, f32[8,392]{1,0:T(8,128)S(1)}, u32[]{:S(2)}, u32[]{:S(2)}) collective-permute-start(f32[8,392]{1,0:T(8,128)S(1)} %get-tuple-element.24.refs_0_), channel_id=1, source_target_pairs={{0,3},{1,2},{2,1},{3,0},{4,7},{5,6},{6,5},{7,4},{8,11},{9,10},{10,... | collective-permute-start | bytes 37640 | tf_op jit(solution)/shard_map/ppermute | solution.py:212
  7.3 0.2 collective-permute-start
  7.5 2.4 %prepare.1 = (bf16[392,256]{1,0:T(8,128)(2,1)S(1)}, f32[1,1024]{1,0:T(1,128)S(1)}, bf16[1,1024]{1,0:T(2,128)(2,1)S(1)}, bf16[1024,1024]{1,0:T(8,128)(2,1)S(1)}, bf16[1024,1024]{1,0:T(8,128)(2,1)S(1)}) custom-call(f32[8,392]{1,0:T(8,128)S(1)} %get-tuple-element.24.refs_0_, bf16[196,2,256]{2,1,0:T(2,128)(2,1)} %bitcast.17, bf16[1,256]{1,0:T(2,128)(2,1)} %refs_2_.1, ...), custom_call_target="tpu_custom_call" | custom-call | tf_op jit(solution)/shard_map/prepare/pallas_call | solution.py:197
  9.9 0.0 collective-permute-done.2.refs_3_
  9.9 1.5 %collective-permute-done.1.refs_2_ = f32[8,392]{1,0:T(8,128)S(1)} collective-permute-done((f32[8,392]{1,0:T(8,128)S(1)}, f32[8,392]{1,0:T(8,128)S(1)}, u32[]{:S(2)}, u32[]{:S(2)}) %collective-permute-start.1) | collective-permute-done | bytes 12576 | tf_op jit(solution)/shard_map/ppermute | solution.py:212
  11.4 0.0 collective-permute-done.refs_1_
  11.4 0.4 %dispatch.1 = (bf16[8,4,2,512]{3,2,1,0:T(2,128)(2,1)S(1)}, f32[8,392]{1,0:T(8,128)S(1)}, f32[8,392]{1,0:T(8,128)S(1)}, f32[1,392]{1,0:T(1,128)S(1)}) custom-call(f32[8,392]{1,0:T(8,128)S(1)} %get-tuple-element.24.refs_0_, f32[8,392]{1,0:T(8,128)S(1)} %collective-permute-done.refs_1_, f32[8,392]{1,0:T(8,128)S(1)} %collective-permute-done.1.refs_2_, ...), custom_call_target="tpu_custom_call" | custom-call | tf_op jit(solution)/shard_map/dispatch/pallas_call | solution.py:197
  11.9 11.6 %all_to_all.10 = bf16[32,2,512]{2,1,0:T(2,128)(2,1)S(1)} all-to-all(bf16[32,2,512]{2,1,0:T(2,128)(2,1)S(1)} %bitcast.14), channel_id=1, replica_groups=mesh['expert'=8,'hidden'=4] {'expert','hidden'}, dimensions={0} | all-to-all | bytes 131072 | tf_op jit(solution)/shard_map/all_to_all | solution.py:256
  23.5 1.7 %expert.1 = bf16[8,4,2,512]{3,2,1,0:T(2,128)(2,1)S(1)} custom-call(bf16[8,4,2,512]{3,2,1,0:T(2,128)(2,1)S(1)} %bitcast.11, bf16[1024,1024]{1,0:T(8,128)(2,1)S(1)} %get-tuple-element.28.win_ref, bf16[1,1024]{1,0:T(2,128)(2,1)S(1)} %get-tuple-element.29.bin_ref, bf16[1024,1024]{1,0:T(8,128)(2,1)S(1)} %get-tuple-element.30.wout_ref, ...), custom_call_target="tpu_custom_call" | custom-call | tf_op jit(solution)/shard_map/expert/pallas_call | solution.py:197
  25.2 9.2 %all_to_all.11 = bf16[32,2,512]{2,1,0:T(2,128)(2,1)S(1)} all-to-all(bf16[32,2,512]{2,1,0:T(2,128)(2,1)S(1)} %bitcast.12), channel_id=1, replica_groups=mesh['expert'=8,'hidden'=4] {'expert','hidden'}, dimensions={0} | all-to-all | bytes 131072 | tf_op jit(solution)/shard_map/all_to_all | solution.py:256
  34.4 0.3 gradient.1
  34.8 0.7 %collective-permute-start.5 = (bf16[8,392]{1,0:T(8,128)(2,1)S(1)}, bf16[8,392]{1,0:T(8,128)(2,1)S(1)}, u32[]{:S(2)}, u32[]{:S(2)}) collective-permute-start(bf16[8,392]{1,0:T(8,128)(2,1)S(1)} %get-tuple-element.34.refs_0_), channel_id=1, source_target_pairs={{0,3},{1,2},{2,1},{3,0},{4,7},{5,6},{6,5},{7,4},{8,11},{9,10},{10,... | collective-permute-start | bytes 18824 | tf_op jit(solution)/shard_map/ppermute | solution.py:212
  35.5 1.0 %collective-permute-start.4 = (bf16[8,392]{1,0:T(8,128)(2,1)S(1)}, bf16[8,392]{1,0:T(8,128)(2,1)S(1)}, u32[]{:S(2)}, u32[]{:S(2)}) collective-permute-start(bf16[8,392]{1,0:T(8,128)(2,1)S(1)} %get-tuple-element.34.refs_0_), channel_id=1, source_target_pairs={{0,2},{1,3},{2,0},{3,1},{4,6},{5,7},{6,4},{7,5},{8,10},{9,11},{10,... | collective-permute-start | bytes 18824 | tf_op jit(solution)/shard_map/ppermute | solution.py:212
  36.5 2.7 %collective-permute-start.3 = (bf16[8,392]{1,0:T(8,128)(2,1)S(1)}, bf16[8,392]{1,0:T(8,128)(2,1)S(1)}, u32[]{:S(2)}, u32[]{:S(2)}) collective-permute-start(bf16[8,392]{1,0:T(8,128)(2,1)S(1)} %get-tuple-element.34.refs_0_), channel_id=1, source_target_pairs={{0,1},{1,0},{2,3},{3,2},{4,5},{5,4},{6,7},{7,6},{8,9},{9,8},{10,11... | collective-permute-start | bytes 18824 | tf_op jit(solution)/shard_map/ppermute | solution.py:212
  39.1 0.8 %mixed.1 = (bf16[196,2,256]{2,1,0:T(2,128)(2,1)S(1)}, f32[392,256]{1,0:T(8,128)S(1)}, f32[2,196]{1,0:T(2,128)S(1)}) custom-call(f32[8,392]{1,0:T(8,128)S(1)} %get-tuple-element.32.dispatch_ref, f32[8,392]{1,0:T(8,128)S(1)} %get-tuple-element.33.combine_ref.refs_4_, f32[1,392]{1,0:T(1,128)S(1)} %get-tuple-element.35.total_ref.refs_5_, ...), custom_call_target="tpu_custom_call" | custom-call | tf_op jit(solution)/shard_map/mixed/pallas_call | solution.py:197
  39.9 0.3 collective-permute-done.5.refs_3_
  40.2 0.0 collective-permute-done.4.refs_2_
  40.2 0.6 %collective-permute-done.3.refs_1_ = bf16[8,392]{1,0:T(8,128)(2,1)S(1)} collective-permute-done((bf16[8,392]{1,0:T(8,128)(2,1)S(1)}, bf16[8,392]{1,0:T(8,128)(2,1)S(1)}, u32[]{:S(2)}, u32[]{:S(2)}) %collective-permute-start.3) | collective-permute-done | bytes 6304 | tf_op jit(solution)/shard_map/ppermute | solution.py:212
  40.8 1.0 %token_grad.1 = (bf16[196,2,256]{2,1,0:T(2,128)(2,1)}, bf16[196,2,256]{2,1,0:T(2,128)(2,1)}, f32[2,196]{1,0:T(2,128)}) custom-call(bf16[8,392]{1,0:T(8,128)(2,1)S(1)} %get-tuple-element.34.refs_0_, bf16[8,392]{1,0:T(8,128)(2,1)S(1)} %collective-permute-done.3.refs_1_, bf16[8,392]{1,0:T(8,128)(2,1)S(1)} %collective-permute-done.4.refs_2_, ...), custom_call_target="tpu_custom_call" | custom-call | tf_op jit(solution)/shard_map/token_grad/pallas_call | solution.py:197
Async XLA Ops:
  1.8 8.1 %collective-permute-start.2 = (f32[8,392]{1,0:T(8,128)S(1)}, f32[8,392]{1,0:T(8,128)S(1)}, u32[]{:S(2)}, u32[]{:S(2)}) collective-permute-start(f32[8,392]{1,0:T(8,128)S(1)} %get-tuple-element.24.refs_0_), channel_id=1, source_target_pairs={{0,2},{1,3},{2,0},{3,1},{4,6},{5,7},{6,4},{7,5},{8,10},{9,11},{10,... | collective-permute-start | bytes 37640 | tf_op jit(solution)/shard_map/ppermute | solution.py:212
  5.9 5.5 %collective-permute-start.1 = (f32[8,392]{1,0:T(8,128)S(1)}, f32[8,392]{1,0:T(8,128)S(1)}, u32[]{:S(2)}, u32[]{:S(2)}) collective-permute-start(f32[8,392]{1,0:T(8,128)S(1)} %get-tuple-element.24.refs_0_), channel_id=1, source_target_pairs={{0,3},{1,2},{2,1},{3,0},{4,7},{5,6},{6,5},{7,4},{8,11},{9,10},{10,... | collective-permute-start | bytes 37640 | tf_op jit(solution)/shard_map/ppermute | solution.py:212
  7.3 4.2 %collective-permute-start = (f32[8,392]{1,0:T(8,128)S(1)}, f32[8,392]{1,0:T(8,128)S(1)}, u32[]{:S(2)}, u32[]{:S(2)}) collective-permute-start(f32[8,392]{1,0:T(8,128)S(1)} %get-tuple-element.24.refs_0_), channel_id=1, source_target_pairs={{0,1},{1,0},{2,3},{3,2},{4,5},{5,4},{6,7},{7,6},{8,9},{9,8},{10,11... | collective-permute-start | bytes 37640 | tf_op jit(solution)/shard_map/ppermute | solution.py:212
  34.8 5.5 %collective-permute-start.5 = (bf16[8,392]{1,0:T(8,128)(2,1)S(1)}, bf16[8,392]{1,0:T(8,128)(2,1)S(1)}, u32[]{:S(2)}, u32[]{:S(2)}) collective-permute-start(bf16[8,392]{1,0:T(8,128)(2,1)S(1)} %get-tuple-element.34.refs_0_), channel_id=1, source_target_pairs={{0,3},{1,2},{2,1},{3,0},{4,7},{5,6},{6,5},{7,4},{8,11},{9,10},{10,... | collective-permute-start | bytes 18824 | tf_op jit(solution)/shard_map/ppermute | solution.py:212
  35.5 4.7 %collective-permute-start.4 = (bf16[8,392]{1,0:T(8,128)(2,1)S(1)}, bf16[8,392]{1,0:T(8,128)(2,1)S(1)}, u32[]{:S(2)}, u32[]{:S(2)}) collective-permute-start(bf16[8,392]{1,0:T(8,128)(2,1)S(1)} %get-tuple-element.34.refs_0_), channel_id=1, source_target_pairs={{0,2},{1,3},{2,0},{3,1},{4,6},{5,7},{6,4},{7,5},{8,10},{9,11},{10,... | collective-permute-start | bytes 18824 | tf_op jit(solution)/shard_map/ppermute | solution.py:212
  36.5 4.3 %collective-permute-start.3 = (bf16[8,392]{1,0:T(8,128)(2,1)S(1)}, bf16[8,392]{1,0:T(8,128)(2,1)S(1)}, u32[]{:S(2)}, u32[]{:S(2)}) collective-permute-start(bf16[8,392]{1,0:T(8,128)(2,1)S(1)} %get-tuple-element.34.refs_0_), channel_id=1, source_target_pairs={{0,1},{1,0},{2,3},{3,2},{4,5},{5,4},{6,7},{7,6},{8,9},{9,8},{10,11... | collective-permute-start | bytes 18824 | tf_op jit(solution)/shard_map/ppermute | solution.py:212

commit v5 on v4

--- a/solution.py
+++ b/solution.py
@@ -10,6 +10,7 @@
 VMEM = pl.BlockSpec(memory_space=pltpu.VMEM)
 HBM = pl.BlockSpec(memory_space=pltpu.HBM)
 MIB = 1024 * 1024
+weight_pieces = 2
 
 
 def gelu_parts(value):
@@ -81,21 +82,32 @@
     part_ref[...] = dot(keys_ref[...], rows, 1, 1)
 
 
-def prepare_kernel(axis, after_ref, tokens_ref, bout_in_ref, bin_in_ref, win_in_ref, wout_in_ref,
-                   rows_ref, bout_ref, bin_ref, win_ref, wout_ref, held_ref, held_bout_ref, sems):
+def prepare_kernel(axis, after_ref, tokens_ref, bout_in_ref, bin_in_ref, wout_in_ref, win_in_ref,
+                   rows_ref, bout_ref, bin_ref, wout_ref, win_ref, wout_turned_ref, win_turned_ref,
+                   held_ref, held_bout_ref, sems):
     del after_ref
     tokens, images, width = tokens_ref.shape
-    sources = (tokens_ref, bout_in_ref, bin_in_ref, win_in_ref, wout_in_ref)
-    copies = load(sources, (held_ref, held_bout_ref, bin_ref, win_ref, wout_ref), sems)
-    for copy in copies[:2]:
+    pieces = []
+    for source, target, turned in (
+        (wout_in_ref, wout_ref, wout_turned_ref), (win_in_ref, win_ref, win_turned_ref)
+    ):
+        step = source.shape[0] // weight_pieces
+        pieces += [(source, target, turned, pl.ds(k * step, step)) for k in range(weight_pieces)]
+    copies = load(
+        (tokens_ref, bout_in_ref, bin_in_ref, *[source.at[part] for source, _, _, part in pieces]),
+        (held_ref, held_bout_ref, bin_ref, *[target.at[part] for _, target, _, part in pieces]),
+        sems,
+    )
+    for copy in copies[:3]:
         copy.wait()
     rows_ref[...] = held_ref[...].reshape(tokens * images, width)
     own = lax.axis_index(axis)
     for index in range(bout_ref.shape[1] // width):
         bias = jnp.where(own == index, held_bout_ref[...].astype(f32), 0.0)
         bout_ref[:, index * width : (index + 1) * width] = bias
-    for copy in copies[2:]:
+    for copy, (_, target, turned, part) in zip(copies[3:], pieces):
         copy.wait()
+        turned[:, part] = target[part].T
 
 
 def steps(size, first):
@@ -134,16 +146,16 @@
             sent_ref[:, index, :, half * width : (half + 1) * width] = parts[index % len(parts)]
 
 
-def expert_kernel(came_ref, win_ref, bin_ref, wout_ref, bout_ref, sent_ref):
+def expert_kernel(came_ref, bout_ref, bin_ref, wout_ref, win_ref, wout_turned_ref, win_turned_ref, sent_ref):
     groups, hidden, images, width = came_ref.shape
     came = [came_ref[:, index].reshape(groups * images, width) for index in range(hidden)]
     width //= 2
     forward = jnp.concatenate([part[:, :width] for part in came], axis=1)
     backward = jnp.concatenate([part[:, width:] for part in came], axis=1)
     activated, slope = gelu_parts(dot(forward, win_ref[...], 1, 0) + bin_ref[...].astype(f32))
-    hidden_grad = dot(backward, wout_ref[...], 1, 1)
+    hidden_grad = dot(backward, wout_turned_ref[...], 1, 0)
     out = dot(activated.astype(bf16), wout_ref[...], 1, 0) + bout_ref[...]
-    back = dot((hidden_grad * slope).astype(bf16), win_ref[...], 1, 1)
+    back = dot((hidden_grad * slope).astype(bf16), win_turned_ref[...], 1, 0)
     parts = [slice(index * width, (index + 1) * width) for index in range(hidden)]
     send(sent_ref, [out[:, part] for part in parts], [back[:, part] for part in parts])
 
@@ -235,13 +247,22 @@
         far=(by_token, jnp.transpose(slot_params)),
         scratch=[held_shape, pltpu.SemaphoreType.DMA((2,))],
     )
-    grad_rows, bias_out, bias_in, weight_in, weight_out = call(
+    grad_rows, *expert_values = call(
         lambda *refs: prepare_kernel("hidden", *refs),
-        [row_shape, pltpu.VMEM((1, wide), f32), *[pltpu.VMEM(v.shape, bf16) for v in (bias_in, weight_in, weight_out)]],
+        [
+            row_shape,
+            pltpu.VMEM((1, wide), f32),
+            *[pltpu.VMEM(value.shape, bf16) for value in (bias_in, weight_out, weight_in)],
+            *[pltpu.VMEM(value.shape[::-1], bf16) for value in (weight_out, weight_in)],
+        ],
         (part,),
         "prepare",
-        far=(grad_by_token, bias_out, bias_in, weight_in, weight_out),
-        scratch=[held_shape, pltpu.VMEM(bias_out.shape, bf16), pltpu.SemaphoreType.DMA((5,))],
+        far=(grad_by_token, bias_out, bias_in, weight_out, weight_in),
+        scratch=[
+            held_shape,
+            pltpu.VMEM(bias_out.shape, bf16),
+            pltpu.SemaphoreType.DMA((3 + 2 * weight_pieces,)),
+        ],
     )
     parts = exchange(part, "hidden", True)
     sent, dispatch, combine, total = call(
@@ -259,7 +280,7 @@
     (sent,) = call(
         expert_kernel,
         [sent_shape],
-        (to_all(sent), weight_in, bias_in, weight_out, bias_out),
+        (to_all(sent), *expert_values),
         "expert",
         24,
     )

time: 41.9 us -> 41.4 us (0.988)
  waiting for transfers between devices: 2.38 us -> 1.96 us
    ppermute x6, waiting for transfers between devices: 2.38 us -> 1.96 us  [exchange(): lax.ppermute(value, axis, [(source, source ^ step) for source in range(si...]
  transfers between devices with their start and end apart: 6 -> 6, of which waited for: 3 -> 3; matrix products, arithmetic and copies ran while one was open for 0% -> 0% of each run, Pallas kernels for 8% -> 9%
where the time goes in v5:
time: 41.4 us; the launch traced here: 41.2 us
  blocking collectives  20.8 us (50%)
  starting transfers between devices  10.1 us (24%)
  Pallas kernels  7.73 us (19%)
  waiting for transfers between devices  1.96 us (5%)
  between operations  0.67 us (2%)
    all_to_all x2, blocking collectives, to_all(): lax.all_to_all(value, ('expert', 'hidden'), split_axis=0, concat_axis=0,...  20.8 us
    ppermute x6, starting transfers between devices, exchange(): lax.ppermute(value, axis, [(source, source ^ step) for source in range(si...  10.1 us
    pallas_call x7, Pallas kernels, call(): pl.pallas_call(kernel, out_shape=outs, in_specs=[VMEM] * len(args) + [HBM...  7.73 us
    ppermute x6, waiting for transfers between devices, exchange(): lax.ppermute(value, axis, [(source, source ^ step) for source in range(si...  1.96 us
  transfers between devices with their start and end apart: 6, of which 3 were waited for; matrix products, arithmetic and copies ran while one was open for 0% of the time, Pallas kernels for 9%

profile of v5, /device:TPU:0, one launch (start us, length us, event | category | flops | bytes accessed | tf_op | source)
XLA Modules:
  0.0 41.2 jit_solution(2872441766310550961)
XLA Ops:
  0.6 1.2 %logits.1 = (f32[8,392]{1,0:T(8,128)S(1)}, bf16[392,256]{1,0:T(8,128)(2,1)S(1)}, bf16[8,256]{1,0:T(8,128)(2,1)S(1)}) custom-call(bf16[196,2,256]{2,1,0:T(2,128)(2,1)} %bitcast.18, bf16[8,256]{1,0:T(8,128)(2,1)} %bitcast.19), custom_call_target="tpu_custom_call" | custom-call | tf_op jit(solution)/shard_map/logits/pallas_call | solution.py:209
  1.8 4.1 %collective-permute-start.2 = (f32[8,392]{1,0:T(8,128)S(1)}, f32[8,392]{1,0:T(8,128)S(1)}, u32[]{:S(2)}, u32[]{:S(2)}) collective-permute-start(f32[8,392]{1,0:T(8,128)S(1)} %get-tuple-element.26.refs_0_), channel_id=1, source_target_pairs={{0,2},{1,3},{2,0},{3,1},{4,6},{5,7},{6,4},{7,5},{8,10},{9,11},{10,... | collective-permute-start | bytes 37640 | tf_op jit(solution)/shard_map/ppermute | solution.py:224
  5.9 1.3 %collective-permute-start.1 = (f32[8,392]{1,0:T(8,128)S(1)}, f32[8,392]{1,0:T(8,128)S(1)}, u32[]{:S(2)}, u32[]{:S(2)}) collective-permute-start(f32[8,392]{1,0:T(8,128)S(1)} %get-tuple-element.26.refs_0_), channel_id=1, source_target_pairs={{0,3},{1,2},{2,1},{3,0},{4,7},{5,6},{6,5},{7,4},{8,11},{9,10},{10,... | collective-permute-start | bytes 37640 | tf_op jit(solution)/shard_map/ppermute | solution.py:224
  7.3 0.2 collective-permute-start
  7.5 2.8 %prepare.1 = (bf16[392,256]{1,0:T(8,128)(2,1)S(1)}, f32[1,1024]{1,0:T(1,128)S(1)}, bf16[1,1024]{1,0:T(2,128)(2,1)S(1)}, bf16[1024,1024]{1,0:T(8,128)(2,1)S(1)}, ...) custom-call(f32[8,392]{1,0:T(8,128)S(1)} %get-tuple-element.26.refs_0_, ...), custom_call_target="tpu_custom_call" | custom-call | tf_op jit(solution)/shard_map/prepare/pallas_call | solution.py:209
  10.3 0.0 collective-permute-done.2.refs_3_
  10.3 1.1 %collective-permute-done.1.refs_2_ = f32[8,392]{1,0:T(8,128)S(1)} collective-permute-done((f32[8,392]{1,0:T(8,128)S(1)}, f32[8,392]{1,0:T(8,128)S(1)}, u32[]{:S(2)}, u32[]{:S(2)}) %collective-permute-start.1) | collective-permute-done | bytes 12576 | tf_op jit(solution)/shard_map/ppermute | solution.py:224
  11.4 0.0 collective-permute-done.refs_1_
  11.4 0.4 %dispatch.1 = (bf16[8,4,2,512]{3,2,1,0:T(2,128)(2,1)S(1)}, f32[8,392]{1,0:T(8,128)S(1)}, f32[8,392]{1,0:T(8,128)S(1)}, f32[1,392]{1,0:T(1,128)S(1)}) custom-call(f32[8,392]{1,0:T(8,128)S(1)} %get-tuple-element.26.refs_0_, f32[8,392]{1,0:T(8,128)S(1)} %collective-permute-done.refs_1_, f32[8,392]{1,0:T(8,128)S(1)} %collective-permute-done.1.refs_2_, ...), custom_call_target="tpu_custom_call" | custom-call | tf_op jit(solution)/shard_map/dispatch/pallas_call | solution.py:209
  11.9 11.6 %all_to_all.10 = bf16[32,2,512]{2,1,0:T(2,128)(2,1)S(1)} all-to-all(bf16[32,2,512]{2,1,0:T(2,128)(2,1)S(1)} %bitcast.14), channel_id=1, replica_groups=mesh['expert'=8,'hidden'=4] {'expert','hidden'}, dimensions={0} | all-to-all | bytes 131072 | tf_op jit(solution)/shard_map/all_to_all | solution.py:277
  23.5 1.2 %expert.1 = bf16[8,4,2,512]{3,2,1,0:T(2,128)(2,1)S(1)} custom-call(bf16[8,4,2,512]{3,2,1,0:T(2,128)(2,1)S(1)} %bitcast.11, f32[1,1024]{1,0:T(1,128)S(1)} %get-tuple-element.30.bout_ref, bf16[1,1024]{1,0:T(2,128)(2,1)S(1)} %get-tuple-element.31.bin_ref, bf16[1024,1024]{1,0:T(8,128)(2,1)S(1)} %get-tuple-element.32.wout_ref, ...), custom_call_target="tpu_custom_call" | custom-call | tf_op jit(solution)/shard_map/expert/pallas_call | solution.py:209
  24.7 9.2 %all_to_all.11 = bf16[32,2,512]{2,1,0:T(2,128)(2,1)S(1)} all-to-all(bf16[32,2,512]{2,1,0:T(2,128)(2,1)S(1)} %bitcast.12), channel_id=1, replica_groups=mesh['expert'=8,'hidden'=4] {'expert','hidden'}, dimensions={0} | all-to-all | bytes 131072 | tf_op jit(solution)/shard_map/all_to_all | solution.py:277
  33.9 0.3 gradient.1
  34.2 0.7 %collective-permute-start.5 = (bf16[8,392]{1,0:T(8,128)(2,1)S(1)}, bf16[8,392]{1,0:T(8,128)(2,1)S(1)}, u32[]{:S(2)}, u32[]{:S(2)}) collective-permute-start(bf16[8,392]{1,0:T(8,128)(2,1)S(1)} %get-tuple-element.38.refs_0_), channel_id=1, source_target_pairs={{0,3},{1,2},{2,1},{3,0},{4,7},{5,6},{6,5},{7,4},{8,11},{9,10},{10,... | collective-permute-start | bytes 18824 | tf_op jit(solution)/shard_map/ppermute | solution.py:224
  35.0 1.0 %collective-permute-start.4 = (bf16[8,392]{1,0:T(8,128)(2,1)S(1)}, bf16[8,392]{1,0:T(8,128)(2,1)S(1)}, u32[]{:S(2)}, u32[]{:S(2)}) collective-permute-start(bf16[8,392]{1,0:T(8,128)(2,1)S(1)} %get-tuple-element.38.refs_0_), channel_id=1, source_target_pairs={{0,2},{1,3},{2,0},{3,1},{4,6},{5,7},{6,4},{7,5},{8,10},{9,11},{10,... | collective-permute-start | bytes 18824 | tf_op jit(solution)/shard_map/ppermute | solution.py:224
  35.9 2.7 %collective-permute-start.3 = (bf16[8,392]{1,0:T(8,128)(2,1)S(1)}, bf16[8,392]{1,0:T(8,128)(2,1)S(1)}, u32[]{:S(2)}, u32[]{:S(2)}) collective-permute-start(bf16[8,392]{1,0:T(8,128)(2,1)S(1)} %get-tuple-element.38.refs_0_), channel_id=1, source_target_pairs={{0,1},{1,0},{2,3},{3,2},{4,5},{5,4},{6,7},{7,6},{8,9},{9,8},{10,11... | collective-permute-start | bytes 18824 | tf_op jit(solution)/shard_map/ppermute | solution.py:224
  38.6 0.8 %mixed.1 = (bf16[196,2,256]{2,1,0:T(2,128)(2,1)S(1)}, f32[392,256]{1,0:T(8,128)S(1)}, f32[2,196]{1,0:T(2,128)S(1)}) custom-call(f32[8,392]{1,0:T(8,128)S(1)} %get-tuple-element.36.dispatch_ref, f32[8,392]{1,0:T(8,128)S(1)} %get-tuple-element.37.combine_ref.refs_4_, f32[1,392]{1,0:T(1,128)S(1)} %get-tuple-element.39.total_ref.refs_5_, ...), custom_call_target="tpu_custom_call" | custom-call | tf_op jit(solution)/shard_map/mixed/pallas_call | solution.py:209
  39.4 0.3 collective-permute-done.5.refs_3_
  39.7 0.0 collective-permute-done.4.refs_2_
  39.7 0.6 %collective-permute-done.3.refs_1_ = bf16[8,392]{1,0:T(8,128)(2,1)S(1)} collective-permute-done((bf16[8,392]{1,0:T(8,128)(2,1)S(1)}, bf16[8,392]{1,0:T(8,128)(2,1)S(1)}, u32[]{:S(2)}, u32[]{:S(2)}) %collective-permute-start.3) | collective-permute-done | bytes 6304 | tf_op jit(solution)/shard_map/ppermute | solution.py:224
  40.2 1.0 %token_grad.1 = (bf16[196,2,256]{2,1,0:T(2,128)(2,1)}, bf16[196,2,256]{2,1,0:T(2,128)(2,1)}, f32[2,196]{1,0:T(2,128)}) custom-call(bf16[8,392]{1,0:T(8,128)(2,1)S(1)} %get-tuple-element.38.refs_0_, bf16[8,392]{1,0:T(8,128)(2,1)S(1)} %collective-permute-done.3.refs_1_, bf16[8,392]{1,0:T(8,128)(2,1)S(1)} %collective-permute-done.4.refs_2_, ...), custom_call_target="tpu_custom_call" | custom-call | tf_op jit(solution)/shard_map/token_grad/pallas_call | solution.py:209
Async XLA Ops:
  1.8 8.5 %collective-permute-start.2 = (f32[8,392]{1,0:T(8,128)S(1)}, f32[8,392]{1,0:T(8,128)S(1)}, u32[]{:S(2)}, u32[]{:S(2)}) collective-permute-start(f32[8,392]{1,0:T(8,128)S(1)} %get-tuple-element.26.refs_0_), channel_id=1, source_target_pairs={{0,2},{1,3},{2,0},{3,1},{4,6},{5,7},{6,4},{7,5},{8,10},{9,11},{10,... | collective-permute-start | bytes 37640 | tf_op jit(solution)/shard_map/ppermute | solution.py:224
  5.9 5.5 %collective-permute-start.1 = (f32[8,392]{1,0:T(8,128)S(1)}, f32[8,392]{1,0:T(8,128)S(1)}, u32[]{:S(2)}, u32[]{:S(2)}) collective-permute-start(f32[8,392]{1,0:T(8,128)S(1)} %get-tuple-element.26.refs_0_), channel_id=1, source_target_pairs={{0,3},{1,2},{2,1},{3,0},{4,7},{5,6},{6,5},{7,4},{8,11},{9,10},{10,... | collective-permute-start | bytes 37640 | tf_op jit(solution)/shard_map/ppermute | solution.py:224
  7.3 4.2 %collective-permute-start = (f32[8,392]{1,0:T(8,128)S(1)}, f32[8,392]{1,0:T(8,128)S(1)}, u32[]{:S(2)}, u32[]{:S(2)}) collective-permute-start(f32[8,392]{1,0:T(8,128)S(1)} %get-tuple-element.26.refs_0_), channel_id=1, source_target_pairs={{0,1},{1,0},{2,3},{3,2},{4,5},{5,4},{6,7},{7,6},{8,9},{9,8},{10,11... | collective-permute-start | bytes 37640 | tf_op jit(solution)/shard_map/ppermute | solution.py:224
  34.2 5.5 %collective-permute-start.5 = (bf16[8,392]{1,0:T(8,128)(2,1)S(1)}, bf16[8,392]{1,0:T(8,128)(2,1)S(1)}, u32[]{:S(2)}, u32[]{:S(2)}) collective-permute-start(bf16[8,392]{1,0:T(8,128)(2,1)S(1)} %get-tuple-element.38.refs_0_), channel_id=1, source_target_pairs={{0,3},{1,2},{2,1},{3,0},{4,7},{5,6},{6,5},{7,4},{8,11},{9,10},{10,... | collective-permute-start | bytes 18824 | tf_op jit(solution)/shard_map/ppermute | solution.py:224
  35.0 4.7 %collective-permute-start.4 = (bf16[8,392]{1,0:T(8,128)(2,1)S(1)}, bf16[8,392]{1,0:T(8,128)(2,1)S(1)}, u32[]{:S(2)}, u32[]{:S(2)}) collective-permute-start(bf16[8,392]{1,0:T(8,128)(2,1)S(1)} %get-tuple-element.38.refs_0_), channel_id=1, source_target_pairs={{0,2},{1,3},{2,0},{3,1},{4,6},{5,7},{6,4},{7,5},{8,10},{9,11},{10,... | collective-permute-start | bytes 18824 | tf_op jit(solution)/shard_map/ppermute | solution.py:224
  35.9 4.3 %collective-permute-start.3 = (bf16[8,392]{1,0:T(8,128)(2,1)S(1)}, bf16[8,392]{1,0:T(8,128)(2,1)S(1)}, u32[]{:S(2)}, u32[]{:S(2)}) collective-permute-start(bf16[8,392]{1,0:T(8,128)(2,1)S(1)} %get-tuple-element.38.refs_0_), channel_id=1, source_target_pairs={{0,1},{1,0},{2,3},{3,2},{4,5},{5,4},{6,7},{7,6},{8,9},{9,8},{10,11... | collective-permute-start | bytes 18824 | tf_op jit(solution)/shard_map/ppermute | solution.py:224

commit v6 on v5

--- a/solution.py
+++ b/solution.py
@@ -10,6 +10,8 @@
 VMEM = pl.BlockSpec(memory_space=pltpu.VMEM)
 HBM = pl.BlockSpec(memory_space=pltpu.HBM)
 MIB = 1024 * 1024
+expert = ("expert_a", "expert_b", "expert_c")
+send_order = ("expert_a", "expert_c", "expert_b", "hidden")
 weight_pieces = 2
 
 
@@ -73,10 +75,25 @@
     return copies
 
 
-def logits_kernel(tokens_ref, keys_in_ref, part_ref, rows_ref, keys_ref, held_ref, sems):
+def in_turn(keys, halves):
+    slots = keys.shape[0]
+    middle = slots // (halves * halves)
+    to, source = iota((slots, slots), 0), iota((slots, slots), 1)
+    pick = jnp.zeros((slots, slots), f32)
+    for a in range(halves):
+        for c in range(halves):
+            b = to - (a * halves + c) * middle
+            here = (b >= 0) & (b < middle) & (source == (a * middle + b) * halves + c)
+            pick = jnp.where(here, 1.0, pick)
+    return dot(pick.astype(bf16), keys, 1, 0).astype(bf16)
+
+
+def logits_kernel(halves, tokens_ref, keys_in_ref, part_ref, rows_ref, keys_ref, held_ref, held_keys_ref, sems):
     tokens, images, width = tokens_ref.shape
-    for copy in load((tokens_ref, keys_in_ref), (held_ref, keys_ref), sems):
-        copy.wait()
+    copies = load((tokens_ref, keys_in_ref), (held_ref, held_keys_ref), sems)
+    copies[1].wait()
+    keys_ref[...] = in_turn(held_keys_ref[...], halves)
+    copies[0].wait()
     rows = held_ref[...].reshape(tokens * images, width)
     rows_ref[...] = rows
     part_ref[...] = dot(keys_ref[...], rows, 1, 1)
@@ -227,7 +244,7 @@
 
 def per_device(tokens, slot_params, weight_in, bias_in, weight_out, bias_out, cotangent):
     images, count, width = tokens.shape
-    groups, hidden = lax.axis_size("expert"), lax.axis_size("hidden")
+    groups, hidden = lax.axis_size(expert), lax.axis_size("hidden")
     slots = slot_params.shape[1]
     wide = weight_in.shape[1]
     rows = images * count
@@ -240,12 +257,12 @@
     sent_shape = pltpu.VMEM((groups, hidden, images, 2 * width), bf16)
 
     part, token_rows, keys = call(
-        logits_kernel,
+        lambda *refs: logits_kernel(lax.axis_size("expert_c"), *refs),
         [table, row_shape, pltpu.VMEM((slots, width), bf16)],
         (),
         "logits",
         far=(by_token, jnp.transpose(slot_params)),
-        scratch=[held_shape, pltpu.SemaphoreType.DMA((2,))],
+        scratch=[held_shape, pltpu.VMEM((slots, width), bf16), pltpu.SemaphoreType.DMA((2,))],
     )
     grad_rows, *expert_values = call(
         lambda *refs: prepare_kernel("hidden", *refs),
@@ -274,7 +291,7 @@
 
     def to_all(value):
         value = value.reshape(groups * hidden, images, 2 * width)
-        value = lax.all_to_all(value, ("expert", "hidden"), split_axis=0, concat_axis=0, tiled=True)
+        value = lax.all_to_all(value, send_order, split_axis=0, concat_axis=0, tiled=True)
         return value.reshape(groups, hidden, images, 2 * width)
 
     (sent,) = call(
@@ -310,18 +327,21 @@
 
 
 def solution(mesh):
+    groups, hidden = mesh.devices.shape
+    halves = 2 if groups % 4 == 0 else 1
+    parts = (halves, groups // (halves * halves), halves, hidden)
     return jax.shard_map(
         per_device,
-        mesh=mesh,
+        mesh=jax.sharding.Mesh(mesh.devices.reshape(parts), (*expert, "hidden")),
         in_specs=(
-            P("expert", None, "hidden"),
+            P(expert, None, "hidden"),
             P("hidden", None),
-            P("expert", None, "hidden"),
-            P("expert", "hidden"),
-            P("expert", "hidden", None),
-            P("expert", "hidden"),
-            P("expert", None, "hidden"),
+            P(expert, None, "hidden"),
+            P(expert, "hidden"),
+            P(expert, "hidden", None),
+            P(expert, "hidden"),
+            P(expert, None, "hidden"),
         ),
-        out_specs=(P("expert", None, "hidden"), P("expert", None, "hidden"), P("expert", None)),
+        out_specs=(P(expert, None, "hidden"), P(expert, None, "hidden"), P(expert, None)),
         check_vma=False,
     )

time: 41.4 us -> 41 us (level)
  blocking collectives: 20.8 us -> 20.3 us
    all_to_all x2, blocking collectives: 20.8 us -> 20.3 us  [to_all(): lax.all_to_all(value, send_order, split_axis=0, concat_axis=0, tiled=True)]
where the time goes in v6:
time: 41 us; the launch traced here: 40.8 us
  blocking collectives  20.3 us (50%)
  starting transfers between devices  10.1 us (25%)
  Pallas kernels  7.73 us (19%)
  waiting for transfers between devices  1.96 us (5%)
  between operations  0.67 us (2%)
    all_to_all x2, blocking collectives, to_all(): lax.all_to_all(value, send_order, split_axis=0, concat_axis=0, tiled=True)  20.3 us
    ppermute x6, starting transfers between devices, exchange(): lax.ppermute(value, axis, [(source, source ^ step) for source in range(si...  10.1 us
    pallas_call x7, Pallas kernels, call(): pl.pallas_call(kernel, out_shape=outs, in_specs=[VMEM] * len(args) + [HBM...  7.73 us
    ppermute x6, waiting for transfers between devices, exchange(): lax.ppermute(value, axis, [(source, source ^ step) for source in range(si...  1.96 us
  transfers between devices with their start and end apart: 6, of which 3 were waited for; matrix products, arithmetic and copies ran while one was open for 0% of the time, Pallas kernels for 9%

profile of v6, /device:TPU:0, one launch (start us, length us, event | category | flops | bytes accessed | tf_op | source)
XLA Modules:
  0.0 40.8 jit_solution(11458042702693228032)
XLA Ops:
  0.6 1.2 %logits.1 = (f32[8,392]{1,0:T(8,128)S(1)}, bf16[392,256]{1,0:T(8,128)(2,1)S(1)}, bf16[8,256]{1,0:T(8,128)(2,1)S(1)}) custom-call(bf16[196,2,256]{2,1,0:T(2,128)(2,1)} %bitcast.18, bf16[8,256]{1,0:T(8,128)(2,1)} %bitcast.19), custom_call_target="tpu_custom_call" | custom-call | tf_op jit(solution)/shard_map/logits/pallas_call | solution.py:226
  1.8 4.1 %collective-permute-start.2 = (f32[8,392]{1,0:T(8,128)S(1)}, f32[8,392]{1,0:T(8,128)S(1)}, u32[]{:S(2)}, u32[]{:S(2)}) collective-permute-start(f32[8,392]{1,0:T(8,128)S(1)} %get-tuple-element.26.refs_0_), channel_id=1, source_target_pairs={{0,2},{1,3},{2,0},{3,1},{4,6},{5,7},{6,4},{7,5},{8,10},{9,11},{10,... | collective-permute-start | bytes 37640 | tf_op jit(solution)/shard_map/ppermute | solution.py:241
  5.9 1.3 %collective-permute-start.1 = (f32[8,392]{1,0:T(8,128)S(1)}, f32[8,392]{1,0:T(8,128)S(1)}, u32[]{:S(2)}, u32[]{:S(2)}) collective-permute-start(f32[8,392]{1,0:T(8,128)S(1)} %get-tuple-element.26.refs_0_), channel_id=1, source_target_pairs={{0,3},{1,2},{2,1},{3,0},{4,7},{5,6},{6,5},{7,4},{8,11},{9,10},{10,... | collective-permute-start | bytes 37640 | tf_op jit(solution)/shard_map/ppermute | solution.py:241
  7.2 0.2 collective-permute-start
  7.5 2.8 %prepare.1 = (bf16[392,256]{1,0:T(8,128)(2,1)S(1)}, f32[1,1024]{1,0:T(1,128)S(1)}, bf16[1,1024]{1,0:T(2,128)(2,1)S(1)}, bf16[1024,1024]{1,0:T(8,128)(2,1)S(1)}, ...) custom-call(f32[8,392]{1,0:T(8,128)S(1)} %get-tuple-element.26.refs_0_, ...), custom_call_target="tpu_custom_call" | custom-call | tf_op jit(solution)/shard_map/prepare/pallas_call | solution.py:226
  10.3 0.0 collective-permute-done.2.refs_3_
  10.3 1.1 %collective-permute-done.1.refs_2_ = f32[8,392]{1,0:T(8,128)S(1)} collective-permute-done((f32[8,392]{1,0:T(8,128)S(1)}, f32[8,392]{1,0:T(8,128)S(1)}, u32[]{:S(2)}, u32[]{:S(2)}) %collective-permute-start.1) | collective-permute-done | bytes 12576 | tf_op jit(solution)/shard_map/ppermute | solution.py:241
  11.4 0.0 collective-permute-done.refs_1_
  11.4 0.4 %dispatch.1 = (bf16[8,4,2,512]{3,2,1,0:T(2,128)(2,1)S(1)}, f32[8,392]{1,0:T(8,128)S(1)}, f32[8,392]{1,0:T(8,128)S(1)}, f32[1,392]{1,0:T(1,128)S(1)}) custom-call(f32[8,392]{1,0:T(8,128)S(1)} %get-tuple-element.26.refs_0_, f32[8,392]{1,0:T(8,128)S(1)} %collective-permute-done.refs_1_, f32[8,392]{1,0:T(8,128)S(1)} %collective-permute-done.1.refs_2_, ...), custom_call_target="tpu_custom_call" | custom-call | tf_op jit(solution)/shard_map/dispatch/pallas_call | solution.py:226
  11.9 11.4 %all_to_all.10 = bf16[32,2,512]{2,1,0:T(2,128)(2,1)S(1)} all-to-all(bf16[32,2,512]{2,1,0:T(2,128)(2,1)S(1)} %bitcast.14), channel_id=1, replica_groups=mesh['expert_a'=2,'expert_b'=2,'expert_c'=2,'hidden'=4] {'expert_a','exp..., dimensions={0} | all-to-all | bytes 131072 | tf_op jit(solution)/shard_map/all_to_all | solution.py:294
  23.2 1.2 %expert.1 = bf16[8,4,2,512]{3,2,1,0:T(2,128)(2,1)S(1)} custom-call(bf16[8,4,2,512]{3,2,1,0:T(2,128)(2,1)S(1)} %bitcast.11, f32[1,1024]{1,0:T(1,128)S(1)} %get-tuple-element.30.bout_ref, bf16[1,1024]{1,0:T(2,128)(2,1)S(1)} %get-tuple-element.31.bin_ref, bf16[1024,1024]{1,0:T(8,128)(2,1)S(1)} %get-tuple-element.32.wout_ref, ...), custom_call_target="tpu_custom_call" | custom-call | tf_op jit(solution)/shard_map/expert/pallas_call | solution.py:226
  24.5 9.0 %all_to_all.11 = bf16[32,2,512]{2,1,0:T(2,128)(2,1)S(1)} all-to-all(bf16[32,2,512]{2,1,0:T(2,128)(2,1)S(1)} %bitcast.12), channel_id=1, replica_groups=mesh['expert_a'=2,'expert_b'=2,'expert_c'=2,'hidden'=4] {'expert_a','exp..., dimensions={0} | all-to-all | bytes 131072 | tf_op jit(solution)/shard_map/all_to_all | solution.py:294
  33.4 0.3 gradient.1
  33.8 0.7 %collective-permute-start.5 = (bf16[8,392]{1,0:T(8,128)(2,1)S(1)}, bf16[8,392]{1,0:T(8,128)(2,1)S(1)}, u32[]{:S(2)}, u32[]{:S(2)}) collective-permute-start(bf16[8,392]{1,0:T(8,128)(2,1)S(1)} %get-tuple-element.38.refs_0_), channel_id=1, source_target_pairs={{0,3},{1,2},{2,1},{3,0},{4,7},{5,6},{6,5},{7,4},{8,11},{9,10},{10,... | collective-permute-start | bytes 18824 | tf_op jit(solution)/shard_map/ppermute | solution.py:241
  34.5 1.5 %collective-permute-start.4 = (bf16[8,392]{1,0:T(8,128)(2,1)S(1)}, bf16[8,392]{1,0:T(8,128)(2,1)S(1)}, u32[]{:S(2)}, u32[]{:S(2)}) collective-permute-start(bf16[8,392]{1,0:T(8,128)(2,1)S(1)} %get-tuple-element.38.refs_0_), channel_id=1, source_target_pairs={{0,2},{1,3},{2,0},{3,1},{4,6},{5,7},{6,4},{7,5},{8,10},{9,11},{10,... | collective-permute-start | bytes 18824 | tf_op jit(solution)/shard_map/ppermute | solution.py:241
  36.0 2.2 %collective-permute-start.3 = (bf16[8,392]{1,0:T(8,128)(2,1)S(1)}, bf16[8,392]{1,0:T(8,128)(2,1)S(1)}, u32[]{:S(2)}, u32[]{:S(2)}) collective-permute-start(bf16[8,392]{1,0:T(8,128)(2,1)S(1)} %get-tuple-element.38.refs_0_), channel_id=1, source_target_pairs={{0,1},{1,0},{2,3},{3,2},{4,5},{5,4},{6,7},{7,6},{8,9},{9,8},{10,11... | collective-permute-start | bytes 18824 | tf_op jit(solution)/shard_map/ppermute | solution.py:241
  38.2 0.8 %mixed.1 = (bf16[196,2,256]{2,1,0:T(2,128)(2,1)S(1)}, f32[392,256]{1,0:T(8,128)S(1)}, f32[2,196]{1,0:T(2,128)S(1)}) custom-call(f32[8,392]{1,0:T(8,128)S(1)} %get-tuple-element.36.dispatch_ref, f32[8,392]{1,0:T(8,128)S(1)} %get-tuple-element.37.combine_ref.refs_4_, f32[1,392]{1,0:T(1,128)S(1)} %get-tuple-element.39.total_ref.refs_5_, ...), custom_call_target="tpu_custom_call" | custom-call | tf_op jit(solution)/shard_map/mixed/pallas_call | solution.py:226
  38.9 0.3 collective-permute-done.5.refs_3_
  39.2 0.0 collective-permute-done.4.refs_2_
  39.2 0.6 %collective-permute-done.3.refs_1_ = bf16[8,392]{1,0:T(8,128)(2,1)S(1)} collective-permute-done((bf16[8,392]{1,0:T(8,128)(2,1)S(1)}, bf16[8,392]{1,0:T(8,128)(2,1)S(1)}, u32[]{:S(2)}, u32[]{:S(2)}) %collective-permute-start.3) | collective-permute-done | bytes 6304 | tf_op jit(solution)/shard_map/ppermute | solution.py:241
  39.8 1.0 %token_grad.1 = (bf16[196,2,256]{2,1,0:T(2,128)(2,1)}, bf16[196,2,256]{2,1,0:T(2,128)(2,1)}, f32[2,196]{1,0:T(2,128)}) custom-call(bf16[8,392]{1,0:T(8,128)(2,1)S(1)} %get-tuple-element.38.refs_0_, bf16[8,392]{1,0:T(8,128)(2,1)S(1)} %collective-permute-done.3.refs_1_, bf16[8,392]{1,0:T(8,128)(2,1)S(1)} %collective-permute-done.4.refs_2_, ...), custom_call_target="tpu_custom_call" | custom-call | tf_op jit(solution)/shard_map/token_grad/pallas_call | solution.py:226
Async XLA Ops:
  1.8 8.5 %collective-permute-start.2 = (f32[8,392]{1,0:T(8,128)S(1)}, f32[8,392]{1,0:T(8,128)S(1)}, u32[]{:S(2)}, u32[]{:S(2)}) collective-permute-start(f32[8,392]{1,0:T(8,128)S(1)} %get-tuple-element.26.refs_0_), channel_id=1, source_target_pairs={{0,2},{1,3},{2,0},{3,1},{4,6},{5,7},{6,4},{7,5},{8,10},{9,11},{10,... | collective-permute-start | bytes 37640 | tf_op jit(solution)/shard_map/ppermute | solution.py:241
  5.9 5.5 %collective-permute-start.1 = (f32[8,392]{1,0:T(8,128)S(1)}, f32[8,392]{1,0:T(8,128)S(1)}, u32[]{:S(2)}, u32[]{:S(2)}) collective-permute-start(f32[8,392]{1,0:T(8,128)S(1)} %get-tuple-element.26.refs_0_), channel_id=1, source_target_pairs={{0,3},{1,2},{2,1},{3,0},{4,7},{5,6},{6,5},{7,4},{8,11},{9,10},{10,... | collective-permute-start | bytes 37640 | tf_op jit(solution)/shard_map/ppermute | solution.py:241
  7.2 4.2 %collective-permute-start = (f32[8,392]{1,0:T(8,128)S(1)}, f32[8,392]{1,0:T(8,128)S(1)}, u32[]{:S(2)}, u32[]{:S(2)}) collective-permute-start(f32[8,392]{1,0:T(8,128)S(1)} %get-tuple-element.26.refs_0_), channel_id=1, source_target_pairs={{0,1},{1,0},{2,3},{3,2},{4,5},{5,4},{6,7},{7,6},{8,9},{9,8},{10,11... | collective-permute-start | bytes 37640 | tf_op jit(solution)/shard_map/ppermute | solution.py:241
  33.8 5.5 %collective-permute-start.5 = (bf16[8,392]{1,0:T(8,128)(2,1)S(1)}, bf16[8,392]{1,0:T(8,128)(2,1)S(1)}, u32[]{:S(2)}, u32[]{:S(2)}) collective-permute-start(bf16[8,392]{1,0:T(8,128)(2,1)S(1)} %get-tuple-element.38.refs_0_), channel_id=1, source_target_pairs={{0,3},{1,2},{2,1},{3,0},{4,7},{5,6},{6,5},{7,4},{8,11},{9,10},{10,... | collective-permute-start | bytes 18824 | tf_op jit(solution)/shard_map/ppermute | solution.py:241
  34.5 4.7 %collective-permute-start.4 = (bf16[8,392]{1,0:T(8,128)(2,1)S(1)}, bf16[8,392]{1,0:T(8,128)(2,1)S(1)}, u32[]{:S(2)}, u32[]{:S(2)}) collective-permute-start(bf16[8,392]{1,0:T(8,128)(2,1)S(1)} %get-tuple-element.38.refs_0_), channel_id=1, source_target_pairs={{0,2},{1,3},{2,0},{3,1},{4,6},{5,7},{6,4},{7,5},{8,10},{9,11},{10,... | collective-permute-start | bytes 18824 | tf_op jit(solution)/shard_map/ppermute | solution.py:241
  36.0 3.8 %collective-permute-start.3 = (bf16[8,392]{1,0:T(8,128)(2,1)S(1)}, bf16[8,392]{1,0:T(8,128)(2,1)S(1)}, u32[]{:S(2)}, u32[]{:S(2)}) collective-permute-start(bf16[8,392]{1,0:T(8,128)(2,1)S(1)} %get-tuple-element.38.refs_0_), channel_id=1, source_target_pairs={{0,1},{1,0},{2,3},{3,2},{4,5},{5,4},{6,7},{7,6},{8,9},{9,8},{10,11... | collective-permute-start | bytes 18824 | tf_op jit(solution)/shard_map/ppermute | solution.py:241

commit v7 on v6

--- a/solution.py
+++ b/solution.py
@@ -128,7 +128,7 @@
 
 
 def steps(size, first):
-    return [1] + list(range(size - 1, 1, -1)) if first else list(range(1, size))
+    return list(range(2, size)) + [1] if first else list(range(1, size))
 
 
 def tree_sum(refs, first):

time: 41 us -> 40.9 us (level)
  blocking collectives: 20.3 us -> 19.6 us
  waiting for transfers between devices: 1.96 us -> 2.53 us
    all_to_all x2, blocking collectives: 20.3 us -> 19.6 us  [to_all(): lax.all_to_all(value, send_order, split_axis=0, concat_axis=0, tiled=True)]
    ppermute x6, waiting for transfers between devices: 1.96 us -> 2.53 us  [exchange(): lax.ppermute(value, axis, [(source, source ^ step) for source in range(si...]
  transfers between devices with their start and end apart: 6 -> 6, of which waited for: 3 -> 4; matrix products, arithmetic and copies ran while one was open for 0% -> 0% of each run, Pallas kernels for 9% -> 9%
where the time goes in v7:
time: 40.9 us; the launch traced here: 40.6 us
  blocking collectives  19.6 us (48%)
  starting transfers between devices  10.1 us (25%)
  Pallas kernels  7.73 us (19%)
  waiting for transfers between devices  2.53 us (6%)
  between operations  0.67 us (2%)
    all_to_all x2, blocking collectives, to_all(): lax.all_to_all(value, send_order, split_axis=0, concat_axis=0, tiled=True)  19.6 us
    ppermute x6, starting transfers between devices, exchange(): lax.ppermute(value, axis, [(source, source ^ step) for source in range(si...  10.1 us
    pallas_call x7, Pallas kernels, call(): pl.pallas_call(kernel, out_shape=outs, in_specs=[VMEM] * len(args) + [HBM...  7.73 us
    ppermute x6, waiting for transfers between devices, exchange(): lax.ppermute(value, axis, [(source, source ^ step) for source in range(si...  2.53 us
  transfers between devices with their start and end apart: 6, of which 4 were waited for; matrix products, arithmetic and copies ran while one was open for 0% of the time, Pallas kernels for 9%

profile of v7, /device:TPU:0, one launch (start us, length us, event | category | flops | bytes accessed | tf_op | source)
XLA Modules:
  0.0 40.6 jit_solution(8766473108935347654)
XLA Ops:
  0.6 1.2 %logits.1 = (f32[8,392]{1,0:T(8,128)S(1)}, bf16[392,256]{1,0:T(8,128)(2,1)S(1)}, bf16[8,256]{1,0:T(8,128)(2,1)S(1)}) custom-call(bf16[196,2,256]{2,1,0:T(2,128)(2,1)} %bitcast.18, bf16[8,256]{1,0:T(8,128)(2,1)} %bitcast.19), custom_call_target="tpu_custom_call" | custom-call | tf_op jit(solution)/shard_map/logits/pallas_call | solution.py:226
  1.8 3.1 %collective-permute-start.2 = (f32[8,392]{1,0:T(8,128)S(1)}, f32[8,392]{1,0:T(8,128)S(1)}, u32[]{:S(2)}, u32[]{:S(2)}) collective-permute-start(f32[8,392]{1,0:T(8,128)S(1)} %get-tuple-element.26.refs_0_), channel_id=1, source_target_pairs={{0,1},{1,0},{2,3},{3,2},{4,5},{5,4},{6,7},{7,6},{8,9},{9,8},{10,11... | collective-permute-start | bytes 37640 | tf_op jit(solution)/shard_map/ppermute | solution.py:241
  4.9 2.5 %collective-permute-start.1 = (f32[8,392]{1,0:T(8,128)S(1)}, f32[8,392]{1,0:T(8,128)S(1)}, u32[]{:S(2)}, u32[]{:S(2)}) collective-permute-start(f32[8,392]{1,0:T(8,128)S(1)} %get-tuple-element.26.refs_0_), channel_id=1, source_target_pairs={{0,3},{1,2},{2,1},{3,0},{4,7},{5,6},{6,5},{7,4},{8,11},{9,10},{10,... | collective-permute-start | bytes 37640 | tf_op jit(solution)/shard_map/ppermute | solution.py:241
  7.4 0.1 collective-permute-start
  7.5 2.8 %prepare.1 = (bf16[392,256]{1,0:T(8,128)(2,1)S(1)}, f32[1,1024]{1,0:T(1,128)S(1)}, bf16[1,1024]{1,0:T(2,128)(2,1)S(1)}, bf16[1024,1024]{1,0:T(8,128)(2,1)S(1)}, ...) custom-call(f32[8,392]{1,0:T(8,128)S(1)} %get-tuple-element.26.refs_0_, ...), custom_call_target="tpu_custom_call" | custom-call | tf_op jit(solution)/shard_map/prepare/pallas_call | solution.py:226
  10.3 0.0 collective-permute-done.2.refs_3_
  10.3 0.3 collective-permute-done.1.refs_2_
  10.7 1.4 %collective-permute-done.refs_1_ = f32[8,392]{1,0:T(8,128)S(1)} collective-permute-done((f32[8,392]{1,0:T(8,128)S(1)}, f32[8,392]{1,0:T(8,128)S(1)}, u32[]{:S(2)}, u32[]{:S(2)}) %collective-permute-start) | collective-permute-done | bytes 12576 | tf_op jit(solution)/shard_map/ppermute | solution.py:241
  12.0 0.4 %dispatch.1 = (bf16[8,4,2,512]{3,2,1,0:T(2,128)(2,1)S(1)}, f32[8,392]{1,0:T(8,128)S(1)}, f32[8,392]{1,0:T(8,128)S(1)}, f32[1,392]{1,0:T(1,128)S(1)}) custom-call(f32[8,392]{1,0:T(8,128)S(1)} %get-tuple-element.26.refs_0_, f32[8,392]{1,0:T(8,128)S(1)} %collective-permute-done.refs_1_, f32[8,392]{1,0:T(8,128)S(1)} %collective-permute-done.1.refs_2_, ...), custom_call_target="tpu_custom_call" | custom-call | tf_op jit(solution)/shard_map/dispatch/pallas_call | solution.py:226
  12.5 10.7 %all_to_all.10 = bf16[32,2,512]{2,1,0:T(2,128)(2,1)S(1)} all-to-all(bf16[32,2,512]{2,1,0:T(2,128)(2,1)S(1)} %bitcast.14), channel_id=1, replica_groups=mesh['expert_a'=2,'expert_b'=2,'expert_c'=2,'hidden'=4] {'expert_a','exp..., dimensions={0} | all-to-all | bytes 131072 | tf_op jit(solution)/shard_map/all_to_all | solution.py:294
  23.1 1.2 %expert.1 = bf16[8,4,2,512]{3,2,1,0:T(2,128)(2,1)S(1)} custom-call(bf16[8,4,2,512]{3,2,1,0:T(2,128)(2,1)S(1)} %bitcast.11, f32[1,1024]{1,0:T(1,128)S(1)} %get-tuple-element.30.bout_ref, bf16[1,1024]{1,0:T(2,128)(2,1)S(1)} %get-tuple-element.31.bin_ref, bf16[1024,1024]{1,0:T(8,128)(2,1)S(1)} %get-tuple-element.32.wout_ref, ...), custom_call_target="tpu_custom_call" | custom-call | tf_op jit(solution)/shard_map/expert/pallas_call | solution.py:226
  24.3 9.0 %all_to_all.11 = bf16[32,2,512]{2,1,0:T(2,128)(2,1)S(1)} all-to-all(bf16[32,2,512]{2,1,0:T(2,128)(2,1)S(1)} %bitcast.12), channel_id=1, replica_groups=mesh['expert_a'=2,'expert_b'=2,'expert_c'=2,'hidden'=4] {'expert_a','exp..., dimensions={0} | all-to-all | bytes 131072 | tf_op jit(solution)/shard_map/all_to_all | solution.py:294
  33.3 0.3 gradient.1
  33.7 0.7 %collective-permute-start.5 = (bf16[8,392]{1,0:T(8,128)(2,1)S(1)}, bf16[8,392]{1,0:T(8,128)(2,1)S(1)}, u32[]{:S(2)}, u32[]{:S(2)}) collective-permute-start(bf16[8,392]{1,0:T(8,128)(2,1)S(1)} %get-tuple-element.38.refs_0_), channel_id=1, source_target_pairs={{0,3},{1,2},{2,1},{3,0},{4,7},{5,6},{6,5},{7,4},{8,11},{9,10},{10,... | collective-permute-start | bytes 18824 | tf_op jit(solution)/shard_map/ppermute | solution.py:241
  34.4 1.5 %collective-permute-start.4 = (bf16[8,392]{1,0:T(8,128)(2,1)S(1)}, bf16[8,392]{1,0:T(8,128)(2,1)S(1)}, u32[]{:S(2)}, u32[]{:S(2)}) collective-permute-start(bf16[8,392]{1,0:T(8,128)(2,1)S(1)} %get-tuple-element.38.refs_0_), channel_id=1, source_target_pairs={{0,2},{1,3},{2,0},{3,1},{4,6},{5,7},{6,4},{7,5},{8,10},{9,11},{10,... | collective-permute-start | bytes 18824 | tf_op jit(solution)/shard_map/ppermute | solution.py:241
  35.9 2.2 %collective-permute-start.3 = (bf16[8,392]{1,0:T(8,128)(2,1)S(1)}, bf16[8,392]{1,0:T(8,128)(2,1)S(1)}, u32[]{:S(2)}, u32[]{:S(2)}) collective-permute-start(bf16[8,392]{1,0:T(8,128)(2,1)S(1)} %get-tuple-element.38.refs_0_), channel_id=1, source_target_pairs={{0,1},{1,0},{2,3},{3,2},{4,5},{5,4},{6,7},{7,6},{8,9},{9,8},{10,11... | collective-permute-start | bytes 18824 | tf_op jit(solution)/shard_map/ppermute | solution.py:241
  38.0 0.8 %mixed.1 = (bf16[196,2,256]{2,1,0:T(2,128)(2,1)S(1)}, f32[392,256]{1,0:T(8,128)S(1)}, f32[2,196]{1,0:T(2,128)S(1)}) custom-call(f32[8,392]{1,0:T(8,128)S(1)} %get-tuple-element.36.dispatch_ref, f32[8,392]{1,0:T(8,128)S(1)} %get-tuple-element.37.combine_ref.refs_4_, f32[1,392]{1,0:T(1,128)S(1)} %get-tuple-element.39.total_ref.refs_5_, ...), custom_call_target="tpu_custom_call" | custom-call | tf_op jit(solution)/shard_map/mixed/pallas_call | solution.py:226
  38.8 0.3 collective-permute-done.5.refs_3_
  39.1 0.0 collective-permute-done.4.refs_2_
  39.1 0.6 %collective-permute-done.3.refs_1_ = bf16[8,392]{1,0:T(8,128)(2,1)S(1)} collective-permute-done((bf16[8,392]{1,0:T(8,128)(2,1)S(1)}, bf16[8,392]{1,0:T(8,128)(2,1)S(1)}, u32[]{:S(2)}, u32[]{:S(2)}) %collective-permute-start.3) | collective-permute-done | bytes 6304 | tf_op jit(solution)/shard_map/ppermute | solution.py:241
  39.7 1.0 %token_grad.1 = (bf16[196,2,256]{2,1,0:T(2,128)(2,1)}, bf16[196,2,256]{2,1,0:T(2,128)(2,1)}, f32[2,196]{1,0:T(2,128)}) custom-call(bf16[8,392]{1,0:T(8,128)(2,1)S(1)} %get-tuple-element.38.refs_0_, bf16[8,392]{1,0:T(8,128)(2,1)S(1)} %collective-permute-done.3.refs_1_, bf16[8,392]{1,0:T(8,128)(2,1)S(1)} %collective-permute-done.4.refs_2_, ...), custom_call_target="tpu_custom_call" | custom-call | tf_op jit(solution)/shard_map/token_grad/pallas_call | solution.py:226
Async XLA Ops:
  1.8 8.5 %collective-permute-start.2 = (f32[8,392]{1,0:T(8,128)S(1)}, f32[8,392]{1,0:T(8,128)S(1)}, u32[]{:S(2)}, u32[]{:S(2)}) collective-permute-start(f32[8,392]{1,0:T(8,128)S(1)} %get-tuple-element.26.refs_0_), channel_id=1, source_target_pairs={{0,1},{1,0},{2,3},{3,2},{4,5},{5,4},{6,7},{7,6},{8,9},{9,8},{10,11... | collective-permute-start | bytes 37640 | tf_op jit(solution)/shard_map/ppermute | solution.py:241
  4.9 5.8 %collective-permute-start.1 = (f32[8,392]{1,0:T(8,128)S(1)}, f32[8,392]{1,0:T(8,128)S(1)}, u32[]{:S(2)}, u32[]{:S(2)}) collective-permute-start(f32[8,392]{1,0:T(8,128)S(1)} %get-tuple-element.26.refs_0_), channel_id=1, source_target_pairs={{0,3},{1,2},{2,1},{3,0},{4,7},{5,6},{6,5},{7,4},{8,11},{9,10},{10,... | collective-permute-start | bytes 37640 | tf_op jit(solution)/shard_map/ppermute | solution.py:241
  7.4 4.6 %collective-permute-start = (f32[8,392]{1,0:T(8,128)S(1)}, f32[8,392]{1,0:T(8,128)S(1)}, u32[]{:S(2)}, u32[]{:S(2)}) collective-permute-start(f32[8,392]{1,0:T(8,128)S(1)} %get-tuple-element.26.refs_0_), channel_id=1, source_target_pairs={{0,2},{1,3},{2,0},{3,1},{4,6},{5,7},{6,4},{7,5},{8,10},{9,11},{10,... | collective-permute-start | bytes 37640 | tf_op jit(solution)/shard_map/ppermute | solution.py:241
  33.7 5.5 %collective-permute-start.5 = (bf16[8,392]{1,0:T(8,128)(2,1)S(1)}, bf16[8,392]{1,0:T(8,128)(2,1)S(1)}, u32[]{:S(2)}, u32[]{:S(2)}) collective-permute-start(bf16[8,392]{1,0:T(8,128)(2,1)S(1)} %get-tuple-element.38.refs_0_), channel_id=1, source_target_pairs={{0,3},{1,2},{2,1},{3,0},{4,7},{5,6},{6,5},{7,4},{8,11},{9,10},{10,... | collective-permute-start | bytes 18824 | tf_op jit(solution)/shard_map/ppermute | solution.py:241
  34.4 4.7 %collective-permute-start.4 = (bf16[8,392]{1,0:T(8,128)(2,1)S(1)}, bf16[8,392]{1,0:T(8,128)(2,1)S(1)}, u32[]{:S(2)}, u32[]{:S(2)}) collective-permute-start(bf16[8,392]{1,0:T(8,128)(2,1)S(1)} %get-tuple-element.38.refs_0_), channel_id=1, source_target_pairs={{0,2},{1,3},{2,0},{3,1},{4,6},{5,7},{6,4},{7,5},{8,10},{9,11},{10,... | collective-permute-start | bytes 18824 | tf_op jit(solution)/shard_map/ppermute | solution.py:241
  35.9 3.8 %collective-permute-start.3 = (bf16[8,392]{1,0:T(8,128)(2,1)S(1)}, bf16[8,392]{1,0:T(8,128)(2,1)S(1)}, u32[]{:S(2)}, u32[]{:S(2)}) collective-permute-start(bf16[8,392]{1,0:T(8,128)(2,1)S(1)} %get-tuple-element.38.refs_0_), channel_id=1, source_target_pairs={{0,1},{1,0},{2,3},{3,2},{4,5},{5,4},{6,7},{7,6},{8,9},{9,8},{10,11... | collective-permute-start | bytes 18824 | tf_op jit(solution)/shard_map/ppermute | solution.py:241

commit v8 on v7

--- a/solution.py
+++ b/solution.py
@@ -88,22 +88,22 @@
     return dot(pick.astype(bf16), keys, 1, 0).astype(bf16)
 
 
-def logits_kernel(halves, tokens_ref, keys_in_ref, part_ref, rows_ref, keys_ref, held_ref, held_keys_ref, sems):
+def logits_kernel(halves, tokens_ref, keys_in_ref, grads_ref, part_ref, rows_ref, keys_ref, raw_ref, held_ref, held_keys_ref, sems):
     tokens, images, width = tokens_ref.shape
-    copies = load((tokens_ref, keys_in_ref), (held_ref, held_keys_ref), sems)
+    copies = load((tokens_ref, keys_in_ref, grads_ref), (held_ref, held_keys_ref, raw_ref), sems)
     copies[1].wait()
     keys_ref[...] = in_turn(held_keys_ref[...], halves)
     copies[0].wait()
     rows = held_ref[...].reshape(tokens * images, width)
     rows_ref[...] = rows
     part_ref[...] = dot(keys_ref[...], rows, 1, 1)
-
-
-def prepare_kernel(axis, after_ref, tokens_ref, bout_in_ref, bin_in_ref, wout_in_ref, win_in_ref,
+    copies[2].wait()
+
+
+def prepare_kernel(axis, held_ref, bout_in_ref, bin_in_ref, wout_in_ref, win_in_ref,
                    rows_ref, bout_ref, bin_ref, wout_ref, win_ref, wout_turned_ref, win_turned_ref,
-                   held_ref, held_bout_ref, sems):
-    del after_ref
-    tokens, images, width = tokens_ref.shape
+                   held_bout_ref, sems):
+    tokens, images, width = held_ref.shape
     pieces = []
     for source, target, turned in (
         (wout_in_ref, wout_ref, wout_turned_ref), (win_in_ref, win_ref, win_turned_ref)
@@ -111,24 +111,24 @@
         step = source.shape[0] // weight_pieces
         pieces += [(source, target, turned, pl.ds(k * step, step)) for k in range(weight_pieces)]
     copies = load(
-        (tokens_ref, bout_in_ref, bin_in_ref, *[source.at[part] for source, _, _, part in pieces]),
-        (held_ref, held_bout_ref, bin_ref, *[target.at[part] for _, target, _, part in pieces]),
+        (bout_in_ref, bin_in_ref, *[source.at[part] for source, _, _, part in pieces]),
+        (held_bout_ref, bin_ref, *[target.at[part] for _, target, _, part in pieces]),
         sems,
     )
-    for copy in copies[:3]:
+    for copy in copies[:2]:
         copy.wait()
     rows_ref[...] = held_ref[...].reshape(tokens * images, width)
     own = lax.axis_index(axis)
     for index in range(bout_ref.shape[1] // width):
         bias = jnp.where(own == index, held_bout_ref[...].astype(f32), 0.0)
         bout_ref[:, index * width : (index + 1) * width] = bias
-    for copy, (_, target, turned, part) in zip(copies[3:], pieces):
+    for copy, (_, target, turned, part) in zip(copies[2:], pieces):
         copy.wait()
         turned[:, part] = target[part].T
 
 
 def steps(size, first):
-    return list(range(2, size)) + [1] if first else list(range(1, size))
+    return [1] + list(range(size - 1, 1, -1)) if first else list(range(size - 1, 0, -1))
 
 
 def tree_sum(refs, first):
@@ -256,13 +256,13 @@
     held_shape = pltpu.VMEM(by_token.shape, bf16)
     sent_shape = pltpu.VMEM((groups, hidden, images, 2 * width), bf16)
 
-    part, token_rows, keys = call(
+    part, token_rows, keys, raw = call(
         lambda *refs: logits_kernel(lax.axis_size("expert_c"), *refs),
-        [table, row_shape, pltpu.VMEM((slots, width), bf16)],
+        [table, row_shape, pltpu.VMEM((slots, width), bf16), held_shape],
         (),
         "logits",
-        far=(by_token, jnp.transpose(slot_params)),
-        scratch=[held_shape, pltpu.VMEM((slots, width), bf16), pltpu.SemaphoreType.DMA((2,))],
+        far=(by_token, jnp.transpose(slot_params), grad_by_token),
+        scratch=[held_shape, pltpu.VMEM((slots, width), bf16), pltpu.SemaphoreType.DMA((3,))],
     )
     grad_rows, *expert_values = call(
         lambda *refs: prepare_kernel("hidden", *refs),
@@ -272,13 +272,12 @@
             *[pltpu.VMEM(value.shape, bf16) for value in (bias_in, weight_out, weight_in)],
             *[pltpu.VMEM(value.shape[::-1], bf16) for value in (weight_out, weight_in)],
         ],
-        (part,),
+        (raw,),
         "prepare",
-        far=(grad_by_token, bias_out, bias_in, weight_out, weight_in),
+        far=(bias_out, bias_in, weight_out, weight_in),
         scratch=[
-            held_shape,
             pltpu.VMEM(bias_out.shape, bf16),
-            pltpu.SemaphoreType.DMA((3 + 2 * weight_pieces,)),
+            pltpu.SemaphoreType.DMA((2 + 2 * weight_pieces,)),
         ],
     )
     parts = exchange(part, "hidden", True)

time: 40.9 us -> 40.9 us (level)
  no operation moved by 1% of the time
where the time goes in v8:
time: 40.9 us; the launch traced here: 40.7 us
  blocking collectives  19.6 us (48%)
  starting transfers between devices  10.1 us (25%)
  Pallas kernels  7.62 us (19%)
  waiting for transfers between devices  2.66 us (7%)
  between operations  0.67 us (2%)
    all_to_all x2, blocking collectives, to_all(): lax.all_to_all(value, send_order, split_axis=0, concat_axis=0, tiled=True)  19.6 us
    ppermute x6, starting transfers between devices, exchange(): lax.ppermute(value, axis, [(source, source ^ step) for source in range(si...  10.1 us
    pallas_call x7, Pallas kernels, call(): pl.pallas_call(kernel, out_shape=outs, in_specs=[VMEM] * len(args) + [HBM...  7.62 us
    ppermute x6, waiting for transfers between devices, exchange(): lax.ppermute(value, axis, [(source, source ^ step) for source in range(si...  2.66 us
  transfers between devices with their start and end apart: 6, of which 4 were waited for; matrix products, arithmetic and copies ran while one was open for 0% of the time, Pallas kernels for 9%

profile of v8, /device:TPU:0, one launch (start us, length us, event | category | flops | bytes accessed | tf_op | source)
XLA Modules:
  0.0 40.7 jit_solution(15588076118323486297)
XLA Ops:
  0.6 1.2 %logits.1 = (f32[8,392]{1,0:T(8,128)S(1)}, bf16[392,256]{1,0:T(8,128)(2,1)S(1)}, bf16[8,256]{1,0:T(8,128)(2,1)S(1)}, bf16[196,2,256]{2,1,0:T(2,128)(2,1)S(1)}) custom-call(bf16[196,2,256]{2,1,0:T(2,128)(2,1)} %bitcast.17, bf16[8,256]{1,0:T(8,128)(2,1)} %bitcast.19, bf16[196,2,256]{2,1,0:T(2,128)(2,1)} %bitcast.18), custom_call_target="tpu_custom_call" | custom-call | tf_op jit(solution)/shard_map/logits/pallas_call | solution.py:226
  1.8 3.1 %collective-permute-start = (f32[8,392]{1,0:T(8,128)S(1)}, f32[8,392]{1,0:T(8,128)S(1)}, u32[]{:S(2)}, u32[]{:S(2)}) collective-permute-start(f32[8,392]{1,0:T(8,128)S(1)} %get-tuple-element.27.refs_0_), channel_id=1, source_target_pairs={{0,1},{1,0},{2,3},{3,2},{4,5},{5,4},{6,7},{7,6},{8,9},{9,8},{10,11... | collective-permute-start | bytes 37640 | tf_op jit(solution)/shard_map/ppermute | solution.py:241
  4.9 2.5 %collective-permute-start.1 = (f32[8,392]{1,0:T(8,128)S(1)}, f32[8,392]{1,0:T(8,128)S(1)}, u32[]{:S(2)}, u32[]{:S(2)}) collective-permute-start(f32[8,392]{1,0:T(8,128)S(1)} %get-tuple-element.27.refs_0_), channel_id=1, source_target_pairs={{0,3},{1,2},{2,1},{3,0},{4,7},{5,6},{6,5},{7,4},{8,11},{9,10},{10,... | collective-permute-start | bytes 37640 | tf_op jit(solution)/shard_map/ppermute | solution.py:241
  7.4 0.1 collective-permute-start.2
  7.5 2.7 %prepare.1 = (bf16[392,256]{1,0:T(8,128)(2,1)S(1)}, f32[1,1024]{1,0:T(1,128)S(1)}, bf16[1,1024]{1,0:T(2,128)(2,1)S(1)}, bf16[1024,1024]{1,0:T(8,128)(2,1)S(1)}, ...) custom-call(bf16[196,2,256]{2,1,0:T(2,128)(2,1)S(1)} %get-tuple-element.29.refs_0_, ...), custom_call_target="tpu_custom_call" | custom-call | tf_op jit(solution)/shard_map/prepare/pallas_call | solution.py:226
  10.2 0.0 collective-permute-done.refs_1_
  10.2 0.4 %collective-permute-done.1.refs_2_ = f32[8,392]{1,0:T(8,128)S(1)} collective-permute-done((f32[8,392]{1,0:T(8,128)S(1)}, f32[8,392]{1,0:T(8,128)S(1)}, u32[]{:S(2)}, u32[]{:S(2)}) %collective-permute-start.1) | collective-permute-done | bytes 12576 | tf_op jit(solution)/shard_map/ppermute | solution.py:241
  10.7 1.4 %collective-permute-done.2.refs_3_ = f32[8,392]{1,0:T(8,128)S(1)} collective-permute-done((f32[8,392]{1,0:T(8,128)S(1)}, f32[8,392]{1,0:T(8,128)S(1)}, u32[]{:S(2)}, u32[]{:S(2)}) %collective-permute-start.2) | collective-permute-done | bytes 12576 | tf_op jit(solution)/shard_map/ppermute | solution.py:241
  12.0 0.4 %dispatch.1 = (bf16[8,4,2,512]{3,2,1,0:T(2,128)(2,1)S(1)}, f32[8,392]{1,0:T(8,128)S(1)}, f32[8,392]{1,0:T(8,128)S(1)}, f32[1,392]{1,0:T(1,128)S(1)}) custom-call(f32[8,392]{1,0:T(8,128)S(1)} %get-tuple-element.27.refs_0_, f32[8,392]{1,0:T(8,128)S(1)} %collective-permute-done.refs_1_, f32[8,392]{1,0:T(8,128)S(1)} %collective-permute-done.1.refs_2_, ...), custom_call_target="tpu_custom_call" | custom-call | tf_op jit(solution)/shard_map/dispatch/pallas_call | solution.py:226
  12.5 10.7 %all_to_all.10 = bf16[32,2,512]{2,1,0:T(2,128)(2,1)S(1)} all-to-all(bf16[32,2,512]{2,1,0:T(2,128)(2,1)S(1)} %bitcast.14), channel_id=1, replica_groups=mesh['expert_a'=2,'expert_b'=2,'expert_c'=2,'hidden'=4] {'expert_a','exp..., dimensions={0} | all-to-all | bytes 131072 | tf_op jit(solution)/shard_map/all_to_all | solution.py:293
  23.1 1.2 %expert.1 = bf16[8,4,2,512]{3,2,1,0:T(2,128)(2,1)S(1)} custom-call(bf16[8,4,2,512]{3,2,1,0:T(2,128)(2,1)S(1)} %bitcast.11, f32[1,1024]{1,0:T(1,128)S(1)} %get-tuple-element.32.bout_ref, bf16[1,1024]{1,0:T(2,128)(2,1)S(1)} %get-tuple-element.33.bin_ref, bf16[1024,1024]{1,0:T(8,128)(2,1)S(1)} %get-tuple-element.34.wout_ref, ...), custom_call_target="tpu_custom_call" | custom-call | tf_op jit(solution)/shard_map/expert/pallas_call | solution.py:226
  24.4 9.0 %all_to_all.11 = bf16[32,2,512]{2,1,0:T(2,128)(2,1)S(1)} all-to-all(bf16[32,2,512]{2,1,0:T(2,128)(2,1)S(1)} %bitcast.12), channel_id=1, replica_groups=mesh['expert_a'=2,'expert_b'=2,'expert_c'=2,'hidden'=4] {'expert_a','exp..., dimensions={0} | all-to-all | bytes 131072 | tf_op jit(solution)/shard_map/all_to_all | solution.py:293
  33.3 0.3 gradient.1
  33.7 0.7 %collective-permute-start.3 = (bf16[8,392]{1,0:T(8,128)(2,1)S(1)}, bf16[8,392]{1,0:T(8,128)(2,1)S(1)}, u32[]{:S(2)}, u32[]{:S(2)}) collective-permute-start(bf16[8,392]{1,0:T(8,128)(2,1)S(1)} %get-tuple-element.40.refs_0_), channel_id=1, source_target_pairs={{0,3},{1,2},{2,1},{3,0},{4,7},{5,6},{6,5},{7,4},{8,11},{9,10},{10,... | collective-permute-start | bytes 18824 | tf_op jit(solution)/shard_map/ppermute | solution.py:241
  34.4 1.5 %collective-permute-start.4 = (bf16[8,392]{1,0:T(8,128)(2,1)S(1)}, bf16[8,392]{1,0:T(8,128)(2,1)S(1)}, u32[]{:S(2)}, u32[]{:S(2)}) collective-permute-start(bf16[8,392]{1,0:T(8,128)(2,1)S(1)} %get-tuple-element.40.refs_0_), channel_id=1, source_target_pairs={{0,2},{1,3},{2,0},{3,1},{4,6},{5,7},{6,4},{7,5},{8,10},{9,11},{10,... | collective-permute-start | bytes 18824 | tf_op jit(solution)/shard_map/ppermute | solution.py:241
  35.9 2.2 %collective-permute-start.5 = (bf16[8,392]{1,0:T(8,128)(2,1)S(1)}, bf16[8,392]{1,0:T(8,128)(2,1)S(1)}, u32[]{:S(2)}, u32[]{:S(2)}) collective-permute-start(bf16[8,392]{1,0:T(8,128)(2,1)S(1)} %get-tuple-element.40.refs_0_), channel_id=1, source_target_pairs={{0,1},{1,0},{2,3},{3,2},{4,5},{5,4},{6,7},{7,6},{8,9},{9,8},{10,11... | collective-permute-start | bytes 18824 | tf_op jit(solution)/shard_map/ppermute | solution.py:241
  38.1 0.8 %mixed.1 = (bf16[196,2,256]{2,1,0:T(2,128)(2,1)S(1)}, f32[392,256]{1,0:T(8,128)S(1)}, f32[2,196]{1,0:T(2,128)S(1)}) custom-call(f32[8,392]{1,0:T(8,128)S(1)} %get-tuple-element.38.dispatch_ref, f32[8,392]{1,0:T(8,128)S(1)} %get-tuple-element.39.combine_ref.refs_4_, f32[1,392]{1,0:T(1,128)S(1)} %get-tuple-element.41.total_ref.refs_5_, ...), custom_call_target="tpu_custom_call" | custom-call | tf_op jit(solution)/shard_map/mixed/pallas_call | solution.py:226
  38.8 0.3 collective-permute-done.3.refs_1_
  39.1 0.0 collective-permute-done.4.refs_2_
  39.1 0.6 %collective-permute-done.5.refs_3_ = bf16[8,392]{1,0:T(8,128)(2,1)S(1)} collective-permute-done((bf16[8,392]{1,0:T(8,128)(2,1)S(1)}, bf16[8,392]{1,0:T(8,128)(2,1)S(1)}, u32[]{:S(2)}, u32[]{:S(2)}) %collective-permute-start.5) | collective-permute-done | bytes 6304 | tf_op jit(solution)/shard_map/ppermute | solution.py:241
  39.7 1.0 %token_grad.1 = (bf16[196,2,256]{2,1,0:T(2,128)(2,1)}, bf16[196,2,256]{2,1,0:T(2,128)(2,1)}, f32[2,196]{1,0:T(2,128)}) custom-call(bf16[8,392]{1,0:T(8,128)(2,1)S(1)} %get-tuple-element.40.refs_0_, bf16[8,392]{1,0:T(8,128)(2,1)S(1)} %collective-permute-done.3.refs_1_, bf16[8,392]{1,0:T(8,128)(2,1)S(1)} %collective-permute-done.4.refs_2_, ...), custom_call_target="tpu_custom_call" | custom-call | tf_op jit(solution)/shard_map/token_grad/pallas_call | solution.py:226
Async XLA Ops:
  1.8 8.4 %collective-permute-start = (f32[8,392]{1,0:T(8,128)S(1)}, f32[8,392]{1,0:T(8,128)S(1)}, u32[]{:S(2)}, u32[]{:S(2)}) collective-permute-start(f32[8,392]{1,0:T(8,128)S(1)} %get-tuple-element.27.refs_0_), channel_id=1, source_target_pairs={{0,1},{1,0},{2,3},{3,2},{4,5},{5,4},{6,7},{7,6},{8,9},{9,8},{10,11... | collective-permute-start | bytes 37640 | tf_op jit(solution)/shard_map/ppermute | solution.py:241
  4.9 5.8 %collective-permute-start.1 = (f32[8,392]{1,0:T(8,128)S(1)}, f32[8,392]{1,0:T(8,128)S(1)}, u32[]{:S(2)}, u32[]{:S(2)}) collective-permute-start(f32[8,392]{1,0:T(8,128)S(1)} %get-tuple-element.27.refs_0_), channel_id=1, source_target_pairs={{0,3},{1,2},{2,1},{3,0},{4,7},{5,6},{6,5},{7,4},{8,11},{9,10},{10,... | collective-permute-start | bytes 37640 | tf_op jit(solution)/shard_map/ppermute | solution.py:241
  7.4 4.6 %collective-permute-start.2 = (f32[8,392]{1,0:T(8,128)S(1)}, f32[8,392]{1,0:T(8,128)S(1)}, u32[]{:S(2)}, u32[]{:S(2)}) collective-permute-start(f32[8,392]{1,0:T(8,128)S(1)} %get-tuple-element.27.refs_0_), channel_id=1, source_target_pairs={{0,2},{1,3},{2,0},{3,1},{4,6},{5,7},{6,4},{7,5},{8,10},{9,11},{10,... | collective-permute-start | bytes 37640 | tf_op jit(solution)/shard_map/ppermute | solution.py:241
  33.7 5.5 %collective-permute-start.3 = (bf16[8,392]{1,0:T(8,128)(2,1)S(1)}, bf16[8,392]{1,0:T(8,128)(2,1)S(1)}, u32[]{:S(2)}, u32[]{:S(2)}) collective-permute-start(bf16[8,392]{1,0:T(8,128)(2,1)S(1)} %get-tuple-element.40.refs_0_), channel_id=1, source_target_pairs={{0,3},{1,2},{2,1},{3,0},{4,7},{5,6},{6,5},{7,4},{8,11},{9,10},{10,... | collective-permute-start | bytes 18824 | tf_op jit(solution)/shard_map/ppermute | solution.py:241
  34.4 4.7 %collective-permute-start.4 = (bf16[8,392]{1,0:T(8,128)(2,1)S(1)}, bf16[8,392]{1,0:T(8,128)(2,1)S(1)}, u32[]{:S(2)}, u32[]{:S(2)}) collective-permute-start(bf16[8,392]{1,0:T(8,128)(2,1)S(1)} %get-tuple-element.40.refs_0_), channel_id=1, source_target_pairs={{0,2},{1,3},{2,0},{3,1},{4,6},{5,7},{6,4},{7,5},{8,10},{9,11},{10,... | collective-permute-start | bytes 18824 | tf_op jit(solution)/shard_map/ppermute | solution.py:241
  35.9 3.8 %collective-permute-start.5 = (bf16[8,392]{1,0:T(8,128)(2,1)S(1)}, bf16[8,392]{1,0:T(8,128)(2,1)S(1)}, u32[]{:S(2)}, u32[]{:S(2)}) collective-permute-start(bf16[8,392]{1,0:T(8,128)(2,1)S(1)} %get-tuple-element.40.refs_0_), channel_id=1, source_target_pairs={{0,1},{1,0},{2,3},{3,2},{4,5},{5,4},{6,7},{7,6},{8,9},{9,8},{10,11... | collective-permute-start | bytes 18824 | tf_op jit(solution)/shard_map/ppermute | solution.py:241

commit v9 on v7

--- a/solution.py
+++ b/solution.py
@@ -140,13 +140,13 @@
 
 
 def dispatch_kernel(images, count, *refs):
-    parts, (rows_ref, grads_ref, sent_ref, dispatch_ref, combine_ref, total_ref) = refs[:count], refs[count:]
+    parts, (rows_ref, grads_ref, sent_ref, dispatch_ref, combine_ref, norm_ref) = refs[:count], refs[count:]
     logits = tree_sum(parts, True)
     top = jnp.max(logits, axis=0, keepdims=True)
     powers = jnp.exp(logits - top)
     sums = jnp.sum(powers, axis=0, keepdims=True)
     combine = powers / sums
-    total_ref[...] = top + jnp.log(sums)
+    norm_ref[0:1], norm_ref[1:2] = top, sums
     powers = jnp.exp(logits - by_image(logits, images, jnp.max, -jnp.inf))
     dispatch = powers / by_image(powers, images, jnp.sum, 0.0)
     combine_ref[...] = combine
@@ -193,11 +193,16 @@
     part_ref[...] = part.astype(bf16)
 
 
-def mixed_kernel(dispatch_ref, combine_ref, total_ref, out_ref, back_ref, mixed_ref, direct_ref, loss_ref):
+def mixed_kernel(dispatch_ref, combine_ref, norm_ref, keys_ref, out_ref, back_ref,
+                 mixed_out_ref, loss_out_ref, direct_ref, mixed_ref, loss_ref, sems):
     images = loss_ref.shape[0]
     mixed_ref[...] = dot(spread(combine_ref[...], images), out_ref[...], 0, 0).astype(bf16).reshape(mixed_ref.shape)
-    direct_ref[...] = dot(spread(dispatch_ref[...], images), back_ref[...], 0, 0)
-    total = jnp.broadcast_to(total_ref[...], (8, total_ref.shape[1]))
+    copies = load((mixed_ref,), (mixed_out_ref,), sems)
+    total = norm_ref[0:1] + jnp.log(norm_ref[1:2])
+    known = 2.0 * loss_weight * total * combine_ref[...]
+    direct = dot(spread(dispatch_ref[...], images), back_ref[...], 0, 0)
+    direct_ref[...] = direct + dot(known.astype(bf16), keys_ref[...], 0, 0)
+    total = jnp.broadcast_to(total, (8, total.shape[1]))
     tokens = loss_ref.shape[1]
     row, token = iota((images * tokens, tokens), 0), iota((images * tokens, tokens), 1)
     for index in range(images):
@@ -206,28 +211,29 @@
             total, pick, (((1,), (0,)), ((), ())), precision=lax.Precision.HIGHEST, preferred_element_type=f32
         )[:1]
         loss_ref[index : index + 1] = loss_weight * own * own
-
-
-def token_kernel(count, *refs):
-    parts, refs = refs[:count], refs[count:]
-    (combine_ref, total_ref, keys_ref, direct_ref, mixed_ref, loss_ref) = refs[:6]
-    (out_ref, mixed_out_ref, loss_out_ref, held_ref, sems) = refs[6:]
-    copies = load((mixed_ref, loss_ref), (mixed_out_ref, loss_out_ref), sems)
-    logit_grad = tree_sum(parts, False) + 2.0 * loss_weight * total_ref[...] * combine_ref[...]
-    out = dot(logit_grad.astype(bf16), keys_ref[...], 0, 0) + direct_ref[...]
-    held_ref[...] = out.astype(bf16).reshape(held_ref.shape)
-    last = pltpu.make_async_copy(held_ref, out_ref, sems.at[2])
+    last = pltpu.make_async_copy(loss_ref, loss_out_ref, sems.at[1])
     last.start()
     for copy in (*copies, last):
         copy.wait()
 
 
-def call(kernel, outs, args, name, limit=8, far=(), far_outs=False, scratch=(), cost=None):
+def token_kernel(count, *refs):
+    parts, refs = refs[:count], refs[count:]
+    keys_ref, direct_ref, out_ref, held_ref, sem = refs
+    logit_grad = tree_sum(parts, False)
+    out = dot(logit_grad.astype(bf16), keys_ref[...], 0, 0) + direct_ref[...]
+    held_ref[...] = out.astype(bf16).reshape(held_ref.shape)
+    copy = pltpu.make_async_copy(held_ref, out_ref, sem)
+    copy.start()
+    copy.wait()
+
+
+def call(kernel, outs, args, name, limit=8, far=(), far_outs=0, scratch=(), cost=None):
     return pl.pallas_call(
         kernel,
         out_shape=outs,
         in_specs=[VMEM] * len(args) + [HBM] * len(far),
-        out_specs=[HBM if far_outs else VMEM] * len(outs),
+        out_specs=[HBM] * far_outs + [VMEM] * (len(outs) - far_outs),
         scratch_shapes=scratch,
         compiler_params=pltpu.CompilerParams(vmem_limit_bytes=limit * MIB),
         cost_estimate=cost,
@@ -284,7 +290,7 @@
     parts = exchange(part, "hidden", True)
     sent, dispatch, combine, total = call(
         lambda *refs: dispatch_kernel(images, hidden, *refs),
-        [sent_shape, table, table, pltpu.VMEM((1, rows), f32)],
+        [sent_shape, table, table, pltpu.VMEM((2, rows), f32)],
         (*parts, token_rows, grad_rows),
         "dispatch",
     )
@@ -308,20 +314,22 @@
         "gradient",
     )
     parts = exchange(part, "hidden", False)
-    mixed, direct, zloss = call(
+    out_shape, loss_shape = jax.ShapeDtypeStruct(by_token.shape, bf16), (images, count)
+    mixed, zloss, direct = call(
         mixed_kernel,
-        [held_shape, pltpu.VMEM((rows, width), f32), pltpu.VMEM((images, count), f32)],
-        (dispatch, combine, total, slot_out, in_grad),
+        [out_shape, jax.ShapeDtypeStruct(loss_shape, f32), pltpu.VMEM((rows, width), f32)],
+        (dispatch, combine, total, keys, slot_out, in_grad),
         "mixed",
-    )
-    out_shape = jax.ShapeDtypeStruct(by_token.shape, bf16)
-    token_grad, mixed, zloss = call(
+        far_outs=2,
+        scratch=[held_shape, pltpu.VMEM(loss_shape, f32), pltpu.SemaphoreType.DMA((2,))],
+    )
+    (token_grad,) = call(
         lambda *refs: token_kernel(hidden, *refs),
-        [out_shape, out_shape, jax.ShapeDtypeStruct((images, count), f32)],
-        (*parts, combine, total, keys, direct, mixed, zloss),
+        [out_shape],
+        (*parts, keys, direct),
         "token_grad",
-        far_outs=True,
-        scratch=[held_shape, pltpu.SemaphoreType.DMA((3,))],
+        far_outs=1,
+        scratch=[held_shape, pltpu.SemaphoreType.DMA],
     )
     return (jnp.transpose(mixed, (1, 0, 2)), jnp.transpose(token_grad, (1, 0, 2)), zloss)
 

time: 40.9 us -> 40.8 us (level)
  waiting for transfers between devices: 2.53 us -> 1.87 us
  Pallas kernels: 7.73 us -> 8.35 us
    ppermute x6, waiting for transfers between devices: 2.53 us -> 1.87 us  [exchange(): lax.ppermute(value, axis, [(source, source ^ step) for source in range(si...]
    pallas_call x7, Pallas kernels: 7.73 us -> 8.35 us  [call(): pl.pallas_call(kernel, out_shape=outs, in_specs=[VMEM] * len(args) + [HBM...]
  transfers between devices with their start and end apart: 6 -> 6, of which waited for: 4 -> 3; matrix products, arithmetic and copies ran while one was open for 0% -> 0% of each run, Pallas kernels for 9% -> 10%
where the time goes in v9:
time: 40.8 us; the launch traced here: 40.6 us
  blocking collectives  19.6 us (48%)
  starting transfers between devices  10.1 us (25%)
  Pallas kernels  8.35 us (20%)
  waiting for transfers between devices  1.87 us (5%)
  between operations  0.69 us (2%)
    all_to_all x2, blocking collectives, to_all(): lax.all_to_all(value, send_order, split_axis=0, concat_axis=0, tiled=True)  19.6 us
    ppermute x6, starting transfers between devices, exchange(): lax.ppermute(value, axis, [(source, source ^ step) for source in range(si...  10.1 us
    pallas_call x7, Pallas kernels, call(): pl.pallas_call(kernel, out_shape=outs, in_specs=[VMEM] * len(args) + [HBM...  8.35 us
    ppermute x6, waiting for transfers between devices, exchange(): lax.ppermute(value, axis, [(source, source ^ step) for source in range(si...  1.87 us
  transfers between devices with their start and end apart: 6, of which 3 were waited for; matrix products, arithmetic and copies ran while one was open for 0% of the time, Pallas kernels for 10%

profile of v9, /device:TPU:0, one launch (start us, length us, event | category | flops | bytes accessed | tf_op | source)
XLA Modules:
  0.0 40.6 jit_solution(4318719425648444080)
XLA Ops:
  0.6 1.2 %logits.1 = (f32[8,392]{1,0:T(8,128)S(1)}, bf16[392,256]{1,0:T(8,128)(2,1)S(1)}, bf16[8,256]{1,0:T(8,128)(2,1)S(1)}) custom-call(bf16[196,2,256]{2,1,0:T(2,128)(2,1)} %bitcast.19, bf16[8,256]{1,0:T(8,128)(2,1)} %bitcast.20), custom_call_target="tpu_custom_call" | custom-call | tf_op jit(solution)/shard_map/logits/pallas_call | solution.py:232
  1.8 3.1 %collective-permute-start.2 = (f32[8,392]{1,0:T(8,128)S(1)}, f32[8,392]{1,0:T(8,128)S(1)}, u32[]{:S(2)}, u32[]{:S(2)}) collective-permute-start(f32[8,392]{1,0:T(8,128)S(1)} %get-tuple-element.23.refs_0_), channel_id=1, source_target_pairs={{0,1},{1,0},{2,3},{3,2},{4,5},{5,4},{6,7},{7,6},{8,9},{9,8},{10,11... | collective-permute-start | bytes 37640 | tf_op jit(solution)/shard_map/ppermute | solution.py:247
  4.9 2.5 %collective-permute-start.1 = (f32[8,392]{1,0:T(8,128)S(1)}, f32[8,392]{1,0:T(8,128)S(1)}, u32[]{:S(2)}, u32[]{:S(2)}) collective-permute-start(f32[8,392]{1,0:T(8,128)S(1)} %get-tuple-element.23.refs_0_), channel_id=1, source_target_pairs={{0,3},{1,2},{2,1},{3,0},{4,7},{5,6},{6,5},{7,4},{8,11},{9,10},{10,... | collective-permute-start | bytes 37640 | tf_op jit(solution)/shard_map/ppermute | solution.py:247
  7.4 0.1 collective-permute-start
  7.5 2.8 %prepare.1 = (bf16[392,256]{1,0:T(8,128)(2,1)S(1)}, f32[1,1024]{1,0:T(1,128)S(1)}, bf16[1,1024]{1,0:T(2,128)(2,1)S(1)}, bf16[1024,1024]{1,0:T(8,128)(2,1)S(1)}, ...) custom-call(f32[8,392]{1,0:T(8,128)S(1)} %get-tuple-element.23.refs_0_, ...), custom_call_target="tpu_custom_call" | custom-call | tf_op jit(solution)/shard_map/prepare/pallas_call | solution.py:232
  10.3 0.0 collective-permute-done.2.refs_3_
  10.3 0.3 collective-permute-done.1.refs_2_
  10.7 1.4 %collective-permute-done.refs_1_ = f32[8,392]{1,0:T(8,128)S(1)} collective-permute-done((f32[8,392]{1,0:T(8,128)S(1)}, f32[8,392]{1,0:T(8,128)S(1)}, u32[]{:S(2)}, u32[]{:S(2)}) %collective-permute-start) | collective-permute-done | bytes 12576 | tf_op jit(solution)/shard_map/ppermute | solution.py:247
  12.0 0.4 %dispatch.1 = (bf16[8,4,2,512]{3,2,1,0:T(2,128)(2,1)S(1)}, f32[8,392]{1,0:T(8,128)S(1)}, f32[8,392]{1,0:T(8,128)S(1)}, f32[2,392]{1,0:T(2,128)S(1)}) custom-call(f32[8,392]{1,0:T(8,128)S(1)} %get-tuple-element.23.refs_0_, f32[8,392]{1,0:T(8,128)S(1)} %collective-permute-done.refs_1_, f32[8,392]{1,0:T(8,128)S(1)} %collective-permute-done.1.refs_2_, ...), custom_call_target="tpu_custom_call" | custom-call | tf_op jit(solution)/shard_map/dispatch/pallas_call | solution.py:232
  12.5 10.7 %all_to_all.10 = bf16[32,2,512]{2,1,0:T(2,128)(2,1)S(1)} all-to-all(bf16[32,2,512]{2,1,0:T(2,128)(2,1)S(1)} %bitcast.14), channel_id=1, replica_groups=mesh['expert_a'=2,'expert_b'=2,'expert_c'=2,'hidden'=4] {'expert_a','exp..., dimensions={0} | all-to-all | bytes 131072 | tf_op jit(solution)/shard_map/all_to_all | solution.py:300
  23.1 1.2 %expert.1 = bf16[8,4,2,512]{3,2,1,0:T(2,128)(2,1)S(1)} custom-call(bf16[8,4,2,512]{3,2,1,0:T(2,128)(2,1)S(1)} %bitcast.11, f32[1,1024]{1,0:T(1,128)S(1)} %get-tuple-element.31.bout_ref, bf16[1,1024]{1,0:T(2,128)(2,1)S(1)} %get-tuple-element.32.bin_ref, bf16[1024,1024]{1,0:T(8,128)(2,1)S(1)} %get-tuple-element.33.wout_ref, ...), custom_call_target="tpu_custom_call" | custom-call | tf_op jit(solution)/shard_map/expert/pallas_call | solution.py:232
  24.3 9.0 %all_to_all.11 = bf16[32,2,512]{2,1,0:T(2,128)(2,1)S(1)} all-to-all(bf16[32,2,512]{2,1,0:T(2,128)(2,1)S(1)} %bitcast.12), channel_id=1, replica_groups=mesh['expert_a'=2,'expert_b'=2,'expert_c'=2,'hidden'=4] {'expert_a','exp..., dimensions={0} | all-to-all | bytes 131072 | tf_op jit(solution)/shard_map/all_to_all | solution.py:300
  33.3 0.3 gradient.1
  33.7 0.7 %collective-permute-start.5 = (bf16[8,392]{1,0:T(8,128)(2,1)S(1)}, bf16[8,392]{1,0:T(8,128)(2,1)S(1)}, u32[]{:S(2)}, u32[]{:S(2)}) collective-permute-start(bf16[8,392]{1,0:T(8,128)(2,1)S(1)} %get-tuple-element.40.refs_0_), channel_id=1, source_target_pairs={{0,3},{1,2},{2,1},{3,0},{4,7},{5,6},{6,5},{7,4},{8,11},{9,10},{10,... | collective-permute-start | bytes 18824 | tf_op jit(solution)/shard_map/ppermute | solution.py:247
  34.4 1.5 %collective-permute-start.4 = (bf16[8,392]{1,0:T(8,128)(2,1)S(1)}, bf16[8,392]{1,0:T(8,128)(2,1)S(1)}, u32[]{:S(2)}, u32[]{:S(2)}) collective-permute-start(bf16[8,392]{1,0:T(8,128)(2,1)S(1)} %get-tuple-element.40.refs_0_), channel_id=1, source_target_pairs={{0,2},{1,3},{2,0},{3,1},{4,6},{5,7},{6,4},{7,5},{8,10},{9,11},{10,... | collective-permute-start | bytes 18824 | tf_op jit(solution)/shard_map/ppermute | solution.py:247
  35.9 2.2 %collective-permute-start.3 = (bf16[8,392]{1,0:T(8,128)(2,1)S(1)}, bf16[8,392]{1,0:T(8,128)(2,1)S(1)}, u32[]{:S(2)}, u32[]{:S(2)}) collective-permute-start(bf16[8,392]{1,0:T(8,128)(2,1)S(1)} %get-tuple-element.40.refs_0_), channel_id=1, source_target_pairs={{0,1},{1,0},{2,3},{3,2},{4,5},{5,4},{6,7},{7,6},{8,9},{9,8},{10,11... | collective-permute-start | bytes 18824 | tf_op jit(solution)/shard_map/ppermute | solution.py:247
  38.0 1.4 %mixed.1 = (bf16[196,2,256]{2,1,0:T(2,128)(2,1)}, f32[2,196]{1,0:T(2,128)}, f32[392,256]{1,0:T(8,128)S(1)}) custom-call(f32[8,392]{1,0:T(8,128)S(1)} %get-tuple-element.26.dispatch_ref, f32[8,392]{1,0:T(8,128)S(1)} %get-tuple-element.27.combine_ref, f32[2,392]{1,0:T(2,128)S(1)} %get-tuple-element.28.norm_ref, ...), custom_call_target="tpu_custom_call" | custom-call | tf_op jit(solution)/shard_map/mixed/pallas_call | solution.py:232
  39.5 0.0 collective-permute-done.5.refs_3_
  39.5 0.0 collective-permute-done.4.refs_2_
  39.5 0.2 collective-permute-done.3.refs_1_
  39.7 0.9 %token_grad.1 = bf16[196,2,256]{2,1,0:T(2,128)(2,1)} custom-call(bf16[8,392]{1,0:T(8,128)(2,1)S(1)} %get-tuple-element.40.refs_0_, bf16[8,392]{1,0:T(8,128)(2,1)S(1)} %collective-permute-done.3.refs_1_, bf16[8,392]{1,0:T(8,128)(2,1)S(1)} %collective-permute-done.4.refs_2_, bf16[8,392]{1,0:T(8,128)(2,1)S(1)} %collective-permute-done.5.refs_3_, ...), custom_call_target="tpu_custom_call" | custom-call | tf_op jit(solution)/shard_map/token_grad/pallas_call | solution.py:232
Async XLA Ops:
  1.8 8.5 %collective-permute-start.2 = (f32[8,392]{1,0:T(8,128)S(1)}, f32[8,392]{1,0:T(8,128)S(1)}, u32[]{:S(2)}, u32[]{:S(2)}) collective-permute-start(f32[8,392]{1,0:T(8,128)S(1)} %get-tuple-element.23.refs_0_), channel_id=1, source_target_pairs={{0,1},{1,0},{2,3},{3,2},{4,5},{5,4},{6,7},{7,6},{8,9},{9,8},{10,11... | collective-permute-start | bytes 37640 | tf_op jit(solution)/shard_map/ppermute | solution.py:247
  4.9 5.8 %collective-permute-start.1 = (f32[8,392]{1,0:T(8,128)S(1)}, f32[8,392]{1,0:T(8,128)S(1)}, u32[]{:S(2)}, u32[]{:S(2)}) collective-permute-start(f32[8,392]{1,0:T(8,128)S(1)} %get-tuple-element.23.refs_0_), channel_id=1, source_target_pairs={{0,3},{1,2},{2,1},{3,0},{4,7},{5,6},{6,5},{7,4},{8,11},{9,10},{10,... | collective-permute-start | bytes 37640 | tf_op jit(solution)/shard_map/ppermute | solution.py:247
  7.4 4.6 %collective-permute-start = (f32[8,392]{1,0:T(8,128)S(1)}, f32[8,392]{1,0:T(8,128)S(1)}, u32[]{:S(2)}, u32[]{:S(2)}) collective-permute-start(f32[8,392]{1,0:T(8,128)S(1)} %get-tuple-element.23.refs_0_), channel_id=1, source_target_pairs={{0,2},{1,3},{2,0},{3,1},{4,6},{5,7},{6,4},{7,5},{8,10},{9,11},{10,... | collective-permute-start | bytes 37640 | tf_op jit(solution)/shard_map/ppermute | solution.py:247
  33.7 5.8 %collective-permute-start.5 = (bf16[8,392]{1,0:T(8,128)(2,1)S(1)}, bf16[8,392]{1,0:T(8,128)(2,1)S(1)}, u32[]{:S(2)}, u32[]{:S(2)}) collective-permute-start(bf16[8,392]{1,0:T(8,128)(2,1)S(1)} %get-tuple-element.40.refs_0_), channel_id=1, source_target_pairs={{0,3},{1,2},{2,1},{3,0},{4,7},{5,6},{6,5},{7,4},{8,11},{9,10},{10,... | collective-permute-start | bytes 18824 | tf_op jit(solution)/shard_map/ppermute | solution.py:247
  34.4 5.1 %collective-permute-start.4 = (bf16[8,392]{1,0:T(8,128)(2,1)S(1)}, bf16[8,392]{1,0:T(8,128)(2,1)S(1)}, u32[]{:S(2)}, u32[]{:S(2)}) collective-permute-start(bf16[8,392]{1,0:T(8,128)(2,1)S(1)} %get-tuple-element.40.refs_0_), channel_id=1, source_target_pairs={{0,2},{1,3},{2,0},{3,1},{4,6},{5,7},{6,4},{7,5},{8,10},{9,11},{10,... | collective-permute-start | bytes 18824 | tf_op jit(solution)/shard_map/ppermute | solution.py:247
  35.9 3.8 %collective-permute-start.3 = (bf16[8,392]{1,0:T(8,128)(2,1)S(1)}, bf16[8,392]{1,0:T(8,128)(2,1)S(1)}, u32[]{:S(2)}, u32[]{:S(2)}) collective-permute-start(bf16[8,392]{1,0:T(8,128)(2,1)S(1)} %get-tuple-element.40.refs_0_), channel_id=1, source_target_pairs={{0,1},{1,0},{2,3},{3,2},{4,5},{5,4},{6,7},{7,6},{8,9},{9,8},{10,11... | collective-permute-start | bytes 18824 | tf_op jit(solution)/shard_map/ppermute | solution.py:247

commit v10 on v7

--- a/solution.py
+++ b/solution.py
@@ -12,7 +12,7 @@
 MIB = 1024 * 1024
 expert = ("expert_a", "expert_b", "expert_c")
 send_order = ("expert_a", "expert_c", "expert_b", "hidden")
-weight_pieces = 2
+weight_pieces = 4
 
 
 def gelu_parts(value):

time: 40.9 us -> 40.9 us (level)
  no operation moved by 1% of the time
where the time goes in v10:
time: 40.9 us; the launch traced here: 40.6 us
  blocking collectives  19.6 us (48%)
  starting transfers between devices  10.1 us (25%)
  Pallas kernels  7.8 us (19%)
  waiting for transfers between devices  2.47 us (6%)
  between operations  0.67 us (2%)
    all_to_all x2, blocking collectives, to_all(): lax.all_to_all(value, send_order, split_axis=0, concat_axis=0, tiled=True)  19.6 us
    ppermute x6, starting transfers between devices, exchange(): lax.ppermute(value, axis, [(source, source ^ step) for source in range(si...  10.1 us
    pallas_call x7, Pallas kernels, call(): pl.pallas_call(kernel, out_shape=outs, in_specs=[VMEM] * len(args) + [HBM...  7.8 us
    ppermute x6, waiting for transfers between devices, exchange(): lax.ppermute(value, axis, [(source, source ^ step) for source in range(si...  2.47 us
  transfers between devices with their start and end apart: 6, of which 4 were waited for; matrix products, arithmetic and copies ran while one was open for 0% of the time, Pallas kernels for 9%

profile of v10, /device:TPU:0, one launch (start us, length us, event | category | flops | bytes accessed | tf_op | source)
XLA Modules:
  0.0 40.6 jit_solution(2110778152181278781)
XLA Ops:
  0.6 1.2 %logits.1 = (f32[8,392]{1,0:T(8,128)S(1)}, bf16[392,256]{1,0:T(8,128)(2,1)S(1)}, bf16[8,256]{1,0:T(8,128)(2,1)S(1)}) custom-call(bf16[196,2,256]{2,1,0:T(2,128)(2,1)} %bitcast.18, bf16[8,256]{1,0:T(8,128)(2,1)} %bitcast.19), custom_call_target="tpu_custom_call" | custom-call | tf_op jit(solution)/shard_map/logits/pallas_call | solution.py:226
  1.8 3.1 %collective-permute-start.2 = (f32[8,392]{1,0:T(8,128)S(1)}, f32[8,392]{1,0:T(8,128)S(1)}, u32[]{:S(2)}, u32[]{:S(2)}) collective-permute-start(f32[8,392]{1,0:T(8,128)S(1)} %get-tuple-element.26.refs_0_), channel_id=1, source_target_pairs={{0,1},{1,0},{2,3},{3,2},{4,5},{5,4},{6,7},{7,6},{8,9},{9,8},{10,11... | collective-permute-start | bytes 37640 | tf_op jit(solution)/shard_map/ppermute | solution.py:241
  4.9 2.5 %collective-permute-start.1 = (f32[8,392]{1,0:T(8,128)S(1)}, f32[8,392]{1,0:T(8,128)S(1)}, u32[]{:S(2)}, u32[]{:S(2)}) collective-permute-start(f32[8,392]{1,0:T(8,128)S(1)} %get-tuple-element.26.refs_0_), channel_id=1, source_target_pairs={{0,3},{1,2},{2,1},{3,0},{4,7},{5,6},{6,5},{7,4},{8,11},{9,10},{10,... | collective-permute-start | bytes 37640 | tf_op jit(solution)/shard_map/ppermute | solution.py:241
  7.4 0.1 collective-permute-start
  7.5 2.9 %prepare.1 = (bf16[392,256]{1,0:T(8,128)(2,1)S(1)}, f32[1,1024]{1,0:T(1,128)S(1)}, bf16[1,1024]{1,0:T(2,128)(2,1)S(1)}, bf16[1024,1024]{1,0:T(8,128)(2,1)S(1)}, ...) custom-call(f32[8,392]{1,0:T(8,128)S(1)} %get-tuple-element.26.refs_0_, ...), custom_call_target="tpu_custom_call" | custom-call | tf_op jit(solution)/shard_map/prepare/pallas_call | solution.py:226
  10.4 0.0 collective-permute-done.2.refs_3_
  10.4 0.3 collective-permute-done.1.refs_2_
  10.7 1.4 %collective-permute-done.refs_1_ = f32[8,392]{1,0:T(8,128)S(1)} collective-permute-done((f32[8,392]{1,0:T(8,128)S(1)}, f32[8,392]{1,0:T(8,128)S(1)}, u32[]{:S(2)}, u32[]{:S(2)}) %collective-permute-start) | collective-permute-done | bytes 12576 | tf_op jit(solution)/shard_map/ppermute | solution.py:241
  12.0 0.4 %dispatch.1 = (bf16[8,4,2,512]{3,2,1,0:T(2,128)(2,1)S(1)}, f32[8,392]{1,0:T(8,128)S(1)}, f32[8,392]{1,0:T(8,128)S(1)}, f32[1,392]{1,0:T(1,128)S(1)}) custom-call(f32[8,392]{1,0:T(8,128)S(1)} %get-tuple-element.26.refs_0_, f32[8,392]{1,0:T(8,128)S(1)} %collective-permute-done.refs_1_, f32[8,392]{1,0:T(8,128)S(1)} %collective-permute-done.1.refs_2_, ...), custom_call_target="tpu_custom_call" | custom-call | tf_op jit(solution)/shard_map/dispatch/pallas_call | solution.py:226
  12.5 10.7 %all_to_all.10 = bf16[32,2,512]{2,1,0:T(2,128)(2,1)S(1)} all-to-all(bf16[32,2,512]{2,1,0:T(2,128)(2,1)S(1)} %bitcast.14), channel_id=1, replica_groups=mesh['expert_a'=2,'expert_b'=2,'expert_c'=2,'hidden'=4] {'expert_a','exp..., dimensions={0} | all-to-all | bytes 131072 | tf_op jit(solution)/shard_map/all_to_all | solution.py:294
  23.1 1.2 %expert.1 = bf16[8,4,2,512]{3,2,1,0:T(2,128)(2,1)S(1)} custom-call(bf16[8,4,2,512]{3,2,1,0:T(2,128)(2,1)S(1)} %bitcast.11, f32[1,1024]{1,0:T(1,128)S(1)} %get-tuple-element.30.bout_ref, bf16[1,1024]{1,0:T(2,128)(2,1)S(1)} %get-tuple-element.31.bin_ref, bf16[1024,1024]{1,0:T(8,128)(2,1)S(1)} %get-tuple-element.32.wout_ref, ...), custom_call_target="tpu_custom_call" | custom-call | tf_op jit(solution)/shard_map/expert/pallas_call | solution.py:226
  24.3 9.0 %all_to_all.11 = bf16[32,2,512]{2,1,0:T(2,128)(2,1)S(1)} all-to-all(bf16[32,2,512]{2,1,0:T(2,128)(2,1)S(1)} %bitcast.12), channel_id=1, replica_groups=mesh['expert_a'=2,'expert_b'=2,'expert_c'=2,'hidden'=4] {'expert_a','exp..., dimensions={0} | all-to-all | bytes 131072 | tf_op jit(solution)/shard_map/all_to_all | solution.py:294
  33.3 0.3 gradient.1
  33.7 0.7 %collective-permute-start.5 = (bf16[8,392]{1,0:T(8,128)(2,1)S(1)}, bf16[8,392]{1,0:T(8,128)(2,1)S(1)}, u32[]{:S(2)}, u32[]{:S(2)}) collective-permute-start(bf16[8,392]{1,0:T(8,128)(2,1)S(1)} %get-tuple-element.38.refs_0_), channel_id=1, source_target_pairs={{0,3},{1,2},{2,1},{3,0},{4,7},{5,6},{6,5},{7,4},{8,11},{9,10},{10,... | collective-permute-start | bytes 18824 | tf_op jit(solution)/shard_map/ppermute | solution.py:241
  34.4 1.5 %collective-permute-start.4 = (bf16[8,392]{1,0:T(8,128)(2,1)S(1)}, bf16[8,392]{1,0:T(8,128)(2,1)S(1)}, u32[]{:S(2)}, u32[]{:S(2)}) collective-permute-start(bf16[8,392]{1,0:T(8,128)(2,1)S(1)} %get-tuple-element.38.refs_0_), channel_id=1, source_target_pairs={{0,2},{1,3},{2,0},{3,1},{4,6},{5,7},{6,4},{7,5},{8,10},{9,11},{10,... | collective-permute-start | bytes 18824 | tf_op jit(solution)/shard_map/ppermute | solution.py:241
  35.9 2.2 %collective-permute-start.3 = (bf16[8,392]{1,0:T(8,128)(2,1)S(1)}, bf16[8,392]{1,0:T(8,128)(2,1)S(1)}, u32[]{:S(2)}, u32[]{:S(2)}) collective-permute-start(bf16[8,392]{1,0:T(8,128)(2,1)S(1)} %get-tuple-element.38.refs_0_), channel_id=1, source_target_pairs={{0,1},{1,0},{2,3},{3,2},{4,5},{5,4},{6,7},{7,6},{8,9},{9,8},{10,11... | collective-permute-start | bytes 18824 | tf_op jit(solution)/shard_map/ppermute | solution.py:241
  38.0 0.8 %mixed.1 = (bf16[196,2,256]{2,1,0:T(2,128)(2,1)S(1)}, f32[392,256]{1,0:T(8,128)S(1)}, f32[2,196]{1,0:T(2,128)S(1)}) custom-call(f32[8,392]{1,0:T(8,128)S(1)} %get-tuple-element.36.dispatch_ref, f32[8,392]{1,0:T(8,128)S(1)} %get-tuple-element.37.combine_ref.refs_4_, f32[1,392]{1,0:T(1,128)S(1)} %get-tuple-element.39.total_ref.refs_5_, ...), custom_call_target="tpu_custom_call" | custom-call | tf_op jit(solution)/shard_map/mixed/pallas_call | solution.py:226
  38.8 0.3 collective-permute-done.5.refs_3_
  39.1 0.0 collective-permute-done.4.refs_2_
  39.1 0.6 %collective-permute-done.3.refs_1_ = bf16[8,392]{1,0:T(8,128)(2,1)S(1)} collective-permute-done((bf16[8,392]{1,0:T(8,128)(2,1)S(1)}, bf16[8,392]{1,0:T(8,128)(2,1)S(1)}, u32[]{:S(2)}, u32[]{:S(2)}) %collective-permute-start.3) | collective-permute-done | bytes 6304 | tf_op jit(solution)/shard_map/ppermute | solution.py:241
  39.7 1.0 %token_grad.1 = (bf16[196,2,256]{2,1,0:T(2,128)(2,1)}, bf16[196,2,256]{2,1,0:T(2,128)(2,1)}, f32[2,196]{1,0:T(2,128)}) custom-call(bf16[8,392]{1,0:T(8,128)(2,1)S(1)} %get-tuple-element.38.refs_0_, bf16[8,392]{1,0:T(8,128)(2,1)S(1)} %collective-permute-done.3.refs_1_, bf16[8,392]{1,0:T(8,128)(2,1)S(1)} %collective-permute-done.4.refs_2_, ...), custom_call_target="tpu_custom_call" | custom-call | tf_op jit(solution)/shard_map/token_grad/pallas_call | solution.py:226
Async XLA Ops:
  1.8 8.6 %collective-permute-start.2 = (f32[8,392]{1,0:T(8,128)S(1)}, f32[8,392]{1,0:T(8,128)S(1)}, u32[]{:S(2)}, u32[]{:S(2)}) collective-permute-start(f32[8,392]{1,0:T(8,128)S(1)} %get-tuple-element.26.refs_0_), channel_id=1, source_target_pairs={{0,1},{1,0},{2,3},{3,2},{4,5},{5,4},{6,7},{7,6},{8,9},{9,8},{10,11... | collective-permute-start | bytes 37640 | tf_op jit(solution)/shard_map/ppermute | solution.py:241
  4.9 5.8 %collective-permute-start.1 = (f32[8,392]{1,0:T(8,128)S(1)}, f32[8,392]{1,0:T(8,128)S(1)}, u32[]{:S(2)}, u32[]{:S(2)}) collective-permute-start(f32[8,392]{1,0:T(8,128)S(1)} %get-tuple-element.26.refs_0_), channel_id=1, source_target_pairs={{0,3},{1,2},{2,1},{3,0},{4,7},{5,6},{6,5},{7,4},{8,11},{9,10},{10,... | collective-permute-start | bytes 37640 | tf_op jit(solution)/shard_map/ppermute | solution.py:241
  7.4 4.6 %collective-permute-start = (f32[8,392]{1,0:T(8,128)S(1)}, f32[8,392]{1,0:T(8,128)S(1)}, u32[]{:S(2)}, u32[]{:S(2)}) collective-permute-start(f32[8,392]{1,0:T(8,128)S(1)} %get-tuple-element.26.refs_0_), channel_id=1, source_target_pairs={{0,2},{1,3},{2,0},{3,1},{4,6},{5,7},{6,4},{7,5},{8,10},{9,11},{10,... | collective-permute-start | bytes 37640 | tf_op jit(solution)/shard_map/ppermute | solution.py:241
  33.7 5.5 %collective-permute-start.5 = (bf16[8,392]{1,0:T(8,128)(2,1)S(1)}, bf16[8,392]{1,0:T(8,128)(2,1)S(1)}, u32[]{:S(2)}, u32[]{:S(2)}) collective-permute-start(bf16[8,392]{1,0:T(8,128)(2,1)S(1)} %get-tuple-element.38.refs_0_), channel_id=1, source_target_pairs={{0,3},{1,2},{2,1},{3,0},{4,7},{5,6},{6,5},{7,4},{8,11},{9,10},{10,... | collective-permute-start | bytes 18824 | tf_op jit(solution)/shard_map/ppermute | solution.py:241
  34.4 4.7 %collective-permute-start.4 = (bf16[8,392]{1,0:T(8,128)(2,1)S(1)}, bf16[8,392]{1,0:T(8,128)(2,1)S(1)}, u32[]{:S(2)}, u32[]{:S(2)}) collective-permute-start(bf16[8,392]{1,0:T(8,128)(2,1)S(1)} %get-tuple-element.38.refs_0_), channel_id=1, source_target_pairs={{0,2},{1,3},{2,0},{3,1},{4,6},{5,7},{6,4},{7,5},{8,10},{9,11},{10,... | collective-permute-start | bytes 18824 | tf_op jit(solution)/shard_map/ppermute | solution.py:241
  35.9 3.8 %collective-permute-start.3 = (bf16[8,392]{1,0:T(8,128)(2,1)S(1)}, bf16[8,392]{1,0:T(8,128)(2,1)S(1)}, u32[]{:S(2)}, u32[]{:S(2)}) collective-permute-start(bf16[8,392]{1,0:T(8,128)(2,1)S(1)} %get-tuple-element.38.refs_0_), channel_id=1, source_target_pairs={{0,1},{1,0},{2,3},{3,2},{4,5},{5,4},{6,7},{7,6},{8,9},{9,8},{10,11... | collective-permute-start | bytes 18824 | tf_op jit(solution)/shard_map/ppermute | solution.py:241

commit v11 on v7

--- a/solution.py
+++ b/solution.py
@@ -128,7 +128,7 @@
 
 
 def steps(size, first):
-    return list(range(2, size)) + [1] if first else list(range(1, size))
+    return list(range(2, size)) + [1] if first else list(range(2, size - 1)) + [1] + list(range(size - 1, size))
 
 
 def tree_sum(refs, first):

time: 40.9 us -> 40.9 us (level)
  no operation moved by 1% of the time
where the time goes in v11:
time: 40.9 us; the launch traced here: 40.6 us
  blocking collectives  19.6 us (48%)
  starting transfers between devices  10.1 us (25%)
  Pallas kernels  7.73 us (19%)
  waiting for transfers between devices  2.53 us (6%)
  between operations  0.67 us (2%)
    all_to_all x2, blocking collectives, to_all(): lax.all_to_all(value, send_order, split_axis=0, concat_axis=0, tiled=True)  19.6 us
    ppermute x6, starting transfers between devices, exchange(): lax.ppermute(value, axis, [(source, source ^ step) for source in range(si...  10.1 us
    pallas_call x7, Pallas kernels, call(): pl.pallas_call(kernel, out_shape=outs, in_specs=[VMEM] * len(args) + [HBM...  7.73 us
    ppermute x6, waiting for transfers between devices, exchange(): lax.ppermute(value, axis, [(source, source ^ step) for source in range(si...  2.53 us
  transfers between devices with their start and end apart: 6, of which 4 were waited for; matrix products, arithmetic and copies ran while one was open for 0% of the time, Pallas kernels for 9%

profile of v11, /device:TPU:0, one launch (start us, length us, event | category | flops | bytes accessed | tf_op | source)
XLA Modules:
  0.0 40.6 jit_solution(10065467073081437843)
XLA Ops:
  0.6 1.2 %logits.1 = (f32[8,392]{1,0:T(8,128)S(1)}, bf16[392,256]{1,0:T(8,128)(2,1)S(1)}, bf16[8,256]{1,0:T(8,128)(2,1)S(1)}) custom-call(bf16[196,2,256]{2,1,0:T(2,128)(2,1)} %bitcast.18, bf16[8,256]{1,0:T(8,128)(2,1)} %bitcast.19), custom_call_target="tpu_custom_call" | custom-call | tf_op jit(solution)/shard_map/logits/pallas_call | solution.py:226
  1.8 3.1 %collective-permute-start.2 = (f32[8,392]{1,0:T(8,128)S(1)}, f32[8,392]{1,0:T(8,128)S(1)}, u32[]{:S(2)}, u32[]{:S(2)}) collective-permute-start(f32[8,392]{1,0:T(8,128)S(1)} %get-tuple-element.26.refs_0_), channel_id=1, source_target_pairs={{0,1},{1,0},{2,3},{3,2},{4,5},{5,4},{6,7},{7,6},{8,9},{9,8},{10,11... | collective-permute-start | bytes 37640 | tf_op jit(solution)/shard_map/ppermute | solution.py:241
  4.9 2.5 %collective-permute-start.1 = (f32[8,392]{1,0:T(8,128)S(1)}, f32[8,392]{1,0:T(8,128)S(1)}, u32[]{:S(2)}, u32[]{:S(2)}) collective-permute-start(f32[8,392]{1,0:T(8,128)S(1)} %get-tuple-element.26.refs_0_), channel_id=1, source_target_pairs={{0,3},{1,2},{2,1},{3,0},{4,7},{5,6},{6,5},{7,4},{8,11},{9,10},{10,... | collective-permute-start | bytes 37640 | tf_op jit(solution)/shard_map/ppermute | solution.py:241
  7.4 0.1 collective-permute-start
  7.5 2.8 %prepare.1 = (bf16[392,256]{1,0:T(8,128)(2,1)S(1)}, f32[1,1024]{1,0:T(1,128)S(1)}, bf16[1,1024]{1,0:T(2,128)(2,1)S(1)}, bf16[1024,1024]{1,0:T(8,128)(2,1)S(1)}, ...) custom-call(f32[8,392]{1,0:T(8,128)S(1)} %get-tuple-element.26.refs_0_, ...), custom_call_target="tpu_custom_call" | custom-call | tf_op jit(solution)/shard_map/prepare/pallas_call | solution.py:226
  10.3 0.0 collective-permute-done.2.refs_3_
  10.3 0.3 collective-permute-done.1.refs_2_
  10.7 1.4 %collective-permute-done.refs_1_ = f32[8,392]{1,0:T(8,128)S(1)} collective-permute-done((f32[8,392]{1,0:T(8,128)S(1)}, f32[8,392]{1,0:T(8,128)S(1)}, u32[]{:S(2)}, u32[]{:S(2)}) %collective-permute-start) | collective-permute-done | bytes 12576 | tf_op jit(solution)/shard_map/ppermute | solution.py:241
  12.0 0.4 %dispatch.1 = (bf16[8,4,2,512]{3,2,1,0:T(2,128)(2,1)S(1)}, f32[8,392]{1,0:T(8,128)S(1)}, f32[8,392]{1,0:T(8,128)S(1)}, f32[1,392]{1,0:T(1,128)S(1)}) custom-call(f32[8,392]{1,0:T(8,128)S(1)} %get-tuple-element.26.refs_0_, f32[8,392]{1,0:T(8,128)S(1)} %collective-permute-done.refs_1_, f32[8,392]{1,0:T(8,128)S(1)} %collective-permute-done.1.refs_2_, ...), custom_call_target="tpu_custom_call" | custom-call | tf_op jit(solution)/shard_map/dispatch/pallas_call | solution.py:226
  12.5 10.7 %all_to_all.10 = bf16[32,2,512]{2,1,0:T(2,128)(2,1)S(1)} all-to-all(bf16[32,2,512]{2,1,0:T(2,128)(2,1)S(1)} %bitcast.14), channel_id=1, replica_groups=mesh['expert_a'=2,'expert_b'=2,'expert_c'=2,'hidden'=4] {'expert_a','exp..., dimensions={0} | all-to-all | bytes 131072 | tf_op jit(solution)/shard_map/all_to_all | solution.py:294
  23.1 1.2 %expert.1 = bf16[8,4,2,512]{3,2,1,0:T(2,128)(2,1)S(1)} custom-call(bf16[8,4,2,512]{3,2,1,0:T(2,128)(2,1)S(1)} %bitcast.11, f32[1,1024]{1,0:T(1,128)S(1)} %get-tuple-element.30.bout_ref, bf16[1,1024]{1,0:T(2,128)(2,1)S(1)} %get-tuple-element.31.bin_ref, bf16[1024,1024]{1,0:T(8,128)(2,1)S(1)} %get-tuple-element.32.wout_ref, ...), custom_call_target="tpu_custom_call" | custom-call | tf_op jit(solution)/shard_map/expert/pallas_call | solution.py:226
  24.3 9.0 %all_to_all.11 = bf16[32,2,512]{2,1,0:T(2,128)(2,1)S(1)} all-to-all(bf16[32,2,512]{2,1,0:T(2,128)(2,1)S(1)} %bitcast.12), channel_id=1, replica_groups=mesh['expert_a'=2,'expert_b'=2,'expert_c'=2,'hidden'=4] {'expert_a','exp..., dimensions={0} | all-to-all | bytes 131072 | tf_op jit(solution)/shard_map/all_to_all | solution.py:294
  33.3 0.3 gradient.1
  33.7 0.7 %collective-permute-start.5 = (bf16[8,392]{1,0:T(8,128)(2,1)S(1)}, bf16[8,392]{1,0:T(8,128)(2,1)S(1)}, u32[]{:S(2)}, u32[]{:S(2)}) collective-permute-start(bf16[8,392]{1,0:T(8,128)(2,1)S(1)} %get-tuple-element.38.refs_0_), channel_id=1, source_target_pairs={{0,3},{1,2},{2,1},{3,0},{4,7},{5,6},{6,5},{7,4},{8,11},{9,10},{10,... | collective-permute-start | bytes 18824 | tf_op jit(solution)/shard_map/ppermute | solution.py:241
  34.4 0.3 collective-permute-start.4
  34.7 3.4 %collective-permute-start.3 = (bf16[8,392]{1,0:T(8,128)(2,1)S(1)}, bf16[8,392]{1,0:T(8,128)(2,1)S(1)}, u32[]{:S(2)}, u32[]{:S(2)}) collective-permute-start(bf16[8,392]{1,0:T(8,128)(2,1)S(1)} %get-tuple-element.38.refs_0_), channel_id=1, source_target_pairs={{0,2},{1,3},{2,0},{3,1},{4,6},{5,7},{6,4},{7,5},{8,10},{9,11},{10,... | collective-permute-start | bytes 18824 | tf_op jit(solution)/shard_map/ppermute | solution.py:241
  38.0 0.8 %mixed.1 = (bf16[196,2,256]{2,1,0:T(2,128)(2,1)S(1)}, f32[392,256]{1,0:T(8,128)S(1)}, f32[2,196]{1,0:T(2,128)S(1)}) custom-call(f32[8,392]{1,0:T(8,128)S(1)} %get-tuple-element.36.dispatch_ref, f32[8,392]{1,0:T(8,128)S(1)} %get-tuple-element.37.combine_ref.refs_4_, f32[1,392]{1,0:T(1,128)S(1)} %get-tuple-element.39.total_ref.refs_5_, ...), custom_call_target="tpu_custom_call" | custom-call | tf_op jit(solution)/shard_map/mixed/pallas_call | solution.py:226
  38.8 0.3 collective-permute-done.5.refs_3_
  39.1 0.0 collective-permute-done.4.refs_2_
  39.1 0.6 %collective-permute-done.3.refs_1_ = bf16[8,392]{1,0:T(8,128)(2,1)S(1)} collective-permute-done((bf16[8,392]{1,0:T(8,128)(2,1)S(1)}, bf16[8,392]{1,0:T(8,128)(2,1)S(1)}, u32[]{:S(2)}, u32[]{:S(2)}) %collective-permute-start.3) | collective-permute-done | bytes 6304 | tf_op jit(solution)/shard_map/ppermute | solution.py:241
  39.7 1.0 %token_grad.1 = (bf16[196,2,256]{2,1,0:T(2,128)(2,1)}, bf16[196,2,256]{2,1,0:T(2,128)(2,1)}, f32[2,196]{1,0:T(2,128)}) custom-call(bf16[8,392]{1,0:T(8,128)(2,1)S(1)} %get-tuple-element.38.refs_0_, bf16[8,392]{1,0:T(8,128)(2,1)S(1)} %collective-permute-done.3.refs_1_, bf16[8,392]{1,0:T(8,128)(2,1)S(1)} %collective-permute-done.4.refs_2_, ...), custom_call_target="tpu_custom_call" | custom-call | tf_op jit(solution)/shard_map/token_grad/pallas_call | solution.py:226
Async XLA Ops:
  1.8 8.5 %collective-permute-start.2 = (f32[8,392]{1,0:T(8,128)S(1)}, f32[8,392]{1,0:T(8,128)S(1)}, u32[]{:S(2)}, u32[]{:S(2)}) collective-permute-start(f32[8,392]{1,0:T(8,128)S(1)} %get-tuple-element.26.refs_0_), channel_id=1, source_target_pairs={{0,1},{1,0},{2,3},{3,2},{4,5},{5,4},{6,7},{7,6},{8,9},{9,8},{10,11... | collective-permute-start | bytes 37640 | tf_op jit(solution)/shard_map/ppermute | solution.py:241
  4.9 5.8 %collective-permute-start.1 = (f32[8,392]{1,0:T(8,128)S(1)}, f32[8,392]{1,0:T(8,128)S(1)}, u32[]{:S(2)}, u32[]{:S(2)}) collective-permute-start(f32[8,392]{1,0:T(8,128)S(1)} %get-tuple-element.26.refs_0_), channel_id=1, source_target_pairs={{0,3},{1,2},{2,1},{3,0},{4,7},{5,6},{6,5},{7,4},{8,11},{9,10},{10,... | collective-permute-start | bytes 37640 | tf_op jit(solution)/shard_map/ppermute | solution.py:241
  7.4 4.6 %collective-permute-start = (f32[8,392]{1,0:T(8,128)S(1)}, f32[8,392]{1,0:T(8,128)S(1)}, u32[]{:S(2)}, u32[]{:S(2)}) collective-permute-start(f32[8,392]{1,0:T(8,128)S(1)} %get-tuple-element.26.refs_0_), channel_id=1, source_target_pairs={{0,2},{1,3},{2,0},{3,1},{4,6},{5,7},{6,4},{7,5},{8,10},{9,11},{10,... | collective-permute-start | bytes 37640 | tf_op jit(solution)/shard_map/ppermute | solution.py:241
  33.7 5.5 %collective-permute-start.5 = (bf16[8,392]{1,0:T(8,128)(2,1)S(1)}, bf16[8,392]{1,0:T(8,128)(2,1)S(1)}, u32[]{:S(2)}, u32[]{:S(2)}) collective-permute-start(bf16[8,392]{1,0:T(8,128)(2,1)S(1)} %get-tuple-element.38.refs_0_), channel_id=1, source_target_pairs={{0,3},{1,2},{2,1},{3,0},{4,7},{5,6},{6,5},{7,4},{8,11},{9,10},{10,... | collective-permute-start | bytes 18824 | tf_op jit(solution)/shard_map/ppermute | solution.py:241
  34.4 4.7 %collective-permute-start.4 = (bf16[8,392]{1,0:T(8,128)(2,1)S(1)}, bf16[8,392]{1,0:T(8,128)(2,1)S(1)}, u32[]{:S(2)}, u32[]{:S(2)}) collective-permute-start(bf16[8,392]{1,0:T(8,128)(2,1)S(1)} %get-tuple-element.38.refs_0_), channel_id=1, source_target_pairs={{0,1},{1,0},{2,3},{3,2},{4,5},{5,4},{6,7},{7,6},{8,9},{9,8},{10,11... | collective-permute-start | bytes 18824 | tf_op jit(solution)/shard_map/ppermute | solution.py:241
  34.7 5.0 %collective-permute-start.3 = (bf16[8,392]{1,0:T(8,128)(2,1)S(1)}, bf16[8,392]{1,0:T(8,128)(2,1)S(1)}, u32[]{:S(2)}, u32[]{:S(2)}) collective-permute-start(bf16[8,392]{1,0:T(8,128)(2,1)S(1)} %get-tuple-element.38.refs_0_), channel_id=1, source_target_pairs={{0,2},{1,3},{2,0},{3,1},{4,6},{5,7},{6,4},{7,5},{8,10},{9,11},{10,... | collective-permute-start | bytes 18824 | tf_op jit(solution)/shard_map/ppermute | solution.py:241
